TPU v7x, 32 devices: a whole 2x2x4 slice. The times are simulated.
32 devices in a mesh: dp: 8 (over y, x, core), tensor: 4 (over z).
Axes of the slice: x: 2, y: 2, z: 4, core: 2. Of those that a mesh axis runs over, the one named last changes fastest.
Arguments:
- tokens: bfloat16 [2048, 2560], P('dp'), may hold values from -6 to 6
- segments: int32 [2048], P('dp'), may hold values from 0 to 2047, as said below
- first_gain: float32 [2560], replicated, may hold values from 0.5 to 1.5
- x_weight: bfloat16 [2560, 10, 256], P('dp', None, 'tensor'), may hold values from -0.125 to 0.125
- y_weight: bfloat16 [2560, 10, 256], P('dp', None, 'tensor'), may hold values from -0.125 to 0.125
- conv_weight: float32 [4, 10, 256], P(None, None, 'tensor'), may hold values from -3 to 3
- conv_bias: float32 [10, 256], P(None, 'tensor'), may hold values from -3 to 3
- rate_weight: bfloat16 [10, 256, 256], P(None, None, 'tensor'), may hold values from -0.375 to 0.375
- input_weight: bfloat16 [10, 256, 256], P(None, None, 'tensor'), may hold values from -0.375 to 0.375
- rate_bias: float32 [10, 256], P(None, 'tensor'), may hold values from -4 to 4
- input_bias: float32 [10, 256], P(None, 'tensor'), may hold values from -4 to 4
- decay_logit: float32 [10, 256], P(None, 'tensor'), may hold values from 0.5 to 7
- out_weight: bfloat16 [10, 256, 2560], P(None, 'tensor', 'dp'), may hold values from -0.3125 to 0.3125
- second_gain: float32 [2560], replicated, may hold values from 0.5 to 1.5
- gate_weight: bfloat16 [2560, 7680], P('dp', 'tensor'), may hold values from -0.125 to 0.125
- up_weight: bfloat16 [2560, 7680], P('dp', 'tensor'), may hold values from -0.125 to 0.125
- down_weight: bfloat16 [7680, 2560], P('tensor', 'dp'), may hold values from -0.125 to 0.125
- cotangent: bfloat16 [2048, 2560], P('dp'), may hold values from -6 to 6
Outputs:
- block_out: bfloat16 [2048, 2560], P('dp')
- tokens_grad: float32 [2048, 2560], P('dp')
- first_gain_grad: float32 [2560], replicated
- x_weight_grad: float32 [2560, 10, 256], P('dp', None, 'tensor')
- y_weight_grad: float32 [2560, 10, 256], P('dp', None, 'tensor')
- conv_weight_grad: float32 [4, 10, 256], P(None, None, 'tensor')
- conv_bias_grad: float32 [10, 256], P(None, 'tensor')
- rate_weight_grad: float32 [10, 256, 256], P(None, None, 'tensor')
- input_weight_grad: float32 [10, 256, 256], P(None, None, 'tensor')
- rate_bias_grad: float32 [10, 256], P(None, 'tensor')
- input_bias_grad: float32 [10, 256], P(None, 'tensor')
- decay_logit_grad: float32 [10, 256], P(None, 'tensor')
- out_weight_grad: float32 [10, 256, 2560], P(None, 'tensor', 'dp')
- second_gain_grad: float32 [2560], replicated
- gate_weight_grad: float32 [2560, 7680], P('dp', 'tensor')
- up_weight_grad: float32 [2560, 7680], P('dp', 'tensor')
- down_weight_grad: float32 [7680, 2560], P('tensor', 'dp')
Inputs may be any that keep to these rules, and one draw needn't show every extreme that they name: `segments`: each aligned block of 256 tokens holds whole sequences: a token's value is the index of the first token of its sequence, values never fall, a sequence begins at the first token of every block, the last token of all forms a sequence of its own, and in some block other than the last one sequence fills all 256 tokens.
All inputs are finite; a program needn't handle non-finite values.
Results may differ from a plain program's by a relative error of at most 0.01.
Values may be sent and summed in bfloat16 or wider, within the bound.
No kernel may reach another device: no remote copies, remote signals or barrier semaphores. Data moves between devices by JAX's collectives and lax.ppermute only.
A program may use at most 256 MiB of HBM per device.

v0:
```python
from functools import partial

import jax
import jax.numpy as jnp
from jax import lax
from jax.sharding import PartitionSpec as P

eps = 1e-06


def rms_norm(values, norm_gain):
    inv_root = lax.rsqrt(jnp.mean(values * values, axis=-1, keepdims=True) + eps)
    return values * inv_root * norm_gain


def pair_combine(earlier, later):
    return (earlier[0] * later[0], later[0] * earlier[1] + later[1])


def shift_down(values, steps):
    filler = jnp.zeros((steps,) + values.shape[1:], values.dtype)
    return jnp.concatenate([filler, values[:-steps]], axis=0)


def conv_apply(x_branch, conv_flat, bias_flat, same_masks):
    result = x_branch * conv_flat[0] + bias_flat
    for lag_step in range(1, conv_flat.shape[0]):
        result = (
            result + shift_down(x_branch, lag_step) * same_masks[lag_step - 1] * conv_flat[lag_step]
        )
    return result


def lru_inputs(conv_value, pre_rate, pre_entry, decay_flat, start_col):
    rate_gate = jax.nn.sigmoid(pre_rate)
    entry_gate = jax.nn.sigmoid(pre_entry)
    log_decay = -8.0 * rate_gate * jax.nn.softplus(-decay_flat)
    scaled = jnp.where(start_col, 1.0, jnp.sqrt(-jnp.expm1(2.0 * log_decay)))
    carried = jnp.where(start_col, 0.0, jnp.exp(log_decay))
    return (carried, conv_value * entry_gate * scaled)


def body(
    tokens,
    segments,
    first_gain,
    x_weight,
    y_weight,
    conv_weight,
    conv_bias,
    rate_weight,
    input_weight,
    rate_bias,
    input_bias,
    decay_logit,
    out_weight,
    second_gain,
    gate_weight,
    up_weight,
    down_weight,
    cotangent,
):
    row_count = tokens.shape[0]
    model_width = tokens.shape[1]
    heads_count = rate_weight.shape[0]
    local_width = rate_weight.shape[2]
    chan_count = heads_count * local_width
    conv_taps = conv_weight.shape[0]
    x_rows, y_rows, out_cols = (
        lax.all_gather(x_weight, "dp", axis=0, tiled=True),
        lax.all_gather(y_weight, "dp", axis=0, tiled=True),
        lax.all_gather(out_weight, "dp", axis=2, tiled=True),
    )
    gate_rows, up_rows, down_cols = (
        lax.all_gather(gate_weight, "dp", axis=0, tiled=True),
        lax.all_gather(up_weight, "dp", axis=0, tiled=True),
        lax.all_gather(down_weight, "dp", axis=1, tiled=True),
    )
    x_full = x_rows.reshape(model_width, chan_count)
    y_full = y_rows.reshape(model_width, chan_count)
    out_full = out_cols.reshape(chan_count, model_width)
    x_input = tokens.astype(jnp.float32)
    earlier_ids = [
        jnp.concatenate([jnp.full((lag_step,), -1, jnp.int32), segments[:-lag_step]])
        for lag_step in range(1, conv_taps)
    ]
    same_masks = [(earlier == segments).astype(jnp.float32)[:, None] for earlier in earlier_ids]
    start_col = (earlier_ids[0] != segments)[:, None]
    normed_first, first_pull = jax.vjp(rms_norm, x_input, first_gain)
    first_low = normed_first.astype(jnp.bfloat16)
    x_branch = jnp.dot(first_low, x_full, preferred_element_type=jnp.float32)
    y_branch = jnp.dot(first_low, y_full, preferred_element_type=jnp.float32)
    conv_flat = conv_weight.reshape(conv_taps, chan_count)
    conv_out, conv_pull = jax.vjp(
        partial(conv_apply, same_masks=same_masks),
        x_branch,
        conv_flat,
        conv_bias.reshape(chan_count),
    )
    conv_low = conv_out.astype(jnp.bfloat16)
    block_heads = lax.all_gather(
        conv_low.reshape(row_count, heads_count, local_width), "tensor", axis=2, tiled=True
    )
    both_weights = jnp.concatenate([rate_weight, input_weight], axis=2)
    pre_both = jnp.einsum(
        "thi,hij->thj", block_heads, both_weights, preferred_element_type=jnp.float32
    )
    pre_rate = pre_both[:, :, :local_width].reshape(row_count, chan_count) + rate_bias.reshape(
        chan_count
    )
    pre_entry = pre_both[:, :, local_width:].reshape(row_count, chan_count) + input_bias.reshape(
        chan_count
    )
    (carried, driven), lru_pull = jax.vjp(
        partial(lru_inputs, start_col=start_col),
        conv_low.astype(jnp.float32),
        pre_rate,
        pre_entry,
        decay_logit.reshape(chan_count),
    )
    _, hidden = lax.associative_scan(pair_combine, (carried, driven), axis=0)
    gelu_y, gelu_y_pull = jax.vjp(jax.nn.gelu, y_branch)
    mixed_low = (hidden * gelu_y).astype(jnp.bfloat16)
    recurrent = lax.psum(jnp.dot(mixed_low, out_full, preferred_element_type=jnp.float32), "tensor")
    residual = x_input + recurrent
    normed_second, second_pull = jax.vjp(rms_norm, residual, second_gain)
    second_low = normed_second.astype(jnp.bfloat16)
    gate_pre = jnp.dot(second_low, gate_rows, preferred_element_type=jnp.float32)
    up_pre = jnp.dot(second_low, up_rows, preferred_element_type=jnp.float32)
    gelu_gate, gelu_gate_pull = jax.vjp(jax.nn.gelu, gate_pre)
    ffn_low = (gelu_gate * up_pre).astype(jnp.bfloat16)
    ffn_out = lax.psum(jnp.dot(ffn_low, down_cols, preferred_element_type=jnp.float32), "tensor")
    block_out = (residual + ffn_out).astype(jnp.bfloat16)
    gate_back, up_back, down_back = (
        lax.all_gather(gate_weight, "dp", axis=0, tiled=True),
        lax.all_gather(up_weight, "dp", axis=0, tiled=True),
        lax.all_gather(down_weight, "dp", axis=1, tiled=True),
    )
    grad_out = cotangent.astype(jnp.float32)
    grad_ffn = jnp.einsum("td,fd->tf", cotangent, down_back, preferred_element_type=jnp.float32)
    grad_up_low = (grad_ffn * gelu_gate).astype(jnp.bfloat16)
    grad_gate_low = gelu_gate_pull(grad_ffn * up_pre)[0].astype(jnp.bfloat16)
    second_terms = jnp.einsum(
        "tf,df->td", grad_gate_low, gate_back, preferred_element_type=jnp.float32
    ) + jnp.einsum("tf,df->td", grad_up_low, up_back, preferred_element_type=jnp.float32)
    grad_second = lax.psum(second_terms, "tensor")
    grad_residual_norm, second_gain_grad = second_pull(grad_second)
    grad_residual = grad_out + grad_residual_norm
    x_again, y_again, out_again = (
        lax.all_gather(x_weight, "dp", axis=0, tiled=True),
        lax.all_gather(y_weight, "dp", axis=0, tiled=True),
        lax.all_gather(out_weight, "dp", axis=2, tiled=True),
    )
    x_back = x_again.reshape(model_width, chan_count)
    y_back = y_again.reshape(model_width, chan_count)
    out_back = out_again.reshape(chan_count, model_width)
    grad_rec_low = grad_residual.astype(jnp.bfloat16)
    grad_mixed = jnp.einsum("td,cd->tc", grad_rec_low, out_back, preferred_element_type=jnp.float32)
    grad_y_low = gelu_y_pull(grad_mixed * hidden)[0].astype(jnp.bfloat16)
    grad_state_in = grad_mixed * gelu_y
    next_carried = jnp.concatenate([carried[1:], jnp.zeros((1, chan_count), jnp.float32)], axis=0)
    _, flipped = lax.associative_scan(
        pair_combine, (jnp.flip(next_carried, 0), jnp.flip(grad_state_in, 0)), axis=0
    )
    grad_state = jnp.flip(flipped, 0)
    grad_conv_direct, grad_pre_rate, grad_pre_entry, decay_grad = lru_pull(
        (grad_state * shift_down(hidden, 1), grad_state)
    )
    rate_low = grad_pre_rate.astype(jnp.bfloat16)
    entry_low = grad_pre_entry.astype(jnp.bfloat16)
    rate_bias_grad = jnp.sum(rate_low.astype(jnp.float32), axis=0).reshape(heads_count, local_width)
    input_bias_grad = jnp.sum(entry_low.astype(jnp.float32), axis=0).reshape(
        heads_count, local_width
    )
    grad_both = jnp.concatenate(
        [
            rate_low.reshape(row_count, heads_count, local_width),
            entry_low.reshape(row_count, heads_count, local_width),
        ],
        axis=2,
    )
    both_grad = jnp.einsum(
        "thi,thj->hij", block_heads, grad_both, preferred_element_type=jnp.float32
    )
    rate_weight_grad = both_grad[:, :, :local_width]
    input_weight_grad = both_grad[:, :, local_width:]
    head_terms = jnp.einsum(
        "thj,hij->thi", grad_both, both_weights, preferred_element_type=jnp.float32
    )
    grad_conv_gates = lax.psum_scatter(
        head_terms.astype(jnp.bfloat16), "tensor", scatter_dimension=2, tiled=True
    ).astype(jnp.float32)
    grad_conv = grad_conv_direct + grad_conv_gates.reshape(row_count, chan_count)
    grad_x_branch, conv_flat_grad, conv_bias_flat = conv_pull(grad_conv)
    grad_x_low = grad_x_branch.astype(jnp.bfloat16)
    first_terms = jnp.einsum(
        "tc,dc->td", grad_x_low, x_back, preferred_element_type=jnp.float32
    ) + jnp.einsum("tc,dc->td", grad_y_low, y_back, preferred_element_type=jnp.float32)
    grad_first = lax.psum(first_terms, "tensor")
    grad_input_norm, first_gain_grad = first_pull(grad_first)
    tokens_grad = grad_residual + grad_input_norm
    down_grad = jnp.einsum("tf,td->fd", ffn_low, cotangent, preferred_element_type=jnp.float32)
    gate_grad = jnp.einsum(
        "td,tf->df", second_low, grad_gate_low, preferred_element_type=jnp.float32
    )
    up_grad = jnp.einsum("td,tf->df", second_low, grad_up_low, preferred_element_type=jnp.float32)
    out_grad = jnp.einsum(
        "tc,td->cd", mixed_low, grad_rec_low, preferred_element_type=jnp.float32
    ).reshape(heads_count, local_width, model_width)
    x_grad = jnp.einsum(
        "td,tc->dc", first_low, grad_x_low, preferred_element_type=jnp.float32
    ).reshape(model_width, heads_count, local_width)
    y_grad = jnp.einsum(
        "td,tc->dc", first_low, grad_y_low, preferred_element_type=jnp.float32
    ).reshape(model_width, heads_count, local_width)
    x_share, y_share, out_share, gate_share, up_share, down_share = (
        lax.psum_scatter(x_grad, "dp", scatter_dimension=0, tiled=True),
        lax.psum_scatter(y_grad, "dp", scatter_dimension=0, tiled=True),
        lax.psum_scatter(out_grad, "dp", scatter_dimension=2, tiled=True),
        lax.psum_scatter(gate_grad, "dp", scatter_dimension=0, tiled=True),
        lax.psum_scatter(up_grad, "dp", scatter_dimension=0, tiled=True),
        lax.psum_scatter(down_grad, "dp", scatter_dimension=1, tiled=True),
    )
    summed_small = lax.psum(
        (
            first_gain_grad,
            conv_flat_grad.reshape(conv_taps, heads_count, local_width),
            conv_bias_flat.reshape(heads_count, local_width),
            rate_weight_grad,
            input_weight_grad,
            rate_bias_grad,
            input_bias_grad,
            decay_grad.reshape(heads_count, local_width),
            second_gain_grad,
        ),
        "dp",
    )
    return (
        block_out,
        tokens_grad,
        summed_small[0],
        x_share,
        y_share,
        summed_small[1],
        summed_small[2],
        summed_small[3],
        summed_small[4],
        summed_small[5],
        summed_small[6],
        summed_small[7],
        out_share,
        summed_small[8],
        gate_share,
        up_share,
        down_share,
    )


def solution(mesh):
    return jax.shard_map(
        body,
        mesh=mesh,
        in_specs=(
            P("dp", None),
            P("dp"),
            P(),
            P("dp", None, "tensor"),
            P("dp", None, "tensor"),
            P(None, None, "tensor"),
            P(None, "tensor"),
            P(None, None, "tensor"),
            P(None, None, "tensor"),
            P(None, "tensor"),
            P(None, "tensor"),
            P(None, "tensor"),
            P(None, "tensor", "dp"),
            P(),
            P("dp", "tensor"),
            P("dp", "tensor"),
            P("tensor", "dp"),
            P("dp", None),
        ),
        out_specs=(
            P("dp", None),
            P("dp", None),
            P(),
            P("dp", None, "tensor"),
            P("dp", None, "tensor"),
            P(None, None, "tensor"),
            P(None, "tensor"),
            P(None, None, "tensor"),
            P(None, None, "tensor"),
            P(None, "tensor"),
            P(None, "tensor"),
            P(None, "tensor"),
            P(None, "tensor", "dp"),
            P(),
            P("dp", "tensor"),
            P("dp", "tensor"),
            P("tensor", "dp"),
        ),
        check_vma=False,
    )
```

profile of v0, /device:TPU:0, one launch (start us, length us, event | category | flops | bytes accessed | tf_op | source)
XLA Modules:
  0.0 1717.4 jit_solution(5525568513261155856)
XLA Ops:
  7.2 2.7 copy.68
  15.4 61.1 %all-gather.8.cloned.1.call-done = bf16[2560,10,64]{2,1,0:T(8,128)(2,1)} async-done(((bf16[320,10,64]{2,1,0:T(8,128)(2,1)}), bf16[2560,10,64]{2,1,0:T(8,128)(2,1)}) %all-gather.8.cloned.1.call-update) | async-done | bytes 3276816 | tf_op jit(solution)/shard_map/all_gather | solution.py:70
  76.5 11.2 copy.69
  87.7 3.5 fusion.72
  94.7 47.5 %all-gather.12.cloned.1.call-done = bf16[2560,10,64]{2,1,0:T(8,128)(2,1)} async-done(((bf16[320,10,64]{2,1,0:T(8,128)(2,1)}), bf16[2560,10,64]{2,1,0:T(8,128)(2,1)}) %all-gather.12.cloned.1.call-update) | async-done | bytes 3276816 | tf_op jit(solution)/shard_map/all_gather | solution.py:71
  142.2 11.1 copy.74
  153.4 54.6 %all-gather.14.cloned.1.call-done = bf16[10,64,2560]{1,0,2:T(8,128)(2,1)} async-done(((bf16[10,64,320]{1,0,2:T(8,128)(2,1)}), bf16[10,64,2560]{1,0,2:T(8,128)(2,1)}) %all-gather.14.cloned.1.call-update) | async-done | bytes 3276816 | tf_op jit(solution)/shard_map/all_gather | solution.py:72
  208.0 11.1 copy.76
  219.1 23.7 %all-gather.10.cloned.1.call-done = bf16[256,10,256]{0,2,1:T(8,128)(2,1)} async-done(((bf16[256,10,64]{0,2,1:T(8,128)(2,1)}), bf16[256,10,256]{0,2,1:T(8,128)(2,1)}) %all-gather.10.cloned.1.call-update) | async-done | bytes 1310736 | tf_op jit(solution)/shard_map/all_gather | solution.py:101
  247.2 3.0 exponential_select_fusion
  250.3 2.6 slice.455
  255.5 2.7 slice.450
  259.5 2.7 slice.507
  262.1 2.6 slice.453
  277.0 4.5 multiply_convert_fusion.3
  282.3 2.7 fusion.95
  287.6 100.6 %all-reduce.54.cloned.1.call-done = f32[256,2560]{1,0:T(8,128)} async-done(((f32[256,2560]{1,0:T(8,128)}), f32[256,2560]{1,0:T(8,128)}) %all-reduce.54.cloned.1.call-update) | async-done | bytes 2621456 | tf_op jit(solution)/shard_map/psum | solution.py:124
  392.2 57.3 %all-gather.18.cloned.1.call-done = bf16[2560,1920]{1,0:T(8,128)(2,1)} async-done(((bf16[320,1920]{1,0:T(8,128)(2,1)}), bf16[2560,1920]{1,0:T(8,128)(2,1)}) %all-gather.18.cloned.1.call-update) | async-done | bytes 9830416 | tf_op jit(solution)/shard_map/all_gather | solution.py:76
  449.5 7.9 fusion.97
  457.4 54.5 %all-gather.16.cloned.1.call-done = bf16[2560,1920]{1,0:T(8,128)(2,1)} async-done(((bf16[320,1920]{1,0:T(8,128)(2,1)}), bf16[2560,1920]{1,0:T(8,128)(2,1)}) %all-gather.16.cloned.1.call-update) | async-done | bytes 9830416 | tf_op jit(solution)/shard_map/all_gather | solution.py:75
  511.9 7.9 fusion.96
  519.8 54.5 %all-gather.20.cloned.1.call-done = bf16[1920,2560]{0,1:T(8,128)(2,1)} async-done(((bf16[1920,320]{0,1:T(8,128)(2,1)}), bf16[1920,2560]{0,1:T(8,128)(2,1)}) %all-gather.20.cloned.1.call-update) | async-done | bytes 9830416 | tf_op jit(solution)/shard_map/all_gather | solution.py:77
  574.3 10.3 multiply_convert_fusion.1
  584.6 6.3 fusion.99
  591.0 4.4 convolution_add_fusion.1
  600.3 2.7 slice.512
  605.6 3.3 slice.520
  608.9 3.3 slice.511
  612.1 3.2 slice.513
  617.6 82.1 %all-reduce.56.cloned.1.call-done = f32[256,2560]{1,0:T(8,128)} async-done(((f32[256,2560]{1,0:T(8,128)}), f32[256,2560]{1,0:T(8,128)}) %all-reduce.56.cloned.1.call-update) | async-done | bytes 2621456 | tf_op jit(solution)/shard_map/psum | solution.py:146
  699.7 3.9 multiply_reduce_fusion
  717.9 3.2 slice.515
  721.1 3.2 slice.517
  757.8 3.3 slice.573
  781.3 2.7 pad.156
  784.1 2.7 pad.157
  789.0 5.9 rev.6
  794.9 4.0 multiply_reduce_fusion.3
  809.0 3.3 fusion.15
  812.8 8.5 fusion.98
  821.3 21.4 %reduce-scatter.14.cloned.1.call-done = bf16[256,10,64]{0,2,1:T(8,128)(2,1)} async-done(((bf16[256,10,256]{0,2,1:T(8,128)(2,1)}), bf16[256,10,64]{0,2,1:T(8,128)(2,1)}) %reduce-scatter.14.cloned.1.call-update) | async-done | bytes 327696 | tf_op jit(solution)/shard_map/reduce_scatter | solution.py:190
  846.7 2.9 fusion.74
  853.6 2.8 convolution_add_fusion
  857.4 5.7 fusion.30
  863.1 16.0 copy.91
  879.1 15.8 reshape.215
  895.8 4.1 fusion.66
  900.0 4.1 fusion.68
  908.9 11.2 fusion.103
  920.2 9.5 fusion.102
  929.8 9.5 fusion.101
  940.2 104.5 %all-reduce.60.cloned.1.call-done = (f32[256,2560]{1,0:T(8,128)}, f32[256,2560]{1,0:T(8,128)}) async-done(((f32[256,2560]{1,0:T(8,128)}, f32[256,2560]{1,0:T(8,128)}), (f32[256,2560]{1,0:T(8,128)}, f32[256,2560]{1,0:T(8,128)})) %all-reduce.60.cloned.1.call-update) | async-done | bytes 5242896 | tf_op jit(solution)/shard_map/psum | solution.py:132
  1044.7 2.7 fusion.3
  1047.4 25.6 %all-reduce.46 = (f32[2560]{0:T(1024)}, f32[4,10,64]{2,1,0:T(8,128)S(1)}, f32[10,64]{1,0:T(8,128)}, f32[10,64]{1,0:T(8,128)}, f32[10,64]{1,0:T(8,128)}, /*index=5*/f32[10,64]{1,0:T(8,128)}, f32[2560]{0:T(1024)}) all-reduce(f32[2560]{0:T(1024)S(1)} %get-tuple-element.70, ...), channel_id=1, replica_groups=mesh['dp'=8,'tensor'=4] {'dp'}, use_global_device_ids=true, to_apply=%region_10.11 | all-reduce | flops 10240 | bytes 81920 | tf_op jit(solution)/shard_map/psum | solution.py:224
  1073.6 7.4 fusion.5
  1081.0 29.0 %reduce-scatter.26.cloned.1.call-done = f32[320,640]{1,0:T(8,128)} async-done(((f32[2560,640]{1,0:T(8,128)}), f32[320,640]{1,0:T(8,128)}) %reduce-scatter.26.cloned.1.call-update) | async-done | bytes 819216
  1110.0 2.9 reshape.216
  1112.9 2.9 copy.92
  1115.8 61.1 %reduce-scatter.24.cloned.1.call-done = f32[320,640]{1,0:T(8,128)} async-done(((f32[2560,640]{1,0:T(8,128)}), f32[320,640]{1,0:T(8,128)}) %reduce-scatter.24.cloned.1.call-update) | async-done | bytes 819216
  1179.3 63.9 %reduce-scatter.22.cloned.1.call-done = f32[320,640]{1,0:T(8,128)} async-done(((f32[2560,640]{1,0:T(8,128)}), f32[320,640]{1,0:T(8,128)}) %reduce-scatter.22.cloned.1.call-update) | async-done | bytes 819216
  1245.6 60.1 %all-reduce.58.cloned.1.call-done = (f32[10,256,64]{1,2,0:T(8,128)}, f32[10,256,64]{1,2,0:T(8,128)}) async-done(((f32[10,256,64]{1,2,0:T(8,128)}, f32[10,256,64]{1,2,0:T(8,128)}), (f32[10,256,64]{1,2,0:T(8,128)}, f32[10,256,64]{1,2,0:T(8,128)})) %all-reduce.58.cloned.1.call-update) | async-done | bytes 1310736 | tf_op jit(solution)/shard_map/psum | solution.py:224
  1305.7 133.0 %reduce-scatter.20.cloned.1.call-done = f32[1920,320]{0,1:T(8,128)} async-done(((f32[1920,2560]{0,1:T(8,128)}), f32[1920,320]{0,1:T(8,128)}) %reduce-scatter.20.cloned.1.call-update) | async-done | bytes 2457616 | tf_op jit(solution)/shard_map/reduce_scatter | solution.py:222
  1438.6 133.8 %reduce-scatter.18.cloned.1.call-done = f32[320,1920]{1,0:T(8,128)} async-done(((f32[2560,1920]{1,0:T(8,128)}), f32[320,1920]{1,0:T(8,128)}) %reduce-scatter.18.cloned.1.call-update) | async-done | bytes 2457616 | tf_op jit(solution)/shard_map/reduce_scatter | solution.py:221
  1572.4 133.8 %reduce-scatter.16.cloned.1.call-done = f32[320,1920]{1,0:T(8,128)} async-done(((f32[2560,1920]{1,0:T(8,128)}), f32[320,1920]{1,0:T(8,128)}) %reduce-scatter.16.cloned.1.call-update) | async-done | bytes 2457616 | tf_op jit(solution)/shard_map/reduce_scatter | solution.py:220
  (400 shorter events, 151.6 us)
Async XLA Ops:
  7.2 2.8 copy-start.25
  7.2 69.3 %all-gather.8.cloned.1.call-start = ((), (), s32[]{:S(2)}) async-start(), calls=%async_computation.7 | async-start | bytes 11796480 | tf_op jit(solution)/shard_map/all_gather | solution.py:70
  9.9 2.0 copy-start.26
  9.9 132.3 %all-gather.12.cloned.1.call-start = ((), (), s32[]{:S(2)}) async-start(), calls=%async_computation.9 | async-start | bytes 11796480 | tf_op jit(solution)/shard_map/all_gather | solution.py:71
  11.9 2.0 copy-start.54
  11.9 2.1 copy-start.39
  11.9 2.5 copy-start
  11.9 3.4 copy-start.47
  11.9 196.1 %all-gather.14.cloned.1.call-start = ((), (), s32[]{:S(2)}) async-start(), calls=%async_computation.10 | async-start | bytes 11796480 | tf_op jit(solution)/shard_map/all_gather | solution.py:72
  13.8 228.9 %all-gather.10.cloned.1.call-start = ((), (), s32[]{:S(2)}) async-start(), calls=%async_computation.8 | async-start | bytes 1638400 | tf_op jit(solution)/shard_map/all_gather | solution.py:101
  14.2 77.1 %copy-start.33 = (f32[640]{0:T(1024)}, f32[640]{0:T(1024)S(1)}, u32[]{:S(2)}) copy-start(f32[640]{0:T(1024)S(1)} %mul.554) | copy-start | bytes 7684
  14.3 77.0 %copy-start.31 = (f32[640]{0:T(1024)}, f32[640]{0:T(1024)S(1)}, u32[]{:S(2)}) copy-start(f32[640]{0:T(1024)S(1)} %mul.564) | copy-start | bytes 7684
  14.3 76.9 %copy-start.35 = (f32[640]{0:T(1024)}, f32[640]{0:T(1024)S(1)}, u32[]{:S(2)}) copy-start(f32[640]{0:T(1024)S(1)} %mul.559) | copy-start | bytes 7684
  15.3 75.9 %copy-start.41 = (f32[256]{0:T(256)}, f32[256]{0:T(256)S(1)}, u32[]{:S(2)}) copy-start(f32[256]{0:T(256)S(1)} %get-tuple-element.151) | copy-start | bytes 3076
  15.3 76.0 %copy-start.43 = (f32[256]{0:T(256)}, f32[256]{0:T(256)S(1)}, u32[]{:S(2)}) copy-start(f32[256]{0:T(256)S(1)} %get-tuple-element.152) | copy-start | bytes 3076
  15.4 76.0 %copy-start.45 = (f32[256]{0:T(256)}, f32[256]{0:T(256)S(1)}, u32[]{:S(2)}) copy-start(f32[256]{0:T(256)S(1)} %get-tuple-element.153) | copy-start | bytes 3076
  15.4 231.9 %copy-start.52 = (pred[256]{0:T(512)(128)(4,1)}, pred[256]{0:T(512)(128)(4,1)S(1)}, u32[]{:S(2)}) copy-start(pred[256]{0:T(512)(128)(4,1)S(1)} %get-tuple-element.150) | copy-start | bytes 772
  15.4 72.3 %copy-start.28 = (f32[2560]{0:T(1024)S(1)}, f32[2560]{0:T(1024)}, u32[]{:S(2)}) copy-start(f32[2560]{0:T(1024)} %param.20) | copy-start | bytes 30724
  91.8 61.6 %copy-start.12 = (bf16[256,640]{1,0:T(8,128)(2,1)}, bf16[256,640]{1,0:T(8,128)(2,1)S(1)}, u32[]{:S(2)}) copy-start(bf16[256,640]{1,0:T(8,128)(2,1)S(1)} %add_convert_fusion.2) | copy-start | bytes 983044
  92.7 295.5 %all-reduce.54.cloned.1.call-start = ((), (), s32[]{:S(2)}) async-start(), calls=%async_computation.11 | async-start | bytes 5242880 | tf_op jit(solution)/shard_map/psum | solution.py:124
  94.1 148.7 %copy-start.13 = (bf16[10,256,128]{1,2,0:T(8,128)(2,1)}, bf16[10,256,128]{1,2,0:T(8,128)(2,1)S(1)}, u32[]{:S(2)}) copy-start(bf16[10,256,128]{1,2,0:T(8,128)(2,1)S(1)} %constant_dynamic-update-slice_fusion) | copy-start | bytes 1966084
  245.6 9.9 copy-start.4
  247.2 14.9 copy-start.9
  271.3 4.2 copy-start.21
  271.3 4.2 copy-start.22
  272.2 3.3 copy-start.49
  275.7 5.9 copy-start.14
  277.0 4.5 copy-start.15
  277.0 5.3 copy-start.7
  285.0 164.5 %all-gather.18.cloned.1.call-start = ((), (), s32[]{:S(2)}) async-start(), calls=%async_computation.13 | async-start | bytes 11059200 | tf_op jit(solution)/shard_map/all_gather | solution.py:76
  285.5 226.3 %all-gather.16.cloned.1.call-start = ((), (), s32[]{:S(2)}) async-start(), calls=%async_computation.12 | async-start | bytes 11059200 | tf_op jit(solution)/shard_map/all_gather | solution.py:75
  286.3 288.0 %all-gather.20.cloned.1.call-start = ((), (), s32[]{:S(2)}) async-start(), calls=%async_computation.14 | async-start | bytes 11059200 | tf_op jit(solution)/shard_map/all_gather | solution.py:77
  287.0 104.8 %copy-start.29 = (f32[2560]{0:T(1024)S(1)}, f32[2560]{0:T(1024)}, u32[]{:S(2)}) copy-start(f32[2560]{0:T(1024)} %param.31) | copy-start | bytes 30724
  287.1 412.6 %all-reduce.56.cloned.1.call-start = ((), (), s32[]{:S(2)}) async-start(), calls=%async_computation.15 | async-start | bytes 5242880 | tf_op jit(solution)/shard_map/psum | solution.py:146
  574.3 16.7 slice-start
  574.3 16.7 slice-start.1
  584.6 6.3 copy-start.23
  584.6 6.3 copy-start.24
  584.6 6.3 slice-start.2
  595.4 247.3 %reduce-scatter.14.cloned.1.call-start = ((), (), s32[]{:S(2)}) async-start(), calls=%async_computation.16 | async-start | bytes 1638400 | tf_op jit(solution)/shard_map/reduce_scatter | solution.py:190
  699.7 3.9 copy-start.2
  699.7 4.1 copy-start.10
  703.8 2.4 copy-start.8
  703.8 2.5 copy-start.57
  703.8 2.7 copy-start.58
  706.1 2.5 copy-start.3
  770.1 10.5 copy-start.48
  781.3 13.6 copy-start.53
  794.9 7.9 copy-start.40
  807.0 5.6 copy-start.42
  807.0 5.7 copy-start.44
  807.0 5.8 copy-start.46
  812.3 232.3 %all-reduce.60.cloned.1.call-start = ((), (), s32[]{:S(2)}) async-start(), calls=%async_computation.24 | async-start | bytes 10485760 | tf_op jit(solution)/shard_map/psum | solution.py:132
  846.7 2.9 copy-start.34
  846.7 3.0 copy-start.36
  856.4 253.5 %reduce-scatter.26.cloned.1.call-start = ((), (), s32[]{:S(2)}) async-start(), calls=%async_computation.22 | async-start | bytes 7372800
  894.9 282.0 %reduce-scatter.24.cloned.1.call-start = ((), (), s32[]{:S(2)}) async-start(), calls=%async_computation.21 | async-start | bytes 7372800
  900.0 343.2 %reduce-scatter.22.cloned.1.call-start = ((), (), s32[]{:S(2)}) async-start(), calls=%async_computation.20 | async-start | bytes 7372800
  904.1 401.6 %all-reduce.58.cloned.1.call-start = ((), (), s32[]{:S(2)}) async-start(), calls=%async_computation.23 | async-start | bytes 2621440 | tf_op jit(solution)/shard_map/psum | solution.py:224
  908.6 530.0 %reduce-scatter.20.cloned.1.call-start = ((), (), s32[]{:S(2)}) async-start(), calls=%async_computation.19 | async-start | bytes 22118400 | tf_op jit(solution)/shard_map/reduce_scatter | solution.py:222
  920.1 652.3 %reduce-scatter.18.cloned.1.call-start = ((), (), s32[]{:S(2)}) async-start(), calls=%async_computation.18 | async-start | bytes 22118400 | tf_op jit(solution)/shard_map/reduce_scatter | solution.py:221
  929.7 776.4 %reduce-scatter.16.cloned.1.call-start = ((), (), s32[]{:S(2)}) async-start(), calls=%async_computation.17 | async-start | bytes 22118400 | tf_op jit(solution)/shard_map/reduce_scatter | solution.py:220
  939.3 108.1 %copy-start.30 = (f32[2560]{0:T(1024)S(1)}, f32[2560]{0:T(1024)}, u32[]{:S(2)}) copy-start(f32[2560]{0:T(1024)} %get-tuple-element.68) | copy-start | bytes 30724
  939.3 134.3 %copy-start.51 = (f32[256]{0:T(256)S(1)}, f32[256]{0:T(256)}, u32[]{:S(2)}) copy-start(f32[256]{0:T(256)} %copy-done.50) | copy-start | bytes 3076
  (16 other events, 20.6 us)
Sparse Core Ops, SparseCore 0:
  10.5 65.9 all-gather.7
  78.9 63.2 all-gather.11
  144.7 63.2 all-gather.13
  210.0 32.7 all-gather.9
  285.1 103.0 all-reduce.53
  389.9 59.4 all-gather.17
  451.4 60.4 all-gather.15
  513.8 60.4 all-gather.19
  595.5 104.1 all-reduce.55
  812.5 30.2 reduce-scatter.13
  856.6 188.0 all-reduce.59
  1048.0 61.9 reduce-scatter.25
  1113.8 62.9 reduce-scatter.23
  1180.2 62.9 reduce-scatter.21
  1247.7 57.8 all-reduce.57
  1309.8 128.8 reduce-scatter.19
  1442.7 129.6 reduce-scatter.17
  1576.5 129.6 reduce-scatter.15
where the time goes:
time: 1730 us; the launch traced here: 1720 us
  waiting for transfers between devices  1280 us (74%)
  local copies, waits for them, and re-layouts  218 us (13%)
  matrix products  114 us (7%)
  other arithmetic  64.5 us (4%)
  blocking collectives  25.6 us (1%)
    unnamed x21, waiting for transfers between devices  156 us
    reduce_scatter x1, waiting for transfers between devices, body(): lax.psum_scatter(gate_grad, 'dp', scatter_dimension=0, tiled=True)  134 us
    reduce_scatter x1, waiting for transfers between devices, body(): lax.psum_scatter(up_grad, 'dp', scatter_dimension=0, tiled=True)  134 us
    reduce_scatter x1, waiting for transfers between devices, body(): lax.psum_scatter(down_grad, 'dp', scatter_dimension=1, tiled=True)  133 us
    psum x1, waiting for transfers between devices, body(): lax.psum(jnp.dot(ffn_low, down_cols, preferred_element_type=jnp.float32),...  104 us
    psum x1, waiting for transfers between devices, body(): lax.psum(jnp.dot(mixed_low, out_full, preferred_element_type=jnp.float32)...  101 us
    psum x1, waiting for transfers between devices, body(): grad_second = lax.psum(second_terms, 'tensor')  82.1 us
    unnamed x137, local copies, waits for them, and re-layouts  63.2 us
  transfers between devices with their start and end apart: 18, of which 18 were waited for; matrix products, arithmetic and copies ran while one was open for 11% of the time, Pallas kernels for 0%

commit v1 on v0

v1 whole, which is shorter than its diff:
```python
from functools import partial

import jax
import jax.numpy as jnp
from jax import lax
from jax.experimental import pallas as pl
from jax.experimental.pallas import tpu as pltpu
from jax.sharding import PartitionSpec as P

eps = 1e-06
f32 = jnp.float32
bf16 = jnp.bfloat16
vmem = pl.BlockSpec(memory_space=pltpu.VMEM)
smem = pl.BlockSpec(memory_space=pltpu.SMEM)
MIB = 1024 * 1024
chunk_count = 3


def nn(a, b):
    return lax.dot_general(a, b, (((1,), (0,)), ((), ())), preferred_element_type=f32)


def nt(a, b):
    return lax.dot_general(a, b, (((1,), (1,)), ((), ())), preferred_element_type=f32)


def tn(a, b):
    return lax.dot_general(a, b, (((0,), (0,)), ((), ())), preferred_element_type=f32)


def call(kernel, outs, *args, scalars=0, mem=48, flops=0, name=None):
    moved = sum(a.size * a.dtype.itemsize for a in args)
    moved += sum(s.size * jnp.dtype(s.dtype).itemsize for s in outs)
    return pl.pallas_call(
        kernel,
        out_shape=outs,
        in_specs=[smem] * scalars + [vmem] * (len(args) - scalars),
        out_specs=[vmem] * len(outs),
        compiler_params=pltpu.CompilerParams(vmem_limit_bytes=mem * MIB),
        cost_estimate=pl.CostEstimate(flops=flops, bytes_accessed=moved, transcendentals=0),
        name=name,
    )(*args)


def like(shape, dtype):
    return jax.ShapeDtypeStruct(shape, dtype)


def gelu_pair(v):
    c = 0.7978845608028654
    sq = v * v
    t = jnp.tanh(c * v * (1.0 + 0.044715 * sq))
    half = 0.5 * (1.0 + t)
    slope = half + 0.5 * v * (1.0 - t * t) * c * (1.0 + 3.0 * 0.044715 * sq)
    return v * half, slope


def one_less_exp(x):
    series = x * (
        1.0
        - x * (1 / 2) * (1.0 - x * (1 / 3) * (1.0 - x * (1 / 4) * (1.0 - x * (1 / 5) * (
            1.0 - x * (1 / 6) * (1.0 - x * (1 / 7) * (1.0 - x * (1 / 8)))))))
    )
    return jnp.where(x < 0.5, series, 1.0 - jnp.exp(-x))


def softplus(v):
    return jnp.maximum(v, 0.0) + jnp.log1p(jnp.exp(-jnp.abs(v)))


def sigmoid(v):
    return 1.0 / (1.0 + jnp.exp(-v))


def row_ids(shape):
    return lax.broadcasted_iota(jnp.int32, shape, 0)


def down_rows(v, steps, fill=0.0):
    return jnp.where(row_ids(v.shape) >= steps, pltpu.roll(v, steps, 0), fill)


def up_rows(v, steps, fill=0.0):
    rows = v.shape[0]
    return jnp.where(row_ids(v.shape) < rows - steps, pltpu.roll(v, rows - steps, 0), fill)


def scan_rows(decay, drive, shift):
    steps = 1
    while steps < decay.shape[0]:
        drive = decay * shift(drive, steps) + drive
        if steps * 2 < decay.shape[0]:
            decay = decay * shift(decay, steps, 1.0)
        steps *= 2
    return drive


def norm_first_kernel(x_ref, gain_ref, out_ref):
    x = x_ref[...].astype(f32)
    inv = lax.rsqrt(jnp.mean(x * x, axis=1, keepdims=True) + eps)
    out_ref[...] = (x * inv * gain_ref[...]).astype(bf16)


def branches_kernel(nf_ref, w0_ref, w1_ref, taps_ref, bias_ref, mask_ref, x_ref, y_ref, conv_ref):
    half, chan = w0_ref.shape[0], x_ref.shape[1]
    both = nn(nf_ref[:, :half], w0_ref[...]) + nn(nf_ref[:, half:], w1_ref[...])
    x_ref[...] = both[:, :chan]
    y_ref[...] = both[:, chan:]
    for c in range(0, chan, 128):
        cols = slice(c, c + 128)
        x = x_ref[:, cols]
        total = x * taps_ref[0:1, cols] + bias_ref[:, cols]
        for lag in range(1, taps_ref.shape[0]):
            total = total + down_rows(x, lag) * mask_ref[lag - 1] * taps_ref[lag : lag + 1, cols]
        conv_ref[:, cols] = total.astype(bf16)


def gates_of(rate, decay_logit, start):
    soft = softplus(-decay_logit)
    minus_log = 8.0 * rate * soft
    lost = one_less_exp(2.0 * minus_log)
    mult = jnp.where(start, 1.0, jnp.sqrt(lost))
    carried = jnp.where(start, 0.0, jnp.exp(-minus_log))
    return soft, mult, carried


def forward_scan_kernel(
    c0, c1, c2, c3, block_ref, rb_ref, ib_ref, dl_ref, y_ref, mask_ref,
    rate_ref, entry_ref, hidden_ref, mixed_ref,
):
    start = mask_ref[0] == 0.0
    pre = nn(jnp.concatenate([c0[...], c1[...], c2[...], c3[...]], axis=1), block_ref[0])
    rate = sigmoid(pre[:, :128] + rb_ref[...])
    entry = sigmoid(pre[:, 128:] + ib_ref[...])
    _, mult, carried = gates_of(rate, dl_ref[...], start)
    driven = c0[...].astype(f32) * entry * mult
    hidden = scan_rows(carried, driven, down_rows)
    rate_ref[...] = rate
    entry_ref[...] = entry
    hidden_ref[...] = hidden
    mixed_ref[...] = (hidden * gelu_pair(y_ref[...])[0]).astype(bf16)


def backward_scan_kernel(
    g_ref, w0_ref, w1_ref, c0, c1, c2, c3, block_ref, dl_ref, y_ref, mask_ref, rate_ref, entry_ref,
    hidden_ref,
    gy_ref, direct_ref, h1_ref, h2_ref, h3_ref, wg_ref, sums_ref,
):
    start = mask_ref[0] == 0.0
    half = w0_ref.shape[0]
    grad_mixed = nn(g_ref[:, :half], w0_ref[...]) + nn(g_ref[:, half:], w1_ref[...])
    hidden, rate, entry = hidden_ref[...], rate_ref[...], entry_ref[...]
    conv = c0[...].astype(f32)
    gelu_y, slope_y = gelu_pair(y_ref[...])
    gy_ref[...] = (grad_mixed * hidden * slope_y).astype(bf16)
    decay_logit = dl_ref[...]
    soft, mult, carried = gates_of(rate, decay_logit, start)
    state = scan_rows(up_rows(carried, 1), grad_mixed * gelu_y, up_rows)
    kept = carried * carried
    grad_log = jnp.where(
        start, 0.0, state * (down_rows(hidden, 1) * carried - conv * entry * kept / mult)
    )
    rate_low = (grad_log * (-8.0 * soft) * rate * (1.0 - rate)).astype(bf16)
    entry_low = (state * conv * mult * entry * (1.0 - entry)).astype(bf16)
    both = jnp.concatenate([rate_low, entry_low], axis=1)
    sums_ref[...] = jnp.concatenate(
        [
            jnp.sum(grad_log * rate, axis=0, keepdims=True) * (8.0 * sigmoid(-decay_logit)),
            jnp.sum(rate_low.astype(f32), axis=0, keepdims=True),
            jnp.sum(entry_low.astype(f32), axis=0, keepdims=True),
            jnp.zeros((5, 128), f32),
        ],
        axis=0,
    )
    heads = nt(both, block_ref[0])
    direct_ref[...] = state * entry * mult + heads[:, :128]
    h1_ref[...] = heads[:, 128:256].astype(bf16)
    h2_ref[...] = heads[:, 256:384].astype(bf16)
    h3_ref[...] = heads[:, 384:].astype(bf16)
    units = jnp.concatenate([c0[...], c1[...], c2[...], c3[...]], axis=1)
    grads = tn(units, both)
    first = jnp.concatenate([grads[:, 0:64], grads[:, 128:192]], axis=1)
    second = jnp.concatenate([grads[:, 64:128], grads[:, 192:256]], axis=1)
    for k in range(4):
        wg_ref[0, k] = first[k * 128 : k * 128 + 64]
        wg_ref[1, k] = second[k * 128 + 64 : k * 128 + 128]


def conv_back_kernel(direct_ref, r1, r2, r3, x_ref, taps_ref, mask_ref, gx_ref, sums_ref):
    total = direct_ref[...] + r1[...].astype(f32) + r2[...].astype(f32) + r3[...].astype(f32)
    x = x_ref[...]
    grad = total * taps_ref[0:1]
    sums = [jnp.sum(total * x, axis=0, keepdims=True)]
    for lag in range(1, taps_ref.shape[0]):
        kept = total * mask_ref[lag - 1]
        grad = grad + up_rows(kept, lag) * taps_ref[lag : lag + 1]
        sums.append(jnp.sum(kept * down_rows(x, lag), axis=0, keepdims=True))
    gx_ref[...] = grad.astype(bf16)
    sums.append(jnp.sum(total, axis=0, keepdims=True))
    sums.append(jnp.zeros((8 - len(sums), x.shape[1]), f32))
    sums_ref[...] = jnp.concatenate(sums, axis=0)


def split_rows(z_ref, total_ref, outs):
    rows = outs[0].shape[0]
    for k, out in enumerate(outs):
        at = pl.multiple_of((z_ref[0] ^ k) * rows, rows)
        out[...] = total_ref[pl.ds(at, rows), :].astype(out.dtype)


def product_split_kernel(z_ref, a_ref, w0_ref, w1_ref, o0, o1, o2, o3, total_ref):
    half = w0_ref.shape[0]
    total_ref[:, :half] = nt(a_ref[...], w0_ref[...])
    total_ref[:, half:] = nt(a_ref[...], w1_ref[...])
    split_rows(z_ref, total_ref, (o0, o1, o2, o3))


def assemble_kernel(z_ref, p0, p1, p2, p3, out_ref):
    rows = p0.shape[0]
    for k, piece in enumerate((p0, p1, p2, p3)):
        at = pl.multiple_of((z_ref[0] ^ k) * rows, rows)
        out_ref[pl.ds(at, rows), :] = piece[...].astype(out_ref.dtype)


def sum_pieces(pieces):
    total = pieces[0][...]
    for piece in pieces[1:]:
        total = total + piece[...].astype(f32)
    return total


def my_rows(z_ref, ref, rows):
    return ref[pl.ds(pl.multiple_of(z_ref[0] * rows, rows), rows), :].astype(f32)


def norm_second_kernel(z_ref, x_ref, gain_ref, o0, o1, o2, o3, res_ref, low_ref):
    residual = my_rows(z_ref, x_ref, res_ref.shape[0]) + sum_pieces((o0, o1, o2, o3))
    inv = lax.rsqrt(jnp.mean(residual * residual, axis=1, keepdims=True) + eps)
    res_ref[...] = residual
    low_ref[...] = (residual * inv * gain_ref[...]).astype(bf16)


def norm_back(x, gain, grad):
    inv = lax.rsqrt(jnp.mean(x * x, axis=1, keepdims=True) + eps)
    unit = x * inv
    scaled = grad * gain
    out = inv * (scaled - unit * jnp.mean(scaled * unit, axis=1, keepdims=True))
    return out, jnp.sum(grad * unit, axis=0, keepdims=True)


def second_back_kernel(z_ref, cot_ref, gain_ref, res_ref, o0, o1, o2, o3, gr_ref, low_ref, gain_out):
    grad, gain_grad = norm_back(res_ref[...], gain_ref[...], sum_pieces((o0, o1, o2, o3)))
    grad = grad + my_rows(z_ref, cot_ref, res_ref.shape[0])
    gr_ref[...] = grad
    low_ref[...] = grad.astype(bf16)
    gain_out[...] = gain_grad


def first_back_kernel(z_ref, x_ref, gain_ref, gr_ref, o0, o1, o2, o3, out_ref, gain_out):
    x = my_rows(z_ref, x_ref, gr_ref.shape[0])
    grad, gain_grad = norm_back(x, gain_ref[...], sum_pieces((o0, o1, o2, o3)))
    out_ref[...] = (gr_ref[...] + grad).astype(bf16)
    gain_out[...] = gain_grad


def block_out_kernel(res_ref, o0, o1, o2, o3, out_ref):
    out_ref[...] = (res_ref[...] + sum_pieces((o0, o1, o2, o3))).astype(bf16)


def ffn_kernel(first, last, *refs):
    refs = list(refs)
    z_ref = refs.pop(0)
    s_ref, cot_ref, w0_ref, w1_ref = refs[:4]
    refs = refs[4:]
    if not first:
        in_out, in_grad = refs[:2]
        refs = refs[2:]
    ggu_ref, mid_ref = refs[:2]
    refs = refs[2:]
    pre_ref, back_ref = refs[-2:]
    if last:
        out_pieces, grad_pieces = refs[:4], refs[4:8]
        acc_out, acc_grad = refs[8:10]
    else:
        acc_out, acc_grad = refs[:2]
    half, width = w0_ref.shape[0], mid_ref.shape[1]
    pre_ref[...] = nn(s_ref[:, :half], w0_ref[:, : 2 * width])
    pre_ref[...] += nn(s_ref[:, half:], w1_ref[:, : 2 * width])
    back_ref[...] = nn(cot_ref[:, :half], w0_ref[:, 2 * width :])
    back_ref[...] += nn(cot_ref[:, half:], w1_ref[:, 2 * width :])
    for c in range(0, width, 128):
        gate, up = pre_ref[:, c : c + 128], pre_ref[:, width + c : width + c + 128]
        back = back_ref[:, c : c + 128]
        gelu_gate, slope = gelu_pair(gate)
        mid_ref[:, c : c + 128] = (gelu_gate * up).astype(bf16)
        ggu_ref[:, c : c + 128] = (back * up * slope).astype(bf16)
        ggu_ref[:, width + c : width + c + 128] = (back * gelu_gate).astype(bf16)
    for lo, w_ref in ((0, w0_ref), (half, w1_ref)):
        cols = slice(lo, lo + half)
        out = nt(mid_ref[...], w_ref[:, 2 * width :])
        acc_out[:, cols] = out if first else in_out[:, cols] + out
        grad = nt(ggu_ref[...], w_ref[:, : 2 * width])
        acc_grad[:, cols] = grad if first else in_grad[:, cols] + grad
    if last:
        split_rows(z_ref, acc_out, out_pieces)
        split_rows(z_ref, acc_grad, grad_pieces)


def grads_out_kernel(sides, *refs):
    lefts, rights, out = refs[:sides], refs[sides : 2 * sides], refs[2 * sides]
    at = 0
    for left, right in zip(lefts, rights):
        half, width = left.shape[1] // 2, right.shape[1]
        out[:, at : at + width] = tn(left[:, half:], right[...]).astype(bf16)
        at += width


def grads_own_kernel(sides, *refs):
    lefts, rights = refs[:sides], refs[sides : 2 * sides]
    got, own, x_top, y_bot, send_x, send_y = refs[2 * sides :]
    at = 0
    q = x_top.shape[0]
    for left, right in zip(lefts, rights):
        half, width = left.shape[1] // 2, right.shape[1]
        cols = slice(at, at + width)
        at += width
        near = tn(left[:, : half // 2], right[...]) + got[: half // 2, cols].astype(f32)
        own[:, cols] = near[: 2 * q]
        x_top[:, cols] = near[2 * q : 3 * q]
        send_x[q:, cols] = near[3 * q :].astype(bf16)
        far = tn(left[:, half // 2 : half], right[...]) + got[half // 2 :, cols].astype(f32)
        send_y[q:, cols] = far[:q].astype(bf16)
        y_bot[:, cols] = far[q : 2 * q]
        send_y[:q, cols] = far[2 * q : 3 * q].astype(bf16)
        send_x[:q, cols] = far[3 * q :].astype(bf16)


def exchange(v, axis, size, bit):
    return lax.ppermute(v, axis, [(i, i ^ bit) for i in range(size)])


def after(v, *others):
    return lax.optimization_barrier((v,) + others)[0]


def gather_rows(shard, size, before):
    if before:
        shard = after(shard, *before)
    if size == 8:
        half = shard.shape[0] // 2
        by_x = exchange(shard, "dp", size, 2)
        by_y = exchange(shard, "dp", size, 4)
        top = exchange(by_x[:half], "dp", size, 4)
        bottom = exchange(by_y[half:], "dp", size, 2)
        mine = jnp.concatenate([shard, by_x, by_y, top, bottom], axis=0)
        marks = (by_x, by_y)
    else:
        mine, bit = shard, 2
        while bit < size:
            mine = jnp.concatenate([mine, exchange(mine, "dp", size, bit)], axis=0)
            bit *= 2
        marks = (mine,)
    return mine, exchange(mine, "dp", size, 1), marks


def scatter_grads(lefts, rights, size):
    sides, model = len(lefts), lefts[0].shape[1]
    tokens = lefts[0].shape[0]
    width = sum(r.shape[1] for r in rights)
    flops = tokens * model * width
    out = call(
        partial(grads_out_kernel, sides), [like((model // 2, width), bf16)], *lefts, *rights,
        flops=flops, name="grads_out",
    )[0]
    got = exchange(out, "dp", size, 1)
    q = model // 16
    own, x_top, y_bot, send_x, send_y = call(
        partial(grads_own_kernel, sides),
        [like((2 * q, width), f32), like((q, width), f32), like((q, width), f32),
         like((2 * q, width), bf16), like((2 * q, width), bf16)],
        *lefts, *rights, got, flops=flops, name="grads_own",
    )
    if size == 8:
        from_x = exchange(send_x, "dp", size, 2)
        from_y = exchange(send_y, "dp", size, 4)
        last_x = exchange((x_top + from_y[:q].astype(f32)).astype(bf16), "dp", size, 2)
        last_y = exchange((y_bot + from_x[:q].astype(f32)).astype(bf16), "dp", size, 4)
        return jnp.concatenate(
            [
                own[:q] + from_y[q:].astype(f32) + last_x.astype(f32),
                own[q:] + from_x[q:].astype(f32) + last_y.astype(f32),
            ],
            axis=0,
        )
    total = jnp.concatenate(
        [own, x_top, send_x[q:].astype(f32), send_y[q:].astype(f32), y_bot,
         send_y[:q].astype(f32), send_x[:q].astype(f32)],
        axis=0,
    )
    bit = size // 2
    while bit > 1:
        half = total.shape[0] // 2
        total = total[:half] + exchange(total[half:].astype(bf16), "dp", size, bit).astype(f32)
        bit //= 2
    return total


def send_rows(pieces):
    return [pieces[0]] + [exchange(pieces[k], "tensor", 4, k) for k in range(1, 4)]


def spread_rows(piece):
    return [piece] + [exchange(piece, "tensor", 4, k) for k in range(1, 4)]


def sum_over(v, axis, size):
    bit = 1
    while bit < size:
        v = v + exchange(v, axis, size, bit)
        bit *= 2
    return v


def body(
    tokens, segments, first_gain, x_weight, y_weight, conv_weight, conv_bias, rate_weight,
    input_weight, rate_bias, input_bias, decay_logit, out_weight, second_gain, gate_weight,
    up_weight, down_weight, cotangent, dp_size,
):
    count, model = tokens.shape
    heads, _, units = rate_weight.shape
    chan = heads * units
    pairs = heads // 2
    taps = conv_weight.shape[0]
    hidden_units = gate_weight.shape[1]
    width = hidden_units // chunk_count
    me = lax.axis_index("dp")
    z = lax.axis_index("tensor").astype(jnp.int32)
    z_arr = z.reshape(1)
    part = model // dp_size
    order = [2 * j + c for c in range(2) for j in range(dp_size // 2)]
    rows = count // 4

    def to_rel(v):
        return jnp.concatenate(
            [lax.dynamic_slice_in_dim(v, (me ^ r) * part, part, axis=-1) for r in order], axis=-1
        )

    def to_abs(v):
        places = []
        for s in range(dp_size):
            rel = me ^ s
            places.append((rel % 2) * (dp_size // 2) + rel // 2)
        return jnp.concatenate(
            [lax.dynamic_slice_in_dim(v, p * part, part, axis=-1) for p in places], axis=-1
        )

    xy_shard = jnp.concatenate([x_weight.reshape(part, chan), y_weight.reshape(part, chan)], axis=1)
    out_shard = out_weight.reshape(chan, part).T
    down_shard = down_weight.T
    ffn_shards = [
        jnp.concatenate(
            [v[:, c * width : (c + 1) * width] for v in (gate_weight, up_weight, down_shard)], axis=1
        )
        for c in range(chunk_count)
    ]
    xy0, xy1, marks = gather_rows(xy_shard, dp_size, None)
    out0, out1, marks = gather_rows(out_shard, dp_size, marks)
    ffn_weights = []
    for shard in ffn_shards:
        w0, w1, marks = gather_rows(shard, dp_size, marks)
        ffn_weights.append((w0, w1))

    x_rel = to_rel(tokens)
    cot_rel = to_rel(cotangent)
    gain_one = to_rel(first_gain).reshape(1, model)
    gain_two = to_rel(second_gain).reshape(1, model)
    masks = jnp.stack(
        [
            jnp.concatenate([jnp.full((lag,), -1, jnp.int32), segments[:-lag]]) == segments
            for lag in range(1, taps)
        ]
    ).astype(f32)
    masks = jnp.broadcast_to(masks[:, :, None], (taps - 1, count, 128))
    wide_masks = masks
    taps_flat = conv_weight.reshape(taps, chan)
    bias_flat = conv_bias.reshape(1, chan)
    rate_flat, input_flat = rate_bias.reshape(1, chan), input_bias.reshape(1, chan)
    decay_flat = decay_logit.reshape(1, chan)
    both = jnp.stack([rate_weight, input_weight], axis=2).reshape(pairs, 2, 4, units, 2, units)
    both = jnp.stack([lax.dynamic_index_in_dim(both, z ^ k, 2, False) for k in range(4)], axis=1)
    zero = jnp.zeros((pairs, 4, units, 2, units), bf16)
    blocks = jnp.stack(
        [jnp.stack([both[:, :, 0], zero], axis=4), jnp.stack([zero, both[:, :, 1]], axis=4)], axis=2
    ).reshape(pairs, 8 * units, 4 * units)

    nf = call(norm_first_kernel, [like((count, model), bf16)], x_rel, gain_one, name="norm_first")[0]
    x_branch, y_branch, conv_low = call(
        branches_kernel,
        [like((count, chan), f32), like((count, chan), f32), like((count, chan), bf16)],
        nf, xy0, xy1, taps_flat, bias_flat, masks, flops=4 * count * model * chan, name="branches",
    )
    conv = spread_rows(conv_low)
    lane = pl.BlockSpec((count, 128), lambda p: (0, p))
    line = pl.BlockSpec((1, 128), lambda p: (0, p))
    block_spec = pl.BlockSpec((1, 8 * units, 4 * units), lambda p: (p, 0, 0))
    mask_spec = pl.BlockSpec((taps - 1, count, 128), lambda p: (0, 0, 0))
    rate, entry, hidden, mixed = pl.pallas_call(
        forward_scan_kernel,
        grid=(pairs,),
        in_specs=[lane] * 4 + [block_spec] + [line] * 3 + [lane, mask_spec],
        out_specs=[lane] * 4,
        out_shape=[like((count, chan), f32)] * 3 + [like((count, chan), bf16)],
        compiler_params=pltpu.CompilerParams(vmem_limit_bytes=24 * MIB),
        cost_estimate=pl.CostEstimate(
            flops=pairs * count * 512 * 256 * 2, bytes_accessed=6 * MIB, transcendentals=0),
        name="forward_scan",
    )(*conv, blocks, rate_flat, input_flat, decay_flat, y_branch, masks)

    def product_split(a, w0, w1, name):
        return pl.pallas_call(
            product_split_kernel,
            out_shape=[like((rows, model), f32)] + [like((rows, model), bf16)] * 3,
            in_specs=[smem] + [vmem] * 3,
            out_specs=[vmem] * 4,
            scratch_shapes=[pltpu.VMEM((count, model), f32)],
            compiler_params=pltpu.CompilerParams(vmem_limit_bytes=32 * MIB),
            cost_estimate=pl.CostEstimate(
                flops=2 * count * model * a.shape[1], bytes_accessed=2 * w0.size * 2,
                transcendentals=0),
            name=name,
        )(z_arr, a, w0, w1)

    def assemble(pieces, dtype, name):
        return call(assemble_kernel, [like((count, model), dtype)], z_arr, *pieces, scalars=1, name=name)[0]

    pieces = send_rows(product_split(mixed, out0, out1, "recurrent"))
    residual, second_rows = call(
        norm_second_kernel, [like((rows, model), f32), like((rows, model), bf16)],
        z_arr, x_rel, gain_two, *pieces, scalars=1, name="norm_second",
    )
    second = assemble(spread_rows(second_rows), bf16, "second_all")

    ffn_grads = []
    sums = None
    for c, (w0, w1) in enumerate(ffn_weights):
        first, last = c == 0, c == chunk_count - 1
        outs = [like((count, 2 * width), bf16), like((count, width), bf16)]
        scratch = [pltpu.VMEM((count, 2 * width), f32), pltpu.VMEM((count, width), f32)]
        if last:
            outs += ([like((rows, model), f32)] + [like((rows, model), bf16)] * 3) * 2
            scratch = [pltpu.VMEM((count, model), f32)] * 2 + scratch
        else:
            outs += [like((count, model), f32)] * 2
        ins = [z_arr, second, cot_rel, w0, w1] + ([] if first else sums)
        res = pl.pallas_call(
            partial(ffn_kernel, first, last),
            out_shape=outs,
            in_specs=[smem] + [vmem] * (len(ins) - 1),
            out_specs=[vmem] * len(outs),
            scratch_shapes=scratch,
            compiler_params=pltpu.CompilerParams(vmem_limit_bytes=56 * MIB),
            cost_estimate=pl.CostEstimate(
                flops=12 * count * model * width, bytes_accessed=25 * MIB, transcendentals=0),
            name="ffn_%d" % c,
        )(*ins)
        ffn_grads.append((res[0], res[1]))
        sums = list(res[2:])
    out_pieces, grad_pieces = sums[:4], sums[4:]

    grad_pieces = send_rows(grad_pieces)
    grad_res, rec_rows, second_gain_part = call(
        second_back_kernel,
        [like((rows, model), f32), like((rows, model), bf16), like((1, model), f32)],
        z_arr, cot_rel, gain_two, residual, *grad_pieces, scalars=1, name="second_back",
    )
    grad_rec = assemble(spread_rows(rec_rows), bf16, "grad_rec_all")

    ffn_shares = [
        scatter_grads([second, cot_rel], [ggu, mid], dp_size) for ggu, mid in ffn_grads
    ]

    out_pieces = send_rows(out_pieces)
    block_rows = call(block_out_kernel, [like((rows, model), bf16)], residual, *out_pieces, name="block_out")[0]
    block_out = assemble(spread_rows(to_abs(block_rows)), bf16, "block_out_all")

    half_spec = pl.BlockSpec((model // 2, 128), lambda p: (0, p))
    whole = pl.BlockSpec((count, model), lambda p: (0, 0))
    gate_spec = pl.BlockSpec((2, 4, units, 2 * units), lambda p: (p, 0, 0, 0))
    grad_y, direct, h1, h2, h3, gate_grads, scan_sums = pl.pallas_call(
        backward_scan_kernel,
        grid=(pairs,),
        in_specs=[whole, half_spec, half_spec] + [lane] * 4 + [block_spec, line, lane, mask_spec]
        + [lane] * 3,
        out_specs=[lane, lane, lane, lane, lane, gate_spec, pl.BlockSpec((8, 128), lambda p: (0, p))],
        out_shape=[like((count, chan), bf16), like((count, chan), f32)]
        + [like((count, chan), bf16)] * 3
        + [like((heads, 4, units, 2 * units), f32), like((8, chan), f32)],
        compiler_params=pltpu.CompilerParams(vmem_limit_bytes=32 * MIB),
        cost_estimate=pl.CostEstimate(
            flops=2 * count * model * chan + pairs * count * 512 * 256 * 4, bytes_accessed=12 * MIB,
            transcendentals=0),
        name="backward_scan",
    )(grad_rec, out0, out1, *conv, blocks, decay_flat, y_branch, masks, rate, entry, hidden)
    out_share = scatter_grads([grad_rec], [mixed], dp_size)
    got = send_rows([direct, h1, h2, h3])
    grad_x, conv_sums = pl.pallas_call(
        conv_back_kernel,
        grid=(pairs,),
        in_specs=[lane] * 5 + [pl.BlockSpec((taps, 128), lambda p: (0, p)), mask_spec],
        out_specs=[lane, pl.BlockSpec((8, 128), lambda p: (0, p))],
        out_shape=[like((count, chan), bf16), like((8, chan), f32)],
        compiler_params=pltpu.CompilerParams(vmem_limit_bytes=24 * MIB),
        cost_estimate=pl.CostEstimate(flops=0, bytes_accessed=4 * MIB, transcendentals=0),
        name="conv_back",
    )(*got, x_branch, taps_flat, masks)

    grad_xy = jnp.concatenate([grad_x, grad_y], axis=1)
    first_pieces = send_rows(product_split(grad_xy, xy0, xy1, "grad_first"))
    tokens_rows, first_gain_part = call(
        first_back_kernel, [like((rows, model), bf16), like((1, model), f32)],
        z_arr, x_rel, gain_one, grad_res, *first_pieces, scalars=1, name="first_back",
    )
    tokens_grad = assemble(spread_rows(to_abs(tokens_rows)), f32, "tokens_grad_all")
    xy_share = scatter_grads([nf], [grad_xy], dp_size)

    small = jnp.concatenate([scan_sums, conv_sums], axis=0)
    small = sum_over(small, "dp", dp_size)
    gains = to_abs(jnp.concatenate([first_gain_part, second_gain_part], axis=0))
    gains = sum_over(sum_over(gains, "tensor", 4), "dp", dp_size)
    gate_low = gate_grads.astype(bf16)
    bit = 1
    while bit < dp_size:
        gate_low = gate_low.astype(bf16)
        gate_low = gate_low.astype(f32) + exchange(gate_low, "dp", dp_size, bit).astype(f32)
        bit *= 2
    gate_sum = jnp.concatenate(
        [lax.dynamic_index_in_dim(gate_low, z ^ k, 1, False) for k in range(4)], axis=1
    )

    ffn_cat = [
        jnp.concatenate([s[:, k * width : (k + 1) * width] for s in ffn_shares], axis=1)
        for k in range(3)
    ]
    return (
        block_out,
        tokens_grad,
        gains[0],
        xy_share[:, :chan].reshape(part, heads, units),
        xy_share[:, chan:].reshape(part, heads, units),
        small[8 : 8 + taps].reshape(taps, heads, units),
        small[8 + taps].reshape(heads, units),
        gate_sum[:, :, :units],
        gate_sum[:, :, units:],
        small[1].reshape(heads, units),
        small[2].reshape(heads, units),
        small[0].reshape(heads, units),
        out_share.T.reshape(heads, units, part),
        gains[1],
        ffn_cat[0],
        ffn_cat[1],
        ffn_cat[2].T,
    )


def solution(mesh):
    return jax.shard_map(
        partial(body, dp_size=mesh.shape["dp"]),
        mesh=mesh,
        in_specs=(
            P("dp", None),
            P("dp"),
            P(),
            P("dp", None, "tensor"),
            P("dp", None, "tensor"),
            P(None, None, "tensor"),
            P(None, "tensor"),
            P(None, None, "tensor"),
            P(None, None, "tensor"),
            P(None, "tensor"),
            P(None, "tensor"),
            P(None, "tensor"),
            P(None, "tensor", "dp"),
            P(),
            P("dp", "tensor"),
            P("dp", "tensor"),
            P("tensor", "dp"),
            P("dp", None),
        ),
        out_specs=(
            P("dp", None),
            P("dp", None),
            P(),
            P("dp", None, "tensor"),
            P("dp", None, "tensor"),
            P(None, None, "tensor"),
            P(None, "tensor"),
            P(None, None, "tensor"),
            P(None, None, "tensor"),
            P(None, "tensor"),
            P(None, "tensor"),
            P(None, "tensor"),
            P(None, "tensor", "dp"),
            P(),
            P("dp", "tensor"),
            P("dp", "tensor"),
            P("tensor", "dp"),
        ),
        check_vma=False,
    )
```

time: 1730 us -> 858 us (0.50)
  waiting for transfers between devices: 1280 us -> 424 us
  starting transfers between devices: 1.84 us -> 147 us
  Pallas kernels: 0 us -> 122 us
  matrix products: 114 us -> 0 us
  local copies, waits for them, and re-layouts: 218 us -> 118 us
  other arithmetic: 64.5 us -> 35.4 us
  blocking collectives: 25.6 us -> 0 us
    ppermute x0 -> x91, waiting for transfers between devices: none -> 424 us  [exchange(): return lax.ppermute(v, axis, [(i, i ^ bit) for i in range(size)])]
    reduce_scatter x4 -> x0, waiting for transfers between devices: 422 us -> none  [the longest x1 134 us: body(): lax.psum_scatter(gate_grad, 'dp', scatter_dimension=0, tiled=True)]
    all_gather x7 -> x0, waiting for transfers between devices: 353 us -> none  [the longest x1 61.1 us: body(): lax.all_gather(x_weight, 'dp', axis=0, tiled=True)]
    psum x4 -> x0, waiting for transfers between devices: 347 us -> none  [the longest x1 104 us: body(): lax.psum(jnp.dot(ffn_low, down_cols, preferred_element_type=jnp.float32),...]
    unnamed x21 -> x0, waiting for transfers between devices: 156 us -> none
    ppermute x0 -> x91, starting transfers between devices: none -> 147 us  [exchange(): return lax.ppermute(v, axis, [(i, i ^ bit) for i in range(size)])]
    pallas_call x0 -> x28, Pallas kernels: none -> 122 us  [the longest x20 56.7 us: call(): pl.pallas_call(kernel, out_shape=outs, in_specs=[smem] * scalars + [vmem]...]
    dot_general x19 -> x0, matrix products: 105 us -> none  [the longest x1 11.2 us: body(): jnp.einsum('tf,td->fd', ffn_low, cotangent, preferred_element_type=jnp.fl...]
  transfers between devices with their start and end apart: 18 -> 91, of which waited for: 18 -> 47; matrix products, arithmetic and copies ran while one was open for 11% -> 12% of each run, Pallas kernels for 0% -> 14%
where the time goes in v1:
time: 858 us; the launch traced here: 849 us
  waiting for transfers between devices  424 us (49%)
  starting transfers between devices  147 us (17%)
  Pallas kernels  122 us (14%)
  local copies, waits for them, and re-layouts  118 us (14%)
  other arithmetic  35.4 us (4%)
    ppermute x91, waiting for transfers between devices, exchange(): return lax.ppermute(v, axis, [(i, i ^ bit) for i in range(size)])  424 us
    ppermute x91, starting transfers between devices, exchange(): return lax.ppermute(v, axis, [(i, i ^ bit) for i in range(size)])  147 us
    unnamed x317, local copies, waits for them, and re-layouts  65.4 us
    pallas_call x20, Pallas kernels, call(): pl.pallas_call(kernel, out_shape=outs, in_specs=[smem] * scalars + [vmem]...  56.7 us
    pallas_call x3, Pallas kernels, body(): pl.pallas_call(partial(ffn_kernel, first, last), out_shape=outs, in_specs...  39.4 us
  transfers between devices with their start and end apart: 91, of which 47 were waited for; matrix products, arithmetic and copies ran while one was open for 12% of the time, Pallas kernels for 14%

profile of v1, /device:TPU:0, one launch (start us, length us, event | category | flops | bytes accessed | tf_op | source)
XLA Modules:
  0.0 849.3 jit_solution(5733515099641191321)
XLA Ops:
  4.5 2.9 collective-permute-start
  12.1 13.7 %collective-permute-done = bf16[320,1280]{1,0:T(8,128)(2,1)S(1)} collective-permute-done((bf16[320,1280]{1,0:T(8,128)(2,1)}, bf16[320,1280]{1,0:T(8,128)(2,1)S(1)}, u32[]{:S(2)}, u32[]{:S(2)}) %collective-permute-start) | collective-permute-done | bytes 819232 | tf_op jit(solution)/shard_map/ppermute | solution.py:339
  29.6 7.8 collective-permute-done.8
  44.0 30.0 %collective-permute-done.2 = bf16[160,1280]{1,0:T(8,128)(2,1)S(1)} collective-permute-done((bf16[160,1280]{1,0:T(8,128)(2,1)S(1)}, bf16[160,1280]{1,0:T(8,128)(2,1)S(1)}, u32[]{:S(2)}, u32[]{:S(2)}) %collective-permute-start.2) | collective-permute-done | bytes 409632 | tf_op jit(solution)/shard_map/ppermute | solution.py:339
  84.5 34.4 %collective-permute-done.31 = bf16[160,1920]{1,0:T(8,128)(2,1)S(1)} collective-permute-done((bf16[160,1920]{1,0:T(8,128)(2,1)S(1)}, bf16[160,1920]{1,0:T(8,128)(2,1)S(1)}, u32[]{:S(2)}, u32[]{:S(2)}) %collective-permute-start.31) | collective-permute-done | bytes 614432 | tf_op jit(solution)/shard_map/ppermute | solution.py:339
  128.3 34.5 %collective-permute-done.28 = bf16[160,1920]{1,0:T(8,128)(2,1)S(1)} collective-permute-done((bf16[160,1920]{1,0:T(8,128)(2,1)S(1)}, bf16[160,1920]{1,0:T(8,128)(2,1)S(1)}, u32[]{:S(2)}, u32[]{:S(2)}) %collective-permute-start.28) | collective-permute-done | bytes 614432 | tf_op jit(solution)/shard_map/ppermute | solution.py:339
  169.6 10.5 %collective-permute-done.25 = bf16[160,1920]{1,0:T(8,128)(2,1)S(1)} collective-permute-done((bf16[160,1920]{1,0:T(8,128)(2,1)S(1)}, bf16[160,1920]{1,0:T(8,128)(2,1)S(1)}, u32[]{:S(2)}, u32[]{:S(2)}) %collective-permute-start.25) | collective-permute-done | bytes 614432 | tf_op jit(solution)/shard_map/ppermute | solution.py:339
  185.8 5.3 collective-permute-done.10
  193.3 4.6 collective-permute-done.11
  199.0 3.3 constant_dynamic-slice_fusion.16
  206.2 5.2 branches.1
  219.4 3.9 collective-permute-done.5.c1
  226.3 14.2 %collective-permute-done.6.c2 = bf16[256,640]{1,0:T(8,128)(2,1)S(1)} collective-permute-done((bf16[256,640]{1,0:T(8,128)(2,1)S(1)}, bf16[256,640]{1,0:T(8,128)(2,1)S(1)}, u32[]{:S(2)}, u32[]{:S(2)}) %collective-permute-start.6) | collective-permute-done | bytes 327712 | tf_op jit(solution)/shard_map/ppermute | solution.py:339
  240.5 3.5 collective-permute-start.7
  245.3 4.2 copy.53
  249.6 5.3 reshape.123.block_ref
  258.4 4.9 forward_scan.1
  265.8 4.1 recurrent.1
  273.4 12.8 %collective-permute-done.13.o1 = bf16[64,2560]{1,0:T(8,128)(2,1)S(1)} collective-permute-done((bf16[64,2560]{1,0:T(8,128)(2,1)S(1)}, bf16[64,2560]{1,0:T(8,128)(2,1)S(1)}, u32[]{:S(2)}, u32[]{:S(2)}) %collective-permute-start.13) | collective-permute-done | bytes 327712 | tf_op jit(solution)/shard_map/ppermute | solution.py:339
  289.3 9.0 %collective-permute-done.14.o2 = bf16[64,2560]{1,0:T(8,128)(2,1)S(1)} collective-permute-done((bf16[64,2560]{1,0:T(8,128)(2,1)}, bf16[64,2560]{1,0:T(8,128)(2,1)S(1)}, u32[]{:S(2)}, u32[]{:S(2)}) %collective-permute-start.14) | collective-permute-done | bytes 327712 | tf_op jit(solution)/shard_map/ppermute | solution.py:339
  304.2 5.7 collective-permute-start.16
  310.0 13.4 %collective-permute-done.16.p1 = bf16[64,2560]{1,0:T(8,128)(2,1)S(1)} collective-permute-done((bf16[64,2560]{1,0:T(8,128)(2,1)S(1)}, bf16[64,2560]{1,0:T(8,128)(2,1)S(1)}, u32[]{:S(2)}, u32[]{:S(2)}) %collective-permute-start.16) | collective-permute-done | bytes 327712 | tf_op jit(solution)/shard_map/ppermute | solution.py:339
  324.9 3.8 concatenate.107.refs_2_.cot_ref.refs_1_
  328.7 4.6 collective-permute-done.17.p2
  334.5 12.1 %ffn_0.1 = (bf16[256,1280]{1,0:T(8,128)(2,1)}, bf16[256,640]{1,0:T(8,128)(2,1)}, f32[256,2560]{1,0:T(8,128)}, f32[256,2560]{1,0:T(8,128)}) custom-call(s32[1]{0:T(128)} %bitcast.z_ref.refs_0_, bf16[256,2560]{1,0:T(8,128)(2,1)} %copy-done.2, bf16[256,2560]{1,0:T(8,128)(2,1)} %concatenate.107.refs_2_.cot_ref.refs_1_, ...), custom_call_target="tpu_custom_call" | custom-call | flops 5033164800 | bytes 26214400 | tf_op jit(solution)/shard_map/ffn_0/pallas_call | solution.py:555
  348.7 3.9 grads_out.7
  352.5 13.6 %ffn_1.1 = (bf16[256,1280]{1,0:T(8,128)(2,1)}, bf16[256,640]{1,0:T(8,128)(2,1)}, f32[256,2560]{1,0:T(8,128)}, f32[256,2560]{1,0:T(8,128)}) custom-call(s32[1]{0:T(128)} %bitcast.z_ref.refs_0_, bf16[256,2560]{1,0:T(8,128)(2,1)} %copy-done.2, bf16[256,2560]{1,0:T(8,128)(2,1)} %concatenate.107.refs_2_.cot_ref.refs_1_, ...), custom_call_target="tpu_custom_call" | custom-call | flops 5033164800 | bytes 26214400 | tf_op jit(solution)/shard_map/ffn_1/pallas_call | solution.py:555
  366.2 13.6 %ffn_2.1 = (bf16[256,1280]{1,0:T(8,128)(2,1)}, bf16[256,640]{1,0:T(8,128)(2,1)}, f32[64,2560]{1,0:T(8,128)}, bf16[64,2560]{1,0:T(8,128)(2,1)}, bf16[64,2560]{1,0...) custom-call(s32[1]{0:T(128)} %bitcast.z_ref.refs_0_, ...), custom_call_target="tpu_custom_call" | custom-call | flops 5033164800 | bytes 26214400 | tf_op jit(solution)/shard_map/ffn_2/pallas_call | solution.py:555
  379.8 7.4 collective-permute-start.40
  389.6 12.7 %collective-permute-done.40.o1 = bf16[64,2560]{1,0:T(8,128)(2,1)S(1)} collective-permute-done((bf16[64,2560]{1,0:T(8,128)(2,1)}, bf16[64,2560]{1,0:T(8,128)(2,1)S(1)}, u32[]{:S(2)}, u32[]{:S(2)}) %collective-permute-start.40) | collective-permute-done | bytes 327712 | tf_op jit(solution)/shard_map/ppermute | solution.py:339
  402.3 10.6 %collective-permute-done.41.o2 = bf16[64,2560]{1,0:T(8,128)(2,1)S(1)} collective-permute-done((bf16[64,2560]{1,0:T(8,128)(2,1)}, bf16[64,2560]{1,0:T(8,128)(2,1)S(1)}, u32[]{:S(2)}, u32[]{:S(2)}) %collective-permute-start.41) | collective-permute-done | bytes 327712 | tf_op jit(solution)/shard_map/ppermute | solution.py:339
  415.5 6.9 collective-permute-start.43
  424.9 10.8 %collective-permute-done.43.p1 = bf16[64,2560]{1,0:T(8,128)(2,1)S(1)} collective-permute-done((bf16[64,2560]{1,0:T(8,128)(2,1)S(1)}, bf16[64,2560]{1,0:T(8,128)(2,1)S(1)}, u32[]{:S(2)}, u32[]{:S(2)}) %collective-permute-start.43) | collective-permute-done | bytes 327712 | tf_op jit(solution)/shard_map/ppermute | solution.py:339
  435.7 12.4 %collective-permute-done.44.p2 = bf16[64,2560]{1,0:T(8,128)(2,1)S(1)} collective-permute-done((bf16[64,2560]{1,0:T(8,128)(2,1)S(1)}, bf16[64,2560]{1,0:T(8,128)(2,1)S(1)}, u32[]{:S(2)}, u32[]{:S(2)}) %collective-permute-start.44) | collective-permute-done | bytes 327712 | tf_op jit(solution)/shard_map/ppermute | solution.py:339
  448.3 9.2 %backward_scan.1 = (bf16[256,640]{1,0:T(8,128)(2,1)S(1)}, f32[256,640]{1,0:T(8,128)S(1)}, bf16[256,640]{1,0:T(8,128)(2,1)S(1)}, bf16[256,640]{1,0:T(8,128)(2,1)S...) custom-call(bf16[256,2560]{1,0:T(8,128)(2,1)S(1)} %grad_rec_all.1.g_ref.refs_0_, ...), custom_call_target="tpu_custom_call" | custom-call | flops 1509949440 | bytes 12582912 | tf_op jit(solution)/shard_map/backward_scan/pallas_call | solution.py:589
  457.5 5.8 collective-permute-start.46
  466.8 12.0 %collective-permute-done.46.r1 = bf16[256,640]{1,0:T(8,128)(2,1)S(1)} collective-permute-done((bf16[256,640]{1,0:T(8,128)(2,1)S(1)}, bf16[256,640]{1,0:T(8,128)(2,1)S(1)}, u32[]{:S(2)}, u32[]{:S(2)}) %collective-permute-start.46) | collective-permute-done | bytes 327712 | tf_op jit(solution)/shard_map/ppermute | solution.py:339
  478.8 10.1 %collective-permute-done.47.r2 = bf16[256,640]{1,0:T(8,128)(2,1)S(1)} collective-permute-done((bf16[256,640]{1,0:T(8,128)(2,1)S(1)}, bf16[256,640]{1,0:T(8,128)(2,1)S(1)}, u32[]{:S(2)}, u32[]{:S(2)}) %collective-permute-start.47) | collective-permute-done | bytes 327712 | tf_op jit(solution)/shard_map/ppermute | solution.py:339
  492.9 5.8 grad_first.1
  498.7 21.7 %collective-permute-start.49 = (bf16[64,2560]{1,0:T(8,128)(2,1)S(1)}, bf16[64,2560]{1,0:T(8,128)(2,1)S(1)}, u32[]{:S(2)}, u32[]{:S(2)}) collective-permute-start(bf16[64,2560]{1,0:T(8,128)(2,1)S(1)} %get-tuple-element.133), channel_id=1, source_target_pairs={{0,1},{1,0},{2,3},{3,2},{4,5},{5,4},{6,7},{7,6},{8,9},{9,8},{10,11... | collective-permute-start | bytes 983048 | tf_op jit(solution)/shard_map/ppermute | solution.py:339
  525.1 3.8 grads_out.8
  538.7 6.5 collective-permute-done.50.o2
  545.3 7.3 collective-permute-start.37
  568.6 18.7 %collective-permute-done.38.p2 = bf16[64,2560]{1,0:T(8,128)(2,1)S(1)} collective-permute-done((bf16[64,2560]{1,0:T(8,128)(2,1)}, bf16[64,2560]{1,0:T(8,128)(2,1)S(1)}, u32[]{:S(2)}, u32[]{:S(2)}) %collective-permute-start.38) | collective-permute-done | bytes 327712 | tf_op jit(solution)/shard_map/ppermute | solution.py:339
  588.0 6.3 collective-permute-start.56
  599.2 5.8 collective-permute-done.66
  605.6 3.1 collective-permute-done.58
  609.2 3.6 collective-permute-done.67
  617.5 7.6 collective-permute-done.52.p1
  625.2 4.7 collective-permute-start.54
  635.0 10.1 %collective-permute-done.53.p2 = bf16[64,2560]{1,0:T(8,128)(2,1)S(1)} collective-permute-done((bf16[64,2560]{1,0:T(8,128)(2,1)}, bf16[64,2560]{1,0:T(8,128)(2,1)S(1)}, u32[]{:S(2)}, u32[]{:S(2)}) %collective-permute-start.53) | collective-permute-done | bytes 327712 | tf_op jit(solution)/shard_map/ppermute | solution.py:339
  645.7 3.7 grads_out.9
  655.1 6.7 grads_own.7
  686.5 15.7 %collective-permute-done.77 = bf16[320,1920]{1,0:T(8,128)(2,1)} collective-permute-done((bf16[320,1920]{1,0:T(8,128)(2,1)}, bf16[320,1920]{1,0:T(8,128)(2,1)}, u32[]{:S(2)}, u32[]{:S(2)}) %collective-permute-start.77) | collective-permute-done | bytes 1228832 | tf_op jit(solution)/shard_map/ppermute | solution.py:339
  705.0 5.7 collective-permute-done.79
  720.2 7.0 grads_own.8
  734.0 4.2 grads_own.5
  743.8 15.8 %collective-permute-done.82 = bf16[320,1920]{1,0:T(8,128)(2,1)} collective-permute-done((bf16[320,1920]{1,0:T(8,128)(2,1)}, bf16[320,1920]{1,0:T(8,128)(2,1)}, u32[]{:S(2)}, u32[]{:S(2)}) %collective-permute-start.82) | collective-permute-done | bytes 1228832 | tf_op jit(solution)/shard_map/ppermute | solution.py:339
  762.9 7.0 grads_own.9
  770.8 6.2 collective-permute-done.61
  783.6 15.6 %collective-permute-done.62 = bf16[160,1280]{1,0:T(8,128)(2,1)S(1)} collective-permute-done((bf16[160,1280]{1,0:T(8,128)(2,1)S(1)}, bf16[160,1280]{1,0:T(8,128)(2,1)S(1)}, u32[]{:S(2)}, u32[]{:S(2)}) %collective-permute-start.62) | collective-permute-done | bytes 409632 | tf_op jit(solution)/shard_map/ppermute | solution.py:339
  800.6 11.5 %collective-permute-done.64 = bf16[160,1280]{1,0:T(8,128)(2,1)S(1)} collective-permute-done((bf16[160,1280]{1,0:T(8,128)(2,1)S(1)}, bf16[160,1280]{1,0:T(8,128)(2,1)S(1)}, u32[]{:S(2)}, u32[]{:S(2)}) %collective-permute-start.64) | collective-permute-done | bytes 409632 | tf_op jit(solution)/shard_map/ppermute | solution.py:339
  819.8 9.7 %collective-permute-done.89 = bf16[320,1920]{1,0:T(8,128)(2,1)} collective-permute-done((bf16[320,1920]{1,0:T(8,128)(2,1)}, bf16[320,1920]{1,0:T(8,128)(2,1)}, u32[]{:S(2)}, u32[]{:S(2)}) %collective-permute-start.89) | collective-permute-done | bytes 1228832 | tf_op jit(solution)/shard_map/ppermute | solution.py:339
  834.2 4.6 collective-permute-done.88
  (575 shorter events, 245.7 us)
Async XLA Ops:
  4.5 21.4 %collective-permute-start = (bf16[320,1280]{1,0:T(8,128)(2,1)}, bf16[320,1280]{1,0:T(8,128)(2,1)S(1)}, u32[]{:S(2)}, u32[]{:S(2)}) collective-permute-start(bf16[320,1280]{1,0:T(8,128)(2,1)} %get-tuple-element.268), channel_id=1, source_target_pairs={{0,8},{4,12},{8,0},{12,4},{16,24},{20,28},{24,16},{28,20},{1,9},{5... | collective-permute-start | bytes 2457608 | tf_op jit(solution)/shard_map/ppermute | solution.py:339
  7.4 19.9 %collective-permute-start.1 = (bf16[320,1280]{1,0:T(8,128)(2,1)}, bf16[320,1280]{1,0:T(8,128)(2,1)S(1)}, u32[]{:S(2)}, u32[]{:S(2)}) collective-permute-start(bf16[320,1280]{1,0:T(8,128)(2,1)} %get-tuple-element.268), channel_id=1, source_target_pairs={{0,16},{4,20},{8,24},{12,28},{16,0},{20,4},{24,8},{28,12},{1,17},{... | collective-permute-start | bytes 2457608 | tf_op jit(solution)/shard_map/ppermute | solution.py:339
  37.8 37.8 %collective-permute-start.19 = (bf16[320,1920]{1,0:T(8,128)(2,1)S(1)}, bf16[320,1920]{1,0:T(8,128)(2,1)S(1)}, u32[]{:S(2)}, u32[]{:S(2)}) collective-permute-start(bf16[320,1920]{1,0:T(8,128)(2,1)S(1)} %pad_maximum_fusion.8), channel_id=1, source_target_pairs={{0,8},{4,12},{8,0},{12,4},{16,24},{20,28},{24,16},{28,20},{1,9},{5... | collective-permute-start | bytes 3686408 | tf_op jit(solution)/shard_map/ppermute | solution.py:339
  39.1 36.4 %collective-permute-start.20 = (bf16[320,1920]{1,0:T(8,128)(2,1)S(1)}, bf16[320,1920]{1,0:T(8,128)(2,1)S(1)}, u32[]{:S(2)}, u32[]{:S(2)}) collective-permute-start(bf16[320,1920]{1,0:T(8,128)(2,1)S(1)} %pad_maximum_fusion.8), channel_id=1, source_target_pairs={{0,16},{4,20},{8,24},{12,28},{16,0},{20,4},{24,8},{28,12},{1,17},{... | collective-permute-start | bytes 3686408 | tf_op jit(solution)/shard_map/ppermute | solution.py:339
  40.8 33.2 %collective-permute-start.2 = (bf16[160,1280]{1,0:T(8,128)(2,1)S(1)}, bf16[160,1280]{1,0:T(8,128)(2,1)S(1)}, u32[]{:S(2)}, u32[]{:S(2)}) collective-permute-start(bf16[160,1280]{1,0:T(8,128)(2,1)S(1)} %slice.296), channel_id=1, source_target_pairs={{0,16},{4,20},{8,24},{12,28},{16,0},{20,4},{24,8},{28,12},{1,17},{... | collective-permute-start | bytes 1228808 | tf_op jit(solution)/shard_map/ppermute | solution.py:339
  41.4 33.4 %collective-permute-start.3 = (bf16[160,1280]{1,0:T(8,128)(2,1)S(1)}, bf16[160,1280]{1,0:T(8,128)(2,1)S(1)}, u32[]{:S(2)}, u32[]{:S(2)}) collective-permute-start(bf16[160,1280]{1,0:T(8,128)(2,1)S(1)} %slice.297), channel_id=1, source_target_pairs={{0,8},{4,12},{8,0},{12,4},{16,24},{20,28},{24,16},{28,20},{1,9},{5... | collective-permute-start | bytes 1228808 | tf_op jit(solution)/shard_map/ppermute | solution.py:339
  75.6 130.5 %collective-permute-start.4 = (bf16[1280,1280]{1,0:T(8,128)(2,1)}, bf16[1280,1280]{1,0:T(8,128)(2,1)}, u32[]{:S(2)}, u32[]{:S(2)}) collective-permute-start(bf16[1280,1280]{1,0:T(8,128)(2,1)} %constant_dynamic-update-slice_fusion.w0_ref), channel_id=1, source_target_pairs={{0,4},{4,0},{8,12},{12,8},{16,20},{20,16},{24,28},{28,24},{1,5},{5... | collective-permute-start | bytes 9830408 | tf_op jit(solution)/shard_map/ppermute | solution.py:339
  75.6 44.2 %collective-permute-start.21 = (bf16[320,1920]{1,0:T(8,128)(2,1)S(1)}, bf16[320,1920]{1,0:T(8,128)(2,1)S(1)}, u32[]{:S(2)}, u32[]{:S(2)}) collective-permute-start(bf16[320,1920]{1,0:T(8,128)(2,1)S(1)} %pad_maximum_fusion.7), channel_id=1, source_target_pairs={{0,8},{4,12},{8,0},{12,4},{16,24},{20,28},{24,16},{28,20},{1,9},{5... | collective-permute-start | bytes 3686408 | tf_op jit(solution)/shard_map/ppermute | solution.py:339
  76.6 43.2 %collective-permute-start.22 = (bf16[320,1920]{1,0:T(8,128)(2,1)S(1)}, bf16[320,1920]{1,0:T(8,128)(2,1)S(1)}, u32[]{:S(2)}, u32[]{:S(2)}) collective-permute-start(bf16[320,1920]{1,0:T(8,128)(2,1)S(1)} %pad_maximum_fusion.7), channel_id=1, source_target_pairs={{0,16},{4,20},{8,24},{12,28},{16,0},{20,4},{24,8},{28,12},{1,17},{... | collective-permute-start | bytes 3686408 | tf_op jit(solution)/shard_map/ppermute | solution.py:339
  79.0 39.9 %collective-permute-start.31 = (bf16[160,1920]{1,0:T(8,128)(2,1)S(1)}, bf16[160,1920]{1,0:T(8,128)(2,1)S(1)}, u32[]{:S(2)}, u32[]{:S(2)}) collective-permute-start(bf16[160,1920]{1,0:T(8,128)(2,1)S(1)} %slice.309), channel_id=1, source_target_pairs={{0,16},{4,20},{8,24},{12,28},{16,0},{20,4},{24,8},{28,12},{1,17},{... | collective-permute-start | bytes 1843208 | tf_op jit(solution)/shard_map/ppermute | solution.py:339
  81.1 39.8 %collective-permute-start.32 = (bf16[160,1920]{1,0:T(8,128)(2,1)S(1)}, bf16[160,1920]{1,0:T(8,128)(2,1)S(1)}, u32[]{:S(2)}, u32[]{:S(2)}) collective-permute-start(bf16[160,1920]{1,0:T(8,128)(2,1)S(1)} %slice.310), channel_id=1, source_target_pairs={{0,8},{4,12},{8,0},{12,4},{16,24},{20,28},{24,16},{28,20},{1,9},{5... | collective-permute-start | bytes 1843208 | tf_op jit(solution)/shard_map/ppermute | solution.py:339
  119.8 43.9 %collective-permute-start.23 = (bf16[320,1920]{1,0:T(8,128)(2,1)S(1)}, bf16[320,1920]{1,0:T(8,128)(2,1)S(1)}, u32[]{:S(2)}, u32[]{:S(2)}) collective-permute-start(bf16[320,1920]{1,0:T(8,128)(2,1)S(1)} %pad_maximum_fusion.6), channel_id=1, source_target_pairs={{0,8},{4,12},{8,0},{12,4},{16,24},{20,28},{24,16},{28,20},{1,9},{5... | collective-permute-start | bytes 3686408 | tf_op jit(solution)/shard_map/ppermute | solution.py:339
  121.7 44.8 %collective-permute-start.24 = (bf16[320,1920]{1,0:T(8,128)(2,1)S(1)}, bf16[320,1920]{1,0:T(8,128)(2,1)S(1)}, u32[]{:S(2)}, u32[]{:S(2)}) collective-permute-start(bf16[320,1920]{1,0:T(8,128)(2,1)S(1)} %pad_maximum_fusion.6), channel_id=1, source_target_pairs={{0,16},{4,20},{8,24},{12,28},{16,0},{20,4},{24,8},{28,12},{1,17},{... | collective-permute-start | bytes 3686408 | tf_op jit(solution)/shard_map/ppermute | solution.py:339
  123.3 39.6 %collective-permute-start.28 = (bf16[160,1920]{1,0:T(8,128)(2,1)S(1)}, bf16[160,1920]{1,0:T(8,128)(2,1)S(1)}, u32[]{:S(2)}, u32[]{:S(2)}) collective-permute-start(bf16[160,1920]{1,0:T(8,128)(2,1)S(1)} %slice.307), channel_id=1, source_target_pairs={{0,16},{4,20},{8,24},{12,28},{16,0},{20,4},{24,8},{28,12},{1,17},{... | collective-permute-start | bytes 1843208 | tf_op jit(solution)/shard_map/ppermute | solution.py:339
  125.0 40.4 %collective-permute-start.29 = (bf16[160,1920]{1,0:T(8,128)(2,1)S(1)}, bf16[160,1920]{1,0:T(8,128)(2,1)S(1)}, u32[]{:S(2)}, u32[]{:S(2)}) collective-permute-start(bf16[160,1920]{1,0:T(8,128)(2,1)S(1)} %slice.308), channel_id=1, source_target_pairs={{0,8},{4,12},{8,0},{12,4},{16,24},{20,28},{24,16},{28,20},{1,9},{5... | collective-permute-start | bytes 1843208 | tf_op jit(solution)/shard_map/ppermute | solution.py:339
  162.9 171.6 %collective-permute-start.33 = (bf16[1280,1920]{1,0:T(8,128)(2,1)}, bf16[1280,1920]{1,0:T(8,128)(2,1)}, u32[]{:S(2)}, u32[]{:S(2)}) collective-permute-start(bf16[1280,1920]{1,0:T(8,128)(2,1)} %constant_dynamic-update-slice_fusion.20.refs_3_), channel_id=1, source_target_pairs={{0,4},{4,0},{8,12},{12,8},{16,20},{20,16},{24,28},{28,24},{1,5},{5... | collective-permute-start | bytes 14745608 | tf_op jit(solution)/shard_map/ppermute | solution.py:339
  166.3 186.3 %collective-permute-start.30 = (bf16[1280,1920]{1,0:T(8,128)(2,1)}, bf16[1280,1920]{1,0:T(8,128)(2,1)}, u32[]{:S(2)}, u32[]{:S(2)}) collective-permute-start(bf16[1280,1920]{1,0:T(8,128)(2,1)} %constant_dynamic-update-slice_fusion.15.refs_3_), channel_id=1, source_target_pairs={{0,4},{4,0},{8,12},{12,8},{16,20},{20,16},{24,28},{28,24},{1,5},{5... | collective-permute-start | bytes 14745608 | tf_op jit(solution)/shard_map/ppermute | solution.py:339
  183.5 182.6 %collective-permute-start.27 = (bf16[1280,1920]{1,0:T(8,128)(2,1)}, bf16[1280,1920]{1,0:T(8,128)(2,1)}, u32[]{:S(2)}, u32[]{:S(2)}) collective-permute-start(bf16[1280,1920]{1,0:T(8,128)(2,1)} %constant_dynamic-update-slice_fusion.10.refs_3_), channel_id=1, source_target_pairs={{0,4},{4,0},{8,12},{12,8},{16,20},{20,16},{24,28},{28,24},{1,5},{5... | collective-permute-start | bytes 14745608 | tf_op jit(solution)/shard_map/ppermute | solution.py:339
  198.6 67.2 %collective-permute-start.12 = (bf16[1280,640]{1,0:T(8,128)(2,1)}, bf16[1280,640]{1,0:T(8,128)(2,1)}, u32[]{:S(2)}, u32[]{:S(2)}) collective-permute-start(bf16[1280,640]{1,0:T(8,128)(2,1)} %constant_dynamic-update-slice_fusion.5.w0_ref), channel_id=1, source_target_pairs={{0,4},{4,0},{8,12},{12,8},{16,20},{20,16},{24,28},{28,24},{1,5},{5... | collective-permute-start | bytes 4915208 | tf_op jit(solution)/shard_map/ppermute | solution.py:339
  273.4 24.9 %collective-permute-start.14 = (bf16[64,2560]{1,0:T(8,128)(2,1)}, bf16[64,2560]{1,0:T(8,128)(2,1)S(1)}, u32[]{:S(2)}, u32[]{:S(2)}) collective-permute-start(bf16[64,2560]{1,0:T(8,128)(2,1)} %get-tuple-element.101), channel_id=1, source_target_pairs={{0,2},{1,3},{2,0},{3,1},{4,6},{5,7},{6,4},{7,5},{8,10},{9,11},{10,... | collective-permute-start | bytes 983048 | tf_op jit(solution)/shard_map/ppermute | solution.py:339
  309.9 23.4 %collective-permute-start.17 = (bf16[64,2560]{1,0:T(8,128)(2,1)S(1)}, bf16[64,2560]{1,0:T(8,128)(2,1)S(1)}, u32[]{:S(2)}, u32[]{:S(2)}) collective-permute-start(bf16[64,2560]{1,0:T(8,128)(2,1)S(1)} %get-tuple-element.104.p0), channel_id=1, source_target_pairs={{0,2},{1,3},{2,0},{3,1},{4,6},{5,7},{6,4},{7,5},{8,10},{9,11},{10,... | collective-permute-start | bytes 983048 | tf_op jit(solution)/shard_map/ppermute | solution.py:339
  352.5 302.2 %collective-permute-start.76 = (bf16[1280,1920]{1,0:T(8,128)(2,1)}, bf16[1280,1920]{1,0:T(8,128)(2,1)}, u32[]{:S(2)}, u32[]{:S(2)}) collective-permute-start(bf16[1280,1920]{1,0:T(8,128)(2,1)} %grads_out.7), channel_id=1, source_target_pairs={{0,4},{4,0},{8,12},{12,8},{16,20},{20,16},{24,28},{28,24},{1,5},{5... | collective-permute-start | bytes 14745608 | tf_op jit(solution)/shard_map/ppermute | solution.py:339
  379.8 22.5 %collective-permute-start.40 = (bf16[64,2560]{1,0:T(8,128)(2,1)}, bf16[64,2560]{1,0:T(8,128)(2,1)S(1)}, u32[]{:S(2)}, u32[]{:S(2)}) collective-permute-start(bf16[64,2560]{1,0:T(8,128)(2,1)} %get-tuple-element.117), channel_id=1, source_target_pairs={{0,1},{1,0},{2,3},{3,2},{4,5},{5,4},{6,7},{7,6},{8,9},{9,8},{10,11... | collective-permute-start | bytes 983048 | tf_op jit(solution)/shard_map/ppermute | solution.py:339
  387.2 25.7 %collective-permute-start.41 = (bf16[64,2560]{1,0:T(8,128)(2,1)}, bf16[64,2560]{1,0:T(8,128)(2,1)S(1)}, u32[]{:S(2)}, u32[]{:S(2)}) collective-permute-start(bf16[64,2560]{1,0:T(8,128)(2,1)} %get-tuple-element.118), channel_id=1, source_target_pairs={{0,2},{1,3},{2,0},{3,1},{4,6},{5,7},{6,4},{7,5},{8,10},{9,11},{10,... | collective-permute-start | bytes 983048 | tf_op jit(solution)/shard_map/ppermute | solution.py:339
  388.1 24.8 %collective-permute-start.42 = (bf16[64,2560]{1,0:T(8,128)(2,1)}, bf16[64,2560]{1,0:T(8,128)(2,1)S(1)}, u32[]{:S(2)}, u32[]{:S(2)}) collective-permute-start(bf16[64,2560]{1,0:T(8,128)(2,1)} %get-tuple-element.119), channel_id=1, source_target_pairs={{0,3},{1,2},{2,1},{3,0},{4,7},{5,6},{6,5},{7,4},{8,11},{9,10},{10,... | collective-permute-start | bytes 983048 | tf_op jit(solution)/shard_map/ppermute | solution.py:339
  415.5 20.2 %collective-permute-start.43 = (bf16[64,2560]{1,0:T(8,128)(2,1)S(1)}, bf16[64,2560]{1,0:T(8,128)(2,1)S(1)}, u32[]{:S(2)}, u32[]{:S(2)}) collective-permute-start(bf16[64,2560]{1,0:T(8,128)(2,1)S(1)} %get-tuple-element.121.p0), channel_id=1, source_target_pairs={{0,1},{1,0},{2,3},{3,2},{4,5},{5,4},{6,7},{7,6},{8,9},{9,8},{10,11... | collective-permute-start | bytes 983048 | tf_op jit(solution)/shard_map/ppermute | solution.py:339
  422.4 25.6 %collective-permute-start.44 = (bf16[64,2560]{1,0:T(8,128)(2,1)S(1)}, bf16[64,2560]{1,0:T(8,128)(2,1)S(1)}, u32[]{:S(2)}, u32[]{:S(2)}) collective-permute-start(bf16[64,2560]{1,0:T(8,128)(2,1)S(1)} %get-tuple-element.121.p0), channel_id=1, source_target_pairs={{0,2},{1,3},{2,0},{3,1},{4,6},{5,7},{6,4},{7,5},{8,10},{9,11},{10,... | collective-permute-start | bytes 983048 | tf_op jit(solution)/shard_map/ppermute | solution.py:339
  423.4 24.7 %collective-permute-start.45 = (bf16[64,2560]{1,0:T(8,128)(2,1)S(1)}, bf16[64,2560]{1,0:T(8,128)(2,1)S(1)}, u32[]{:S(2)}, u32[]{:S(2)}) collective-permute-start(bf16[64,2560]{1,0:T(8,128)(2,1)S(1)} %get-tuple-element.121.p0), channel_id=1, source_target_pairs={{0,3},{1,2},{2,1},{3,0},{4,7},{5,6},{6,5},{7,4},{8,11},{9,10},{10,... | collective-permute-start | bytes 983048 | tf_op jit(solution)/shard_map/ppermute | solution.py:339
  457.5 21.3 %collective-permute-start.46 = (bf16[256,640]{1,0:T(8,128)(2,1)S(1)}, bf16[256,640]{1,0:T(8,128)(2,1)S(1)}, u32[]{:S(2)}, u32[]{:S(2)}) collective-permute-start(bf16[256,640]{1,0:T(8,128)(2,1)S(1)} %get-tuple-element.126), channel_id=1, source_target_pairs={{0,1},{1,0},{2,3},{3,2},{4,5},{5,4},{6,7},{7,6},{8,9},{9,8},{10,11... | collective-permute-start | bytes 983048 | tf_op jit(solution)/shard_map/ppermute | solution.py:339
  463.3 25.6 %collective-permute-start.47 = (bf16[256,640]{1,0:T(8,128)(2,1)S(1)}, bf16[256,640]{1,0:T(8,128)(2,1)S(1)}, u32[]{:S(2)}, u32[]{:S(2)}) collective-permute-start(bf16[256,640]{1,0:T(8,128)(2,1)S(1)} %get-tuple-element.127), channel_id=1, source_target_pairs={{0,2},{1,3},{2,0},{3,1},{4,6},{5,7},{6,4},{7,5},{8,10},{9,11},{10,... | collective-permute-start | bytes 983048 | tf_op jit(solution)/shard_map/ppermute | solution.py:339
  464.2 27.0 %collective-permute-start.48 = (bf16[256,640]{1,0:T(8,128)(2,1)S(1)}, bf16[256,640]{1,0:T(8,128)(2,1)S(1)}, u32[]{:S(2)}, u32[]{:S(2)}) collective-permute-start(bf16[256,640]{1,0:T(8,128)(2,1)S(1)} %get-tuple-element.128), channel_id=1, source_target_pairs={{0,3},{1,2},{2,1},{3,0},{4,7},{5,6},{6,5},{7,4},{8,11},{9,10},{10,... | collective-permute-start | bytes 983048 | tf_op jit(solution)/shard_map/ppermute | solution.py:339
  465.7 54.7 %collective-permute-start.34 = (bf16[64,2560]{1,0:T(8,128)(2,1)S(1)}, bf16[64,2560]{1,0:T(8,128)(2,1)S(1)}, u32[]{:S(2)}, u32[]{:S(2)}) collective-permute-start(bf16[64,2560]{1,0:T(8,128)(2,1)S(1)} %copy-done.145), channel_id=1, source_target_pairs={{0,1},{1,0},{2,3},{3,2},{4,5},{5,4},{6,7},{7,6},{8,9},{9,8},{10,11... | collective-permute-start | bytes 983048 | tf_op jit(solution)/shard_map/ppermute | solution.py:339
  478.8 44.8 %collective-permute-start.35 = (bf16[64,2560]{1,0:T(8,128)(2,1)S(1)}, bf16[64,2560]{1,0:T(8,128)(2,1)S(1)}, u32[]{:S(2)}, u32[]{:S(2)}) collective-permute-start(bf16[64,2560]{1,0:T(8,128)(2,1)S(1)} %copy-done.144), channel_id=1, source_target_pairs={{0,2},{1,3},{2,0},{3,1},{4,6},{5,7},{6,4},{7,5},{8,10},{9,11},{10,... | collective-permute-start | bytes 983048 | tf_op jit(solution)/shard_map/ppermute | solution.py:339
  488.9 34.7 %collective-permute-start.36 = (bf16[64,2560]{1,0:T(8,128)(2,1)S(1)}, bf16[64,2560]{1,0:T(8,128)(2,1)S(1)}, u32[]{:S(2)}, u32[]{:S(2)}) collective-permute-start(bf16[64,2560]{1,0:T(8,128)(2,1)S(1)} %copy-done.143), channel_id=1, source_target_pairs={{0,3},{1,2},{2,1},{3,0},{4,7},{5,6},{6,5},{7,4},{8,11},{9,10},{10,... | collective-permute-start | bytes 983048 | tf_op jit(solution)/shard_map/ppermute | solution.py:339
  498.7 31.4 %collective-permute-start.49 = (bf16[64,2560]{1,0:T(8,128)(2,1)S(1)}, bf16[64,2560]{1,0:T(8,128)(2,1)S(1)}, u32[]{:S(2)}, u32[]{:S(2)}) collective-permute-start(bf16[64,2560]{1,0:T(8,128)(2,1)S(1)} %get-tuple-element.133), channel_id=1, source_target_pairs={{0,1},{1,0},{2,3},{3,2},{4,5},{5,4},{6,7},{7,6},{8,9},{9,8},{10,11... | collective-permute-start | bytes 983048 | tf_op jit(solution)/shard_map/ppermute | solution.py:339
  520.4 24.9 %collective-permute-start.50 = (bf16[64,2560]{1,0:T(8,128)(2,1)}, bf16[64,2560]{1,0:T(8,128)(2,1)}, u32[]{:S(2)}, u32[]{:S(2)}) collective-permute-start(bf16[64,2560]{1,0:T(8,128)(2,1)} %get-tuple-element.134), channel_id=1, source_target_pairs={{0,2},{1,3},{2,0},{3,1},{4,6},{5,7},{6,4},{7,5},{8,10},{9,11},{10,... | collective-permute-start | bytes 983048 | tf_op jit(solution)/shard_map/ppermute | solution.py:339
  523.5 39.5 %collective-permute-start.68 = (bf16[10,4,64,128]{3,2,1,0:T(8,128)(2,1)}, bf16[10,4,64,128]{3,2,1,0:T(8,128)(2,1)}, u32[]{:S(2)}, u32[]{:S(2)}) collective-permute-start(bf16[10,4,64,128]{3,2,1,0:T(8,128)(2,1)} %convert_element_type.163), channel_id=1, source_target_pairs={{0,4},{4,0},{8,12},{12,8},{16,20},{20,16},{24,28},{28,24},{1,5},{5... | collective-permute-start | bytes 1966088 | tf_op jit(solution)/shard_map/ppermute | solution.py:339
  523.6 33.2 %collective-permute-start.51 = (bf16[64,2560]{1,0:T(8,128)(2,1)}, bf16[64,2560]{1,0:T(8,128)(2,1)}, u32[]{:S(2)}, u32[]{:S(2)}) collective-permute-start(bf16[64,2560]{1,0:T(8,128)(2,1)} %get-tuple-element.135), channel_id=1, source_target_pairs={{0,3},{1,2},{2,1},{3,0},{4,7},{5,6},{6,5},{7,4},{8,11},{9,10},{10,... | collective-permute-start | bytes 983048 | tf_op jit(solution)/shard_map/ppermute | solution.py:339
  530.8 182.9 %collective-permute-start.81 = (bf16[1280,1920]{1,0:T(8,128)(2,1)}, bf16[1280,1920]{1,0:T(8,128)(2,1)}, u32[]{:S(2)}, u32[]{:S(2)}) collective-permute-start(bf16[1280,1920]{1,0:T(8,128)(2,1)} %grads_out.8), channel_id=1, source_target_pairs={{0,4},{4,0},{8,12},{12,8},{16,20},{20,16},{24,28},{28,24},{1,5},{5... | collective-permute-start | bytes 14745608 | tf_op jit(solution)/shard_map/ppermute | solution.py:339
  556.8 74.7 %collective-permute-start.71 = (bf16[1280,640]{1,0:T(8,128)(2,1)}, bf16[1280,640]{1,0:T(8,128)(2,1)}, u32[]{:S(2)}, u32[]{:S(2)}) collective-permute-start(bf16[1280,640]{1,0:T(8,128)(2,1)} %grads_out.6), channel_id=1, source_target_pairs={{0,4},{4,0},{8,12},{12,8},{16,20},{20,16},{24,28},{28,24},{1,5},{5... | collective-permute-start | bytes 4915208 | tf_op jit(solution)/shard_map/ppermute | solution.py:339
  563.1 24.2 %collective-permute-start.38 = (bf16[64,2560]{1,0:T(8,128)(2,1)}, bf16[64,2560]{1,0:T(8,128)(2,1)S(1)}, u32[]{:S(2)}, u32[]{:S(2)}) collective-permute-start(bf16[64,2560]{1,0:T(8,128)(2,1)} %concatenate.114.p0), channel_id=1, source_target_pairs={{0,2},{1,3},{2,0},{3,1},{4,6},{5,7},{6,4},{7,5},{8,10},{9,11},{10,... | collective-permute-start | bytes 983048 | tf_op jit(solution)/shard_map/ppermute | solution.py:339
  565.1 22.9 %collective-permute-start.39 = (bf16[64,2560]{1,0:T(8,128)(2,1)}, bf16[64,2560]{1,0:T(8,128)(2,1)S(1)}, u32[]{:S(2)}, u32[]{:S(2)}) collective-permute-start(bf16[64,2560]{1,0:T(8,128)(2,1)} %concatenate.114.p0), channel_id=1, source_target_pairs={{0,3},{1,2},{2,1},{3,0},{4,7},{5,6},{6,5},{7,4},{8,11},{9,10},{10,... | collective-permute-start | bytes 983048 | tf_op jit(solution)/shard_map/ppermute | solution.py:339
  587.3 37.9 %collective-permute-start.69 = (bf16[10,4,64,128]{3,2,1,0:T(8,128)(2,1)}, bf16[10,4,64,128]{3,2,1,0:T(8,128)(2,1)}, u32[]{:S(2)}, u32[]{:S(2)}) collective-permute-start(bf16[10,4,64,128]{3,2,1,0:T(8,128)(2,1)} %add_convert_fusion.1), channel_id=1, source_target_pairs={{0,8},{4,12},{8,0},{12,4},{16,24},{20,28},{24,16},{28,20},{1,9},{5... | collective-permute-start | bytes 1966088 | tf_op jit(solution)/shard_map/ppermute | solution.py:339
  625.2 19.8 %collective-permute-start.53 = (bf16[64,2560]{1,0:T(8,128)(2,1)}, bf16[64,2560]{1,0:T(8,128)(2,1)S(1)}, u32[]{:S(2)}, u32[]{:S(2)}) collective-permute-start(bf16[64,2560]{1,0:T(8,128)(2,1)} %concatenate.116.p0), channel_id=1, source_target_pairs={{0,2},{1,3},{2,0},{3,1},{4,6},{5,7},{6,4},{7,5},{8,10},{9,11},{10,... | collective-permute-start | bytes 983048 | tf_op jit(solution)/shard_map/ppermute | solution.py:339
  625.2 24.3 %collective-permute-start.54 = (bf16[64,2560]{1,0:T(8,128)(2,1)}, bf16[64,2560]{1,0:T(8,128)(2,1)S(1)}, u32[]{:S(2)}, u32[]{:S(2)}) collective-permute-start(bf16[64,2560]{1,0:T(8,128)(2,1)} %concatenate.116.p0), channel_id=1, source_target_pairs={{0,3},{1,2},{2,1},{3,0},{4,7},{5,6},{6,5},{7,4},{8,11},{9,10},{10,... | collective-permute-start | bytes 983048 | tf_op jit(solution)/shard_map/ppermute | solution.py:339
  631.5 32.4 %collective-permute-start.70 = (bf16[10,4,64,128]{3,2,1,0:T(8,128)(2,1)S(1)}, bf16[10,4,64,128]{3,2,1,0:T(8,128)(2,1)S(1)}, u32[]{:S(2)}, u32[]{:S(2)}) collective-permute-start(bf16[10,4,64,128]{3,2,1,0:T(8,128)(2,1)S(1)} %add_convert_fusion), channel_id=1, source_target_pairs={{0,16},{4,20},{8,24},{12,28},{16,0},{20,4},{24,8},{28,12},{1,17},{... | collective-permute-start | bytes 1966088 | tf_op jit(solution)/shard_map/ppermute | solution.py:339
  645.0 19.7 %collective-permute-start.74 = (bf16[320,640]{1,0:T(8,128)(2,1)S(1)}, bf16[320,640]{1,0:T(8,128)(2,1)S(1)}, u32[]{:S(2)}, u32[]{:S(2)}) collective-permute-start(bf16[320,640]{1,0:T(8,128)(2,1)S(1)} %get-tuple-element.150), channel_id=1, source_target_pairs={{0,8},{4,12},{8,0},{12,4},{16,24},{20,28},{24,16},{28,20},{1,9},{5... | collective-permute-start | bytes 1228808 | tf_op jit(solution)/shard_map/ppermute | solution.py:339
  649.5 113.4 %collective-permute-start.86 = (bf16[1280,1920]{1,0:T(8,128)(2,1)}, bf16[1280,1920]{1,0:T(8,128)(2,1)}, u32[]{:S(2)}, u32[]{:S(2)}) collective-permute-start(bf16[1280,1920]{1,0:T(8,128)(2,1)} %grads_out.9), channel_id=1, source_target_pairs={{0,4},{4,0},{8,12},{12,8},{16,20},{20,16},{24,28},{28,24},{1,5},{5... | collective-permute-start | bytes 14745608 | tf_op jit(solution)/shard_map/ppermute | solution.py:339
  654.7 78.0 %collective-permute-start.60 = (bf16[1280,1280]{1,0:T(8,128)(2,1)}, bf16[1280,1280]{1,0:T(8,128)(2,1)}, u32[]{:S(2)}, u32[]{:S(2)}) collective-permute-start(bf16[1280,1280]{1,0:T(8,128)(2,1)} %grads_out.5), channel_id=1, source_target_pairs={{0,4},{4,0},{8,12},{12,8},{16,20},{20,16},{24,28},{28,24},{1,5},{5... | collective-permute-start | bytes 9830408 | tf_op jit(solution)/shard_map/ppermute | solution.py:339
  665.5 36.7 %collective-permute-start.77 = (bf16[320,1920]{1,0:T(8,128)(2,1)}, bf16[320,1920]{1,0:T(8,128)(2,1)}, u32[]{:S(2)}, u32[]{:S(2)}) collective-permute-start(bf16[320,1920]{1,0:T(8,128)(2,1)} %get-tuple-element.155), channel_id=1, source_target_pairs={{0,16},{4,20},{8,24},{12,28},{16,0},{20,4},{24,8},{28,12},{1,17},{... | collective-permute-start | bytes 3686408 | tf_op jit(solution)/shard_map/ppermute | solution.py:339
  682.1 28.6 %collective-permute-start.79 = (bf16[320,1920]{1,0:T(8,128)(2,1)S(1)}, bf16[320,1920]{1,0:T(8,128)(2,1)S(1)}, u32[]{:S(2)}, u32[]{:S(2)}) collective-permute-start(bf16[320,1920]{1,0:T(8,128)(2,1)S(1)} %copy-done.98), channel_id=1, source_target_pairs={{0,8},{4,12},{8,0},{12,4},{16,24},{20,28},{24,16},{28,20},{1,9},{5... | collective-permute-start | bytes 3686408 | tf_op jit(solution)/shard_map/ppermute | solution.py:339
  713.0 25.2 %collective-permute-start.78 = (bf16[160,1920]{1,0:T(8,128)(2,1)}, bf16[160,1920]{1,0:T(8,128)(2,1)}, u32[]{:S(2)}, u32[]{:S(2)}) collective-permute-start(bf16[160,1920]{1,0:T(8,128)(2,1)} %add_convert_fusion.7), channel_id=1, source_target_pairs={{0,8},{4,12},{8,0},{12,4},{16,24},{20,28},{24,16},{28,20},{1,9},{5... | collective-permute-start | bytes 1843208 | tf_op jit(solution)/shard_map/ppermute | solution.py:339
  713.7 25.6 %collective-permute-start.80 = (bf16[160,1920]{1,0:T(8,128)(2,1)}, bf16[160,1920]{1,0:T(8,128)(2,1)}, u32[]{:S(2)}, u32[]{:S(2)}) collective-permute-start(bf16[160,1920]{1,0:T(8,128)(2,1)} %add_convert_fusion.6), channel_id=1, source_target_pairs={{0,16},{4,20},{8,24},{12,28},{16,0},{20,4},{24,8},{28,12},{1,17},{... | collective-permute-start | bytes 1843208 | tf_op jit(solution)/shard_map/ppermute | solution.py:339
  729.3 30.3 %collective-permute-start.82 = (bf16[320,1920]{1,0:T(8,128)(2,1)}, bf16[320,1920]{1,0:T(8,128)(2,1)}, u32[]{:S(2)}, u32[]{:S(2)}) collective-permute-start(bf16[320,1920]{1,0:T(8,128)(2,1)} %get-tuple-element.162), channel_id=1, source_target_pairs={{0,16},{4,20},{8,24},{12,28},{16,0},{20,4},{24,8},{28,12},{1,17},{... | collective-permute-start | bytes 3686408 | tf_op jit(solution)/shard_map/ppermute | solution.py:339
  732.7 49.0 %collective-permute-start.84 = (bf16[320,1920]{1,0:T(8,128)(2,1)}, bf16[320,1920]{1,0:T(8,128)(2,1)S(1)}, u32[]{:S(2)}, u32[]{:S(2)}) collective-permute-start(bf16[320,1920]{1,0:T(8,128)(2,1)} %get-tuple-element.164), channel_id=1, source_target_pairs={{0,8},{4,12},{8,0},{12,4},{16,24},{20,28},{24,16},{28,20},{1,9},{5... | collective-permute-start | bytes 3686408 | tf_op jit(solution)/shard_map/ppermute | solution.py:339
  738.2 38.8 %collective-permute-start.61 = (bf16[320,1280]{1,0:T(8,128)(2,1)S(1)}, bf16[320,1280]{1,0:T(8,128)(2,1)S(1)}, u32[]{:S(2)}, u32[]{:S(2)}) collective-permute-start(bf16[320,1280]{1,0:T(8,128)(2,1)S(1)} %get-tuple-element.140), channel_id=1, source_target_pairs={{0,16},{4,20},{8,24},{12,28},{16,0},{20,4},{24,8},{28,12},{1,17},{... | collective-permute-start | bytes 2457608 | tf_op jit(solution)/shard_map/ppermute | solution.py:339
  739.3 41.1 %collective-permute-start.63 = (bf16[320,1280]{1,0:T(8,128)(2,1)S(1)}, bf16[320,1280]{1,0:T(8,128)(2,1)S(1)}, u32[]{:S(2)}, u32[]{:S(2)}) collective-permute-start(bf16[320,1280]{1,0:T(8,128)(2,1)S(1)} %get-tuple-element.142), channel_id=1, source_target_pairs={{0,8},{4,12},{8,0},{12,4},{16,24},{20,28},{24,16},{28,20},{1,9},{5... | collective-permute-start | bytes 2457608 | tf_op jit(solution)/shard_map/ppermute | solution.py:339
  761.6 70.6 %collective-permute-start.83 = (bf16[160,1920]{1,0:T(8,128)(2,1)}, bf16[160,1920]{1,0:T(8,128)(2,1)}, u32[]{:S(2)}, u32[]{:S(2)}) collective-permute-start(bf16[160,1920]{1,0:T(8,128)(2,1)} %add_convert_fusion.5), channel_id=1, source_target_pairs={{0,8},{4,12},{8,0},{12,4},{16,24},{20,28},{24,16},{28,20},{1,9},{5... | collective-permute-start | bytes 1843208 | tf_op jit(solution)/shard_map/ppermute | solution.py:339
  769.9 47.2 %collective-permute-start.87 = (bf16[320,1920]{1,0:T(8,128)(2,1)}, bf16[320,1920]{1,0:T(8,128)(2,1)}, u32[]{:S(2)}, u32[]{:S(2)}) collective-permute-start(bf16[320,1920]{1,0:T(8,128)(2,1)} %get-tuple-element.169), channel_id=1, source_target_pairs={{0,16},{4,20},{8,24},{12,28},{16,0},{20,4},{24,8},{28,12},{1,17},{... | collective-permute-start | bytes 3686408 | tf_op jit(solution)/shard_map/ppermute | solution.py:339
  777.1 22.2 %collective-permute-start.62 = (bf16[160,1280]{1,0:T(8,128)(2,1)S(1)}, bf16[160,1280]{1,0:T(8,128)(2,1)S(1)}, u32[]{:S(2)}, u32[]{:S(2)}) collective-permute-start(bf16[160,1280]{1,0:T(8,128)(2,1)S(1)} %add_convert_fusion.9), channel_id=1, source_target_pairs={{0,8},{4,12},{8,0},{12,4},{16,24},{20,28},{24,16},{28,20},{1,9},{5... | collective-permute-start | bytes 1228808 | tf_op jit(solution)/shard_map/ppermute | solution.py:339
  780.5 31.6 %collective-permute-start.64 = (bf16[160,1280]{1,0:T(8,128)(2,1)S(1)}, bf16[160,1280]{1,0:T(8,128)(2,1)S(1)}, u32[]{:S(2)}, u32[]{:S(2)}) collective-permute-start(bf16[160,1280]{1,0:T(8,128)(2,1)S(1)} %add_convert_fusion.8), channel_id=1, source_target_pairs={{0,16},{4,20},{8,24},{12,28},{16,0},{20,4},{24,8},{28,12},{1,17},{... | collective-permute-start | bytes 1228808 | tf_op jit(solution)/shard_map/ppermute | solution.py:339
  782.7 49.4 %collective-permute-start.85 = (bf16[160,1920]{1,0:T(8,128)(2,1)}, bf16[160,1920]{1,0:T(8,128)(2,1)}, u32[]{:S(2)}, u32[]{:S(2)}) collective-permute-start(bf16[160,1920]{1,0:T(8,128)(2,1)} %add_convert_fusion.4), channel_id=1, source_target_pairs={{0,16},{4,20},{8,24},{12,28},{16,0},{20,4},{24,8},{28,12},{1,17},{... | collective-permute-start | bytes 1843208 | tf_op jit(solution)/shard_map/ppermute | solution.py:339
  799.3 30.3 %collective-permute-start.89 = (bf16[320,1920]{1,0:T(8,128)(2,1)}, bf16[320,1920]{1,0:T(8,128)(2,1)}, u32[]{:S(2)}, u32[]{:S(2)}) collective-permute-start(bf16[320,1920]{1,0:T(8,128)(2,1)} %get-tuple-element.171), channel_id=1, source_target_pairs={{0,8},{4,12},{8,0},{12,4},{16,24},{20,28},{24,16},{28,20},{1,9},{5... | collective-permute-start | bytes 3686408 | tf_op jit(solution)/shard_map/ppermute | solution.py:339
  818.4 20.3 %collective-permute-start.88 = (bf16[160,1920]{1,0:T(8,128)(2,1)S(1)}, bf16[160,1920]{1,0:T(8,128)(2,1)S(1)}, u32[]{:S(2)}, u32[]{:S(2)}) collective-permute-start(bf16[160,1920]{1,0:T(8,128)(2,1)S(1)} %add_convert_fusion.3), channel_id=1, source_target_pairs={{0,8},{4,12},{8,0},{12,4},{16,24},{20,28},{24,16},{28,20},{1,9},{5... | collective-permute-start | bytes 1843208 | tf_op jit(solution)/shard_map/ppermute | solution.py:339
  (173 other events, 1913.5 us)

commit v2 on v1

--- a/solution.py
+++ b/solution.py
@@ -28,14 +28,21 @@
     return lax.dot_general(a, b, (((0,), (0,)), ((), ())), preferred_element_type=f32)
 
 
-def call(kernel, outs, *args, scalars=0, mem=48, flops=0, name=None):
+def full(v):
+    zeros = (0,) * len(v.shape)
+    return pl.BlockSpec(v.shape, lambda i: zeros, pipeline_mode=pl.Buffered(1))
+
+
+def call(kernel, outs, *args, scalars=0, mem=60, flops=0, scratch=(), name=None):
     moved = sum(a.size * a.dtype.itemsize for a in args)
     moved += sum(s.size * jnp.dtype(s.dtype).itemsize for s in outs)
     return pl.pallas_call(
         kernel,
+        grid=(1,),
         out_shape=outs,
-        in_specs=[smem] * scalars + [vmem] * (len(args) - scalars),
-        out_specs=[vmem] * len(outs),
+        in_specs=[smem] * scalars + [full(a) for a in args[scalars:]],
+        out_specs=[full(s) for s in outs],
+        scratch_shapes=scratch,
         compiler_params=pltpu.CompilerParams(vmem_limit_bytes=mem * MIB),
         cost_estimate=pl.CostEstimate(flops=flops, bytes_accessed=moved, transcendentals=0),
         name=name,
@@ -103,7 +110,7 @@
 
 def branches_kernel(nf_ref, w0_ref, w1_ref, taps_ref, bias_ref, mask_ref, x_ref, y_ref, conv_ref):
     half, chan = w0_ref.shape[0], x_ref.shape[1]
-    both = nn(nf_ref[:, :half], w0_ref[...]) + nn(nf_ref[:, half:], w1_ref[...])
+    both = nn(nf_ref[:, :half], w0_ref[:, : 2 * chan]) + nn(nf_ref[:, half:], w1_ref[:, : 2 * chan])
     x_ref[...] = both[:, :chan]
     y_ref[...] = both[:, chan:]
     for c in range(0, chan, 128):
@@ -175,7 +182,7 @@
     heads = nt(both, block_ref[0])
     direct_ref[...] = state * entry * mult + heads[:, :128]
     h1_ref[...] = heads[:, 128:256].astype(bf16)
-    h2_ref[...] = heads[:, 256:384].astype(bf16)
+    h2_ref[...] = heads[:, 256:384]
     h3_ref[...] = heads[:, 384:].astype(bf16)
     units = jnp.concatenate([c0[...], c1[...], c2[...], c3[...]], axis=1)
     grads = tn(units, both)
@@ -186,8 +193,8 @@
         wg_ref[1, k] = second[k * 128 + 64 : k * 128 + 128]
 
 
-def conv_back_kernel(direct_ref, r1, r2, r3, x_ref, taps_ref, mask_ref, gx_ref, sums_ref):
-    total = direct_ref[...] + r1[...].astype(f32) + r2[...].astype(f32) + r3[...].astype(f32)
+def conv_back_kernel(direct_ref, r1, r2, x_ref, taps_ref, mask_ref, gx_ref, sums_ref):
+    total = direct_ref[...] + r1[...].astype(f32) + r2[...].astype(f32)
     x = x_ref[...]
     grad = total * taps_ref[0:1]
     sums = [jnp.sum(total * x, axis=0, keepdims=True)]
@@ -208,10 +215,10 @@
         out[...] = total_ref[pl.ds(at, rows), :].astype(out.dtype)
 
 
-def product_split_kernel(z_ref, a_ref, w0_ref, w1_ref, o0, o1, o2, o3, total_ref):
-    half = w0_ref.shape[0]
-    total_ref[:, :half] = nt(a_ref[...], w0_ref[...])
-    total_ref[:, half:] = nt(a_ref[...], w1_ref[...])
+def product_split_kernel(at, z_ref, a_ref, w0_ref, w1_ref, o0, o1, o2, o3, total_ref):
+    half, cols = w0_ref.shape[0], slice(at, at + a_ref.shape[1])
+    total_ref[:, :half] = nt(a_ref[...], w0_ref[:, cols])
+    total_ref[:, half:] = nt(a_ref[...], w1_ref[:, cols])
     split_rows(z_ref, total_ref, (o0, o1, o2, o3))
 
 
@@ -233,8 +240,8 @@
     return ref[pl.ds(pl.multiple_of(z_ref[0] * rows, rows), rows), :].astype(f32)
 
 
-def norm_second_kernel(z_ref, x_ref, gain_ref, o0, o1, o2, o3, res_ref, low_ref):
-    residual = my_rows(z_ref, x_ref, res_ref.shape[0]) + sum_pieces((o0, o1, o2, o3))
+def norm_second_kernel(z_ref, x_ref, gain_ref, o0, o1, o2, res_ref, low_ref):
+    residual = my_rows(z_ref, x_ref, res_ref.shape[0]) + sum_pieces((o0, o1, o2))
     inv = lax.rsqrt(jnp.mean(residual * residual, axis=1, keepdims=True) + eps)
     res_ref[...] = residual
     low_ref[...] = (residual * inv * gain_ref[...]).astype(bf16)
@@ -248,23 +255,23 @@
     return out, jnp.sum(grad * unit, axis=0, keepdims=True)
 
 
-def second_back_kernel(z_ref, cot_ref, gain_ref, res_ref, o0, o1, o2, o3, gr_ref, low_ref, gain_out):
-    grad, gain_grad = norm_back(res_ref[...], gain_ref[...], sum_pieces((o0, o1, o2, o3)))
+def second_back_kernel(z_ref, cot_ref, gain_ref, res_ref, o0, o1, o2, gr_ref, low_ref, gain_out):
+    grad, gain_grad = norm_back(res_ref[...], gain_ref[...], sum_pieces((o0, o1, o2)))
     grad = grad + my_rows(z_ref, cot_ref, res_ref.shape[0])
     gr_ref[...] = grad
     low_ref[...] = grad.astype(bf16)
     gain_out[...] = gain_grad
 
 
-def first_back_kernel(z_ref, x_ref, gain_ref, gr_ref, o0, o1, o2, o3, out_ref, gain_out):
+def first_back_kernel(z_ref, x_ref, gain_ref, gr_ref, o0, o1, o2, out_ref, gain_out):
     x = my_rows(z_ref, x_ref, gr_ref.shape[0])
-    grad, gain_grad = norm_back(x, gain_ref[...], sum_pieces((o0, o1, o2, o3)))
+    grad, gain_grad = norm_back(x, gain_ref[...], sum_pieces((o0, o1, o2)))
     out_ref[...] = (gr_ref[...] + grad).astype(bf16)
     gain_out[...] = gain_grad
 
 
-def block_out_kernel(res_ref, o0, o1, o2, o3, out_ref):
-    out_ref[...] = (res_ref[...] + sum_pieces((o0, o1, o2, o3))).astype(bf16)
+def block_out_kernel(res_ref, o0, o1, o2, out_ref):
+    out_ref[...] = (res_ref[...] + sum_pieces((o0, o1, o2))).astype(bf16)
 
 
 def ffn_kernel(first, last, *refs):
@@ -339,84 +346,136 @@
     return lax.ppermute(v, axis, [(i, i ^ bit) for i in range(size)])
 
 
-def after(v, *others):
-    return lax.optimization_barrier((v,) + others)[0]
-
-
-def gather_rows(shard, size, before):
-    if before:
-        shard = after(shard, *before)
-    if size == 8:
-        half = shard.shape[0] // 2
-        by_x = exchange(shard, "dp", size, 2)
-        by_y = exchange(shard, "dp", size, 4)
-        top = exchange(by_x[:half], "dp", size, 4)
-        bottom = exchange(by_y[half:], "dp", size, 2)
-        mine = jnp.concatenate([shard, by_x, by_y, top, bottom], axis=0)
-        marks = (by_x, by_y)
-    else:
+def tie(*values):
+    return lax.optimization_barrier(values)
+
+
+def move(size, send_x, send_y):
+    if size != 8:
+        return send_x, send_y
+    return exchange(send_x, "dp", 8, 2), exchange(send_y, "dp", 8, 4)
+
+
+def stack_sends(parts, more):
+    return tuple(jnp.concatenate([a, b], axis=0) for a, b in zip(parts, more))
+
+
+def cut_sends(got, rows):
+    return tuple(v[:rows] for v in got), tuple(v[rows:] for v in got)
+
+
+class Gather:
+    def __init__(self, size):
+        self.size = size
+
+    def second(self, by_x, by_y):
+        half = by_x.shape[0] // 2
+        return by_y[half:], by_x[:half]
+
+    def join(self, shard, first, second):
+        if self.size == 8:
+            return jnp.concatenate([shard, *first, second[1], second[0]], axis=0)
         mine, bit = shard, 2
-        while bit < size:
-            mine = jnp.concatenate([mine, exchange(mine, "dp", size, bit)], axis=0)
+        while bit < self.size:
+            mine = jnp.concatenate([mine, exchange(mine, "dp", self.size, bit)], axis=0)
             bit *= 2
-        marks = (mine,)
-    return mine, exchange(mine, "dp", size, 1), marks
-
-
-def scatter_grads(lefts, rights, size):
-    sides, model = len(lefts), lefts[0].shape[1]
-    tokens = lefts[0].shape[0]
-    width = sum(r.shape[1] for r in rights)
-    flops = tokens * model * width
-    out = call(
-        partial(grads_out_kernel, sides), [like((model // 2, width), bf16)], *lefts, *rights,
-        flops=flops, name="grads_out",
-    )[0]
-    got = exchange(out, "dp", size, 1)
-    q = model // 16
-    own, x_top, y_bot, send_x, send_y = call(
-        partial(grads_own_kernel, sides),
-        [like((2 * q, width), f32), like((q, width), f32), like((q, width), f32),
-         like((2 * q, width), bf16), like((2 * q, width), bf16)],
-        *lefts, *rights, got, flops=flops, name="grads_own",
-    )
-    if size == 8:
-        from_x = exchange(send_x, "dp", size, 2)
-        from_y = exchange(send_y, "dp", size, 4)
-        last_x = exchange((x_top + from_y[:q].astype(f32)).astype(bf16), "dp", size, 2)
-        last_y = exchange((y_bot + from_x[:q].astype(f32)).astype(bf16), "dp", size, 4)
-        return jnp.concatenate(
-            [
-                own[:q] + from_y[q:].astype(f32) + last_x.astype(f32),
-                own[q:] + from_x[q:].astype(f32) + last_y.astype(f32),
-            ],
+        return mine
+
+    def other(self, mine):
+        return exchange(mine, "dp", self.size, 1)
+
+
+class Scatter:
+    def __init__(self, size, lefts, rights, name):
+        self.size, self.name = size, name
+        self.lefts, self.rights = lefts, rights
+        self.model = lefts[0].shape[1]
+        self.width = sum(r.shape[1] for r in rights)
+        self.flops = lefts[0].shape[0] * self.model * self.width
+
+    def sibling(self):
+        return call(
+            partial(grads_out_kernel, len(self.lefts)),
+            [like((self.model // 2, self.width), bf16)],
+            *self.lefts, *self.rights, flops=self.flops, name="grads_out_" + self.name,
+        )[0]
+
+    def swap(self, out):
+        return exchange(out, "dp", self.size, 1)
+
+    def own(self, got):
+        q, w = self.model // 16, self.width
+        return call(
+            partial(grads_own_kernel, len(self.lefts)),
+            [like((2 * q, w), f32), like((q, w), f32), like((q, w), f32),
+             like((2 * q, w), bf16), like((2 * q, w), bf16)],
+            *self.lefts, *self.rights, got, flops=self.flops, name="grads_own_" + self.name,
+        )
+
+    def second(self, cut, got):
+        _, x_top, y_bot, _, _ = cut
+        if self.size != 8:
+            return x_top.astype(bf16), y_bot.astype(bf16)
+        q = x_top.shape[0]
+        return (
+            (x_top + got[1][:q].astype(f32)).astype(bf16),
+            (y_bot + got[0][:q].astype(f32)).astype(bf16),
+        )
+
+    def join(self, cut, got, last):
+        own, x_top, y_bot, _, _ = cut
+        (from_x, from_y), (last_x, last_y) = got, last
+        q = x_top.shape[0]
+        if self.size == 8:
+            return jnp.concatenate(
+                [
+                    own[:q] + from_y[q:].astype(f32) + last_x.astype(f32),
+                    own[q:] + from_x[q:].astype(f32) + last_y.astype(f32),
+                ],
+                axis=0,
+            )
+        total = jnp.concatenate(
+            [own, x_top, from_x[q:].astype(f32), from_y[q:].astype(f32), y_bot,
+             from_y[:q].astype(f32), from_x[:q].astype(f32)],
             axis=0,
         )
-    total = jnp.concatenate(
-        [own, x_top, send_x[q:].astype(f32), send_y[q:].astype(f32), y_bot,
-         send_y[:q].astype(f32), send_x[:q].astype(f32)],
-        axis=0,
-    )
-    bit = size // 2
-    while bit > 1:
-        half = total.shape[0] // 2
-        total = total[:half] + exchange(total[half:].astype(bf16), "dp", size, bit).astype(f32)
-        bit //= 2
-    return total
-
-
-def send_rows(pieces):
-    return [pieces[0]] + [exchange(pieces[k], "tensor", 4, k) for k in range(1, 4)]
-
-
-def spread_rows(piece):
-    return [piece] + [exchange(piece, "tensor", 4, k) for k in range(1, 4)]
-
-
-def sum_over(v, axis, size):
-    bit = 1
-    while bit < size:
+        bit = self.size // 2
+        while bit > 1:
+            half = total.shape[0] // 2
+            total = total[:half] + exchange(total[half:].astype(bf16), "dp", self.size, bit).astype(f32)
+            bit //= 2
+        return total
+
+
+def to_owner(parts):
+    return exchange(parts[3], "tensor", 4, 1), exchange(parts[1], "tensor", 4, 1)
+
+
+def pass_on(part, got):
+    return exchange((part + got.astype(f32)).astype(bf16), "tensor", 4, 2)
+
+
+def spread(piece):
+    return exchange(piece, "tensor", 4, 2), exchange(piece, "tensor", 4, 1)
+
+
+def neighbour(v):
+    return exchange(v, "tensor", 4, 1)
+
+
+def sum_over(v, axis, size, first=1, until=None):
+    bit = first
+    while bit < (until or size):
         v = v + exchange(v, axis, size, bit)
+        bit *= 2
+    return v
+
+
+def sum_low(v, axis, size, first=1, until=None):
+    bit = first
+    while bit < (until or size):
+        low = v.astype(bf16)
+        v = low.astype(f32) + exchange(low, axis, size, bit).astype(f32)
         bit *= 2
     return v
 
@@ -454,26 +513,41 @@
             [lax.dynamic_slice_in_dim(v, p * part, part, axis=-1) for p in places], axis=-1
         )
 
-    xy_shard = jnp.concatenate([x_weight.reshape(part, chan), y_weight.reshape(part, chan)], axis=1)
-    out_shard = out_weight.reshape(chan, part).T
+    gat = Gather(dp_size)
+    lane = pl.BlockSpec((count, 128), lambda p: (0, p))
+    line = pl.BlockSpec((1, 128), lambda p: (0, p))
+    sums_spec = pl.BlockSpec((8, 128), lambda p: (0, p))
+    block_spec = pl.BlockSpec((1, 8 * units, 4 * units), lambda p: (p, 0, 0))
+    mask_spec = pl.BlockSpec((taps - 1, count, 128), lambda p: (0, 0, 0))
+
+    def product_split(a, w0, w1, at, name):
+        return call(
+            partial(product_split_kernel, at), [like((rows, model), t) for t in (f32, bf16, f32, bf16)],
+            z_arr, a, w0, w1, scalars=1, flops=2 * count * model * a.shape[1],
+            scratch=[pltpu.VMEM((count, model), f32)], name=name,
+        )
+
+    def assemble(pieces, dtype, name):
+        return call(assemble_kernel, [like((count, model), dtype)], z_arr, *pieces, scalars=1, name=name)[0]
+
+    hold = lax.optimization_barrier
+    x_flat, y_flat = x_weight.reshape(part, chan), y_weight.reshape(part, chan)
+    xyo = jnp.concatenate([x_flat, y_flat, out_weight.reshape(chan, part).T], axis=1)
+    xyo_first = move(dp_size, xyo, xyo)
     down_shard = down_weight.T
-    ffn_shards = [
-        jnp.concatenate(
-            [v[:, c * width : (c + 1) * width] for v in (gate_weight, up_weight, down_shard)], axis=1
-        )
-        for c in range(chunk_count)
-    ]
-    xy0, xy1, marks = gather_rows(xy_shard, dp_size, None)
-    out0, out1, marks = gather_rows(out_shard, dp_size, marks)
-    ffn_weights = []
-    for shard in ffn_shards:
-        w0, w1, marks = gather_rows(shard, dp_size, marks)
-        ffn_weights.append((w0, w1))
+
+    def ffn_shard(c):
+        cols = slice(c * width, (c + 1) * width)
+        return jnp.concatenate([v[:, cols] for v in (gate_weight, up_weight, down_shard)], axis=1)
 
     x_rel = to_rel(tokens)
-    cot_rel = to_rel(cotangent)
     gain_one = to_rel(first_gain).reshape(1, model)
     gain_two = to_rel(second_gain).reshape(1, model)
+    nf = call(norm_first_kernel, [like((count, model), bf16)], x_rel, gain_one, name="norm_first")[0]
+    f0 = ffn_shard(0)
+    xyo_first, x_rel, gain_one, gain_two, nf, f0 = hold((xyo_first, x_rel, gain_one, gain_two, nf, f0))
+
+    xyo_second = move(dp_size, *gat.second(*xyo_first))
     masks = jnp.stack(
         [
             jnp.concatenate([jnp.full((lag,), -1, jnp.int32), segments[:-lag]]) == segments
@@ -481,109 +555,120 @@
         ]
     ).astype(f32)
     masks = jnp.broadcast_to(masks[:, :, None], (taps - 1, count, 128))
-    wide_masks = masks
     taps_flat = conv_weight.reshape(taps, chan)
     bias_flat = conv_bias.reshape(1, chan)
     rate_flat, input_flat = rate_bias.reshape(1, chan), input_bias.reshape(1, chan)
     decay_flat = decay_logit.reshape(1, chan)
+    lines = (masks, taps_flat, bias_flat, rate_flat, input_flat, decay_flat)
+    xyo_second, lines = hold((xyo_second, lines))
+    masks, taps_flat, bias_flat, rate_flat, input_flat, decay_flat = lines
+
+    f0_first = move(dp_size, f0, f0)
+    xyo0 = gat.join(xyo, xyo_first, xyo_second)
+    xyo1 = gat.other(xyo0)
+    x_branch, y_branch, conv_low = call(
+        branches_kernel,
+        [like((count, chan), f32), like((count, chan), f32), like((count, chan), bf16)],
+        nf, xyo0, xyo1, taps_flat, bias_flat, masks, flops=4 * count * model * chan, name="branches",
+    )
+    conv2, conv1 = spread(conv_low)
     both = jnp.stack([rate_weight, input_weight], axis=2).reshape(pairs, 2, 4, units, 2, units)
     both = jnp.stack([lax.dynamic_index_in_dim(both, z ^ k, 2, False) for k in range(4)], axis=1)
     zero = jnp.zeros((pairs, 4, units, 2, units), bf16)
     blocks = jnp.stack(
         [jnp.stack([both[:, :, 0], zero], axis=4), jnp.stack([zero, both[:, :, 1]], axis=4)], axis=2
     ).reshape(pairs, 8 * units, 4 * units)
-
-    nf = call(norm_first_kernel, [like((count, model), bf16)], x_rel, gain_one, name="norm_first")[0]
-    x_branch, y_branch, conv_low = call(
-        branches_kernel,
-        [like((count, chan), f32), like((count, chan), f32), like((count, chan), bf16)],
-        nf, xy0, xy1, taps_flat, bias_flat, masks, flops=4 * count * model * chan, name="branches",
-    )
-    conv = spread_rows(conv_low)
-    lane = pl.BlockSpec((count, 128), lambda p: (0, p))
-    line = pl.BlockSpec((1, 128), lambda p: (0, p))
-    block_spec = pl.BlockSpec((1, 8 * units, 4 * units), lambda p: (p, 0, 0))
-    mask_spec = pl.BlockSpec((taps - 1, count, 128), lambda p: (0, 0, 0))
+    f1 = ffn_shard(1)
+    conv2, conv1, f0_first, blocks, f1 = hold((conv2, conv1, f0_first, blocks, f1))
+    conv3 = neighbour(conv2)
+    slot = move(dp_size, *stack_sends(gat.second(*f0_first), (f1, f1)))
+    cot_rel = to_rel(cotangent)
+    f2 = ffn_shard(2)
+    conv3, cot_rel, f2 = hold((conv3, cot_rel, f2))
+    conv = [conv_low, conv1, conv2, conv3]
     rate, entry, hidden, mixed = pl.pallas_call(
         forward_scan_kernel,
         grid=(pairs,),
         in_specs=[lane] * 4 + [block_spec] + [line] * 3 + [lane, mask_spec],
         out_specs=[lane] * 4,
         out_shape=[like((count, chan), f32)] * 3 + [like((count, chan), bf16)],
-        compiler_params=pltpu.CompilerParams(vmem_limit_bytes=24 * MIB),
+        compiler_params=pltpu.CompilerParams(vmem_limit_bytes=60 * MIB),
         cost_estimate=pl.CostEstimate(
             flops=pairs * count * 512 * 256 * 2, bytes_accessed=6 * MIB, transcendentals=0),
         name="forward_scan",
     )(*conv, blocks, rate_flat, input_flat, decay_flat, y_branch, masks)
-
-    def product_split(a, w0, w1, name):
-        return pl.pallas_call(
-            product_split_kernel,
-            out_shape=[like((rows, model), f32)] + [like((rows, model), bf16)] * 3,
-            in_specs=[smem] + [vmem] * 3,
-            out_specs=[vmem] * 4,
-            scratch_shapes=[pltpu.VMEM((count, model), f32)],
-            compiler_params=pltpu.CompilerParams(vmem_limit_bytes=32 * MIB),
-            cost_estimate=pl.CostEstimate(
-                flops=2 * count * model * a.shape[1], bytes_accessed=2 * w0.size * 2,
-                transcendentals=0),
-            name=name,
-        )(z_arr, a, w0, w1)
-
-    def assemble(pieces, dtype, name):
-        return call(assemble_kernel, [like((count, model), dtype)], z_arr, *pieces, scalars=1, name=name)[0]
-
-    pieces = send_rows(product_split(mixed, out0, out1, "recurrent"))
+    parts = product_split(mixed, xyo0, xyo1, 2 * chan, "recurrent")
+    got3, got1 = to_owner(parts)
+    got2 = pass_on(parts[2], got3)
+    got1, got2, slot = hold((got1, got2, slot))
+
+    f0_second, f1_first = cut_sends(slot, part // 2)
     residual, second_rows = call(
         norm_second_kernel, [like((rows, model), f32), like((rows, model), bf16)],
-        z_arr, x_rel, gain_two, *pieces, scalars=1, name="norm_second",
-    )
-    second = assemble(spread_rows(second_rows), bf16, "second_all")
-
-    ffn_grads = []
-    sums = None
-    for c, (w0, w1) in enumerate(ffn_weights):
+        z_arr, x_rel, gain_two, parts[0], got1, got2, scalars=1, name="norm_second",
+    )
+    sec2, sec1 = spread(second_rows)
+    slot = move(dp_size, *stack_sends(gat.second(*f1_first), (f2, f2)))
+    f0_w0 = gat.join(f0, f0_first, f0_second)
+    f0_w1 = gat.other(f0_w0)
+    sec2, f0_w1 = hold((sec2, f0_w1))
+    sec3 = neighbour(sec2)
+    second = assemble([second_rows, sec1, sec2, sec3], bf16, "second_all")
+
+    def ffn(c, w0, w1, sums):
         first, last = c == 0, c == chunk_count - 1
         outs = [like((count, 2 * width), bf16), like((count, width), bf16)]
         scratch = [pltpu.VMEM((count, 2 * width), f32), pltpu.VMEM((count, width), f32)]
         if last:
-            outs += ([like((rows, model), f32)] + [like((rows, model), bf16)] * 3) * 2
+            outs += [like((rows, model), t) for t in (f32, bf16, f32, bf16)] * 2
             scratch = [pltpu.VMEM((count, model), f32)] * 2 + scratch
         else:
             outs += [like((count, model), f32)] * 2
-        ins = [z_arr, second, cot_rel, w0, w1] + ([] if first else sums)
-        res = pl.pallas_call(
-            partial(ffn_kernel, first, last),
-            out_shape=outs,
-            in_specs=[smem] + [vmem] * (len(ins) - 1),
-            out_specs=[vmem] * len(outs),
-            scratch_shapes=scratch,
-            compiler_params=pltpu.CompilerParams(vmem_limit_bytes=56 * MIB),
-            cost_estimate=pl.CostEstimate(
-                flops=12 * count * model * width, bytes_accessed=25 * MIB, transcendentals=0),
-            name="ffn_%d" % c,
-        )(*ins)
-        ffn_grads.append((res[0], res[1]))
-        sums = list(res[2:])
-    out_pieces, grad_pieces = sums[:4], sums[4:]
-
-    grad_pieces = send_rows(grad_pieces)
+        res = call(
+            partial(ffn_kernel, first, last), outs, z_arr, second, cot_rel, w0, w1, *sums,
+            scalars=1, flops=12 * count * model * width, scratch=scratch, name="ffn_%d" % c,
+        )
+        return Scatter(dp_size, [second, cot_rel], res[:2], "ffn_%d" % c), res[2:]
+
+    s0, sums = ffn(0, f0_w0, f0_w1, [])
+    s0_out = s0.sibling()
+    sums, slot, s0_out = hold((sums, slot, s0_out))
+    f1_second, f2_first = cut_sends(slot, part // 2)
+    f2_second = move(dp_size, *gat.second(*f2_first))
+    f1_w0 = gat.join(f1, f1_first, f1_second)
+    f1_w1 = gat.other(f1_w0)
+    s0_cut = s0.own(s0.swap(s0_out))
+    f1_w1, s0_cut = hold((f1_w1, s0_cut))
+    s1, sums = ffn(1, f1_w0, f1_w1, sums)
+    sums, f2_second = hold((sums, f2_second))
+    f2_w0 = gat.join(f2, f2_first, f2_second)
+    f2_w1 = gat.other(f2_w0)
+    s0_got = move(dp_size, *s0_cut[3:])
+    s1_out = s1.sibling()
+    f2_w1, s1_out = hold((f2_w1, s1_out))
+    s2, sums = ffn(2, f2_w0, f2_w1, sums)
+    out_parts, grad_parts = sums[:4], sums[4:]
+
+    got3, got1 = to_owner(grad_parts)
+    s1_cut = s1.own(s1.swap(s1_out))
+    got3, s1_cut = hold((got3, s1_cut))
+    got2 = pass_on(grad_parts[2], got3)
+    s2_out = s2.sibling()
+    got1, got2, s0_got, s2_out = hold((got1, got2, s0_got, s2_out))
+    slot = move(dp_size, *stack_sends(s0.second(s0_cut, s0_got), s1_cut[3:]))
     grad_res, rec_rows, second_gain_part = call(
         second_back_kernel,
         [like((rows, model), f32), like((rows, model), bf16), like((1, model), f32)],
-        z_arr, cot_rel, gain_two, residual, *grad_pieces, scalars=1, name="second_back",
-    )
-    grad_rec = assemble(spread_rows(rec_rows), bf16, "grad_rec_all")
-
-    ffn_shares = [
-        scatter_grads([second, cot_rel], [ggu, mid], dp_size) for ggu, mid in ffn_grads
-    ]
-
-    out_pieces = send_rows(out_pieces)
-    block_rows = call(block_out_kernel, [like((rows, model), bf16)], residual, *out_pieces, name="block_out")[0]
-    block_out = assemble(spread_rows(to_abs(block_rows)), bf16, "block_out_all")
-
-    half_spec = pl.BlockSpec((model // 2, 128), lambda p: (0, p))
+        z_arr, cot_rel, gain_two, residual, grad_parts[0], got1, got2, scalars=1, name="second_back",
+    )
+    rec2, rec1 = spread(rec_rows)
+    s2_cut = s2.own(s2.swap(s2_out))
+    rec2, s2_cut = hold((rec2, s2_cut))
+    rec3 = neighbour(rec2)
+    out_got = neighbour(jnp.concatenate([out_parts[3], out_parts[1]], axis=0))
+    grad_rec = assemble([rec_rows, rec1, rec2, rec3], bf16, "grad_rec_all")
+
+    half_spec = pl.BlockSpec((model // 2, 128), lambda p: (0, 2 * pairs + p))
     whole = pl.BlockSpec((count, model), lambda p: (0, 0))
     gate_spec = pl.BlockSpec((2, 4, units, 2 * units), lambda p: (p, 0, 0, 0))
     grad_y, direct, h1, h2, h3, gate_grads, scan_sums = pl.pallas_call(
@@ -591,62 +676,100 @@
         grid=(pairs,),
         in_specs=[whole, half_spec, half_spec] + [lane] * 4 + [block_spec, line, lane, mask_spec]
         + [lane] * 3,
-        out_specs=[lane, lane, lane, lane, lane, gate_spec, pl.BlockSpec((8, 128), lambda p: (0, p))],
-        out_shape=[like((count, chan), bf16), like((count, chan), f32)]
-        + [like((count, chan), bf16)] * 3
+        out_specs=[lane, lane, lane, lane, lane, gate_spec, sums_spec],
+        out_shape=[like((count, chan), t) for t in (bf16, f32, bf16, f32, bf16)]
         + [like((heads, 4, units, 2 * units), f32), like((8, chan), f32)],
-        compiler_params=pltpu.CompilerParams(vmem_limit_bytes=32 * MIB),
+        compiler_params=pltpu.CompilerParams(vmem_limit_bytes=60 * MIB),
         cost_estimate=pl.CostEstimate(
             flops=2 * count * model * chan + pairs * count * 512 * 256 * 4, bytes_accessed=12 * MIB,
             transcendentals=0),
         name="backward_scan",
-    )(grad_rec, out0, out1, *conv, blocks, decay_flat, y_branch, masks, rate, entry, hidden)
-    out_share = scatter_grads([grad_rec], [mixed], dp_size)
-    got = send_rows([direct, h1, h2, h3])
+    )(grad_rec, xyo0, xyo1, *conv, blocks, decay_flat, y_branch, masks, rate, entry, hidden)
+    got3, got1 = to_owner([None, h1, None, h3])
+    out_got, slot, got3 = hold((out_got, slot, got3))
+    got2 = pass_on(h2, got3)
+    s0_last, s1_got = cut_sends(slot, model // 16)
+    slot = move(dp_size, *stack_sends(s1.second(s1_cut, s1_got), s2_cut[3:]))
+    out_got2 = pass_on(out_parts[2], out_got[:rows])
+    gate_sum = sum_low(gate_grads, "dp", dp_size, 1, 2)
+    got1, got2, out_got2, gate_sum = hold((got1, got2, out_got2, gate_sum))
     grad_x, conv_sums = pl.pallas_call(
         conv_back_kernel,
         grid=(pairs,),
-        in_specs=[lane] * 5 + [pl.BlockSpec((taps, 128), lambda p: (0, p)), mask_spec],
-        out_specs=[lane, pl.BlockSpec((8, 128), lambda p: (0, p))],
+        in_specs=[lane] * 4 + [pl.BlockSpec((taps, 128), lambda p: (0, p)), mask_spec],
+        out_specs=[lane, sums_spec],
         out_shape=[like((count, chan), bf16), like((8, chan), f32)],
-        compiler_params=pltpu.CompilerParams(vmem_limit_bytes=24 * MIB),
+        compiler_params=pltpu.CompilerParams(vmem_limit_bytes=60 * MIB),
         cost_estimate=pl.CostEstimate(flops=0, bytes_accessed=4 * MIB, transcendentals=0),
         name="conv_back",
-    )(*got, x_branch, taps_flat, masks)
-
+    )(direct, got1, got2, x_branch, taps_flat, masks)
     grad_xy = jnp.concatenate([grad_x, grad_y], axis=1)
-    first_pieces = send_rows(product_split(grad_xy, xy0, xy1, "grad_first"))
+    first_parts = product_split(grad_xy, xyo0, xyo1, 0, "grad_first")
+    got3, got1 = to_owner(first_parts)
+    sxyo = Scatter(dp_size, [nf, grad_rec], [grad_xy, mixed], "xyo")
+    sxyo_out = sxyo.sibling()
+    block_rows = call(
+        block_out_kernel, [like((rows, model), bf16)], residual, out_parts[0], out_got[rows:], out_got2,
+        name="block_out",
+    )[0]
+    block_rows = to_abs(block_rows)
+    gate_sum = sum_low(gate_sum, "dp", dp_size, 2, 4)
+    got3, slot, sxyo_out, block_rows, gate_sum = hold((got3, slot, sxyo_out, block_rows, gate_sum))
+    got2 = pass_on(first_parts[2], got3)
+    s1_last, s2_got = cut_sends(slot, model // 16)
+    s2_last = move(dp_size, *s2.second(s2_cut, s2_got))
+    sxyo_cut = sxyo.own(sxyo.swap(sxyo_out))
+    block2 = exchange(block_rows, "tensor", 4, 2)
+    small = jnp.concatenate([scan_sums, conv_sums], axis=0)
+    small = sum_over(small, "dp", dp_size, 1, 2)
+    got1, got2, s2_last, sxyo_cut, block2, small, gate_sum = hold(
+        (got1, got2, s2_last, sxyo_cut, block2, small, gate_sum)
+    )
+    sxyo_got = move(dp_size, *sxyo_cut[3:])
     tokens_rows, first_gain_part = call(
         first_back_kernel, [like((rows, model), bf16), like((1, model), f32)],
-        z_arr, x_rel, gain_one, grad_res, *first_pieces, scalars=1, name="first_back",
-    )
-    tokens_grad = assemble(spread_rows(to_abs(tokens_rows)), f32, "tokens_grad_all")
-    xy_share = scatter_grads([nf], [grad_xy], dp_size)
-
-    small = jnp.concatenate([scan_sums, conv_sums], axis=0)
-    small = sum_over(small, "dp", dp_size)
-    gains = to_abs(jnp.concatenate([first_gain_part, second_gain_part], axis=0))
-    gains = sum_over(sum_over(gains, "tensor", 4), "dp", dp_size)
-    gate_low = gate_grads.astype(bf16)
-    bit = 1
-    while bit < dp_size:
-        gate_low = gate_low.astype(bf16)
-        gate_low = gate_low.astype(f32) + exchange(gate_low, "dp", dp_size, bit).astype(f32)
-        bit *= 2
-    gate_sum = jnp.concatenate(
-        [lax.dynamic_index_in_dim(gate_low, z ^ k, 1, False) for k in range(4)], axis=1
-    )
-
-    ffn_cat = [
+        z_arr, x_rel, gain_one, grad_res, first_parts[0], got1, got2, scalars=1, name="first_back",
+    )
+    tokens_rows = to_abs(tokens_rows)
+    tok2, tok1 = spread(tokens_rows)
+    block_more = neighbour(jnp.concatenate([block_rows, block2], axis=0))
+    ffn_shares = [
+        s0.join(s0_cut, s0_got, s0_last),
+        s1.join(s1_cut, s1_got, s1_last),
+        s2.join(s2_cut, s2_got, s2_last),
+    ]
+    gate_share, up_share, down_share = [
         jnp.concatenate([s[:, k * width : (k + 1) * width] for s in ffn_shares], axis=1)
         for k in range(3)
     ]
+    down_share = down_share.T
+    gate_sum = sum_low(gate_sum, "dp", dp_size, 4)
+    gate_sum = jnp.concatenate(
+        [lax.dynamic_index_in_dim(gate_sum, z ^ k, 1, False) for k in range(4)], axis=1
+    )
+    small = sum_over(small, "dp", dp_size, 2, 4)
+    gains = to_abs(jnp.concatenate([first_gain_part, second_gain_part], axis=0))
+    gains = sum_over(gains, "tensor", 4)
+    tok2, gate_share, up_share, down_share, gate_sum, small, gains, block_more = hold(
+        (tok2, gate_share, up_share, down_share, gate_sum, small, gains, block_more)
+    )
+    tok3 = neighbour(tok2)
+    gains = sum_over(gains, "dp", dp_size, 1, 4)
+    small = sum_over(small, "dp", dp_size, 4)
+    block_out = assemble(
+        [block_rows, block_more[:rows], block2, block_more[rows:]], bf16, "block_out_all"
+    )
+    tok3, sxyo_got, gains, block_out = hold((tok3, sxyo_got, gains, block_out))
+    sxyo_last = move(dp_size, *sxyo.second(sxyo_cut, sxyo_got))
+    tokens_grad = assemble([tokens_rows, tok1, tok2, tok3], f32, "tokens_grad_all")
+    gains = sum_over(gains, "dp", dp_size, 4)
+    xyo_share = sxyo.join(sxyo_cut, sxyo_got, sxyo_last)
     return (
         block_out,
         tokens_grad,
         gains[0],
-        xy_share[:, :chan].reshape(part, heads, units),
-        xy_share[:, chan:].reshape(part, heads, units),
+        xyo_share[:, :chan].reshape(part, heads, units),
+        xyo_share[:, chan : 2 * chan].reshape(part, heads, units),
         small[8 : 8 + taps].reshape(taps, heads, units),
         small[8 + taps].reshape(heads, units),
         gate_sum[:, :, :units],
@@ -654,11 +777,11 @@
         small[1].reshape(heads, units),
         small[2].reshape(heads, units),
         small[0].reshape(heads, units),
-        out_share.T.reshape(heads, units, part),
+        xyo_share[:, 2 * chan :].T.reshape(heads, units, part),
         gains[1],
-        ffn_cat[0],
-        ffn_cat[1],
-        ffn_cat[2].T,
+        gate_share,
+        up_share,
+        down_share,
     )
 
 

time: 858 us -> 557 us (0.65)
  waiting for transfers between devices: 424 us -> 172 us
  starting transfers between devices: 147 us -> 68.3 us
  Pallas kernels: 122 us -> 162 us
  local copies, waits for them, and re-layouts: 118 us -> 96.4 us
  other arithmetic: 35.4 us -> 51.7 us
    ppermute x91 -> x71, waiting for transfers between devices: 424 us -> 172 us  [exchange(): return lax.ppermute(v, axis, [(i, i ^ bit) for i in range(size)])]
    ppermute x91 -> x71, starting transfers between devices: 147 us -> 68.3 us  [exchange(): return lax.ppermute(v, axis, [(i, i ^ bit) for i in range(size)])]
    pallas_call x26 -> x24, Pallas kernels: 108 us -> 145 us  [the longest x23 140 us: call(): pl.pallas_call(kernel, grid=(1,), out_shape=outs, in_specs=[smem] * scala...]
    unnamed x317 -> x139, local copies, waits for them, and re-layouts: 65.4 us -> 32.5 us
    slice x14, local copies, waits for them, and re-layouts: 4.39 us -> 19.7 us  [the longest x8 11.2 us: second(): return (by_y[half:], by_x[:half])]
    concatenate x9 -> x15, other arithmetic: 4.23 us -> 13.4 us  [the longest x6 5.95 us: stack_sends(): return tuple((jnp.concatenate([a, b], axis=0) for a, b in zip(parts, more)))]
  transfers between devices with their start and end apart: 91 -> 71, of which waited for: 47 -> 28; matrix products, arithmetic and copies ran while one was open for 12% -> 20% of each run, Pallas kernels for 14% -> 29%
where the time goes in v2:
time: 557 us; the launch traced here: 552 us
  waiting for transfers between devices  172 us (31%)
  Pallas kernels  162 us (29%)
  local copies, waits for them, and re-layouts  96.4 us (17%)
  starting transfers between devices  68.3 us (12%)
  other arithmetic  51.7 us (9%)
    ppermute x71, waiting for transfers between devices, exchange(): return lax.ppermute(v, axis, [(i, i ^ bit) for i in range(size)])  172 us
    pallas_call x23, Pallas kernels, call(): pl.pallas_call(kernel, grid=(1,), out_shape=outs, in_specs=[smem] * scala...  140 us
    ppermute x71, starting transfers between devices, exchange(): return lax.ppermute(v, axis, [(i, i ^ bit) for i in range(size)])  68.3 us
    unnamed x139, local copies, waits for them, and re-layouts  32.5 us
    slice x8, local copies, waits for them, and re-layouts, second(): return (by_y[half:], by_x[:half])  11.2 us
  transfers between devices with their start and end apart: 71, of which 28 were waited for; matrix products, arithmetic and copies ran while one was open for 20% of the time, Pallas kernels for 29%

profile of v2, /device:TPU:0, one launch (start us, length us, event | category | flops | bytes accessed | tf_op | source)
XLA Modules:
  0.0 552.0 jit_solution(17990950693499131615)
XLA Ops:
  5.2 3.0 collective-permute-start.1
  14.6 5.3 constant_dynamic-slice_fusion.16
  19.9 4.1 concatenate.123.x_ref
  24.0 3.1 norm_first.1.nf_ref.refs_0_
  31.6 3.8 collective-permute-done.1
  41.4 10.1 %collective-permute-done.2 = bf16[160,1920]{1,0:T(8,128)(2,1)S(1)} collective-permute-done((bf16[160,1920]{1,0:T(8,128)(2,1)S(1)}, bf16[160,1920]{1,0:T(8,128)(2,1)S(1)}, u32[]{:S(2)}, u32[]{:S(2)}) %collective-permute-start.2) | collective-permute-done | bytes 614432 | tf_op jit(solution)/shard_map/ppermute | solution.py:346
  59.7 4.2 collective-permute-done.4.w1_ref
  63.9 7.3 %branches.1 = (f32[256,640]{1,0:T(8,128)}, f32[256,640]{1,0:T(8,128)}, bf16[256,640]{1,0:T(8,128)(2,1)}) custom-call(bf16[256,2560]{1,0:T(8,128)(2,1)} %norm_first.1.nf_ref.refs_0_, bf16[1280,1920]{1,0:T(8,128)(2,1)} %constant_dynamic-update-slice_fusion.w0_ref, bf16[1280,1920]{1,0:T(8,128)(2,1)} %collective-permute-done.4.w1_ref, ...), custom_call_target="tpu_custom_call" | custom-call | flops 1677721600 | bytes 13185536 | tf_op jit(solution)/shard_map/branches/pallas_call | solution.py:39
  72.8 2.6 collective-permute-start.5
  76.0 2.7 copy.54
  78.7 2.5 reshape.127.block_ref
  81.2 3.8 concatenate.132.refs_2_.refs_1_.cot_ref
  96.6 4.0 collective-permute-done.9.c3
  101.4 7.1 %forward_scan.1 = (f32[256,640]{1,0:T(8,128)}, f32[256,640]{1,0:T(8,128)}, f32[256,640]{1,0:T(8,128)}, bf16[256,640]{1,0:T(8,128)(2,1)}) custom-call(bf16[256,640]{1,0:T(8,128)(2,1)} %get-tuple-element.199.c0, bf16[256,640]{1,0:T(8,128)(2,1)} %collective-permute-done.6.c1, bf16[256,640]{1,0:T(8,128)(2,1)} %collective-permute-done.5.c2, ...), custom_call_target="tpu_custom_call" | custom-call | flops 335544320 | bytes 6291456 | tf_op jit(solution)/shard_map/forward_scan/pallas_call | solution.py:589
  108.4 6.5 %recurrent.1 = (f32[64,2560]{1,0:T(8,128)}, bf16[64,2560]{1,0:T(8,128)(2,1)}, f32[64,2560]{1,0:T(8,128)}, bf16[64,2560]{1,0:T(8,128)(2,1)}) custom-call(s32[1]{0:T(128)} %bitcast.z_ref.refs_0_, bf16[256,640]{1,0:T(8,128)(2,1)} %get-tuple-element.211.a_ref.refs_3_, bf16[1280,1920]{1,0:T(8,128)(2,1)} %constant_dynamic-update-slice_fusion.w0_ref, ...), custom_call_target="tpu_custom_call" | custom-call | flops 838860800 | bytes 12124164 | tf_op jit(solution)/shard_map/recurrent/pallas_call | solution.py:39
  116.7 2.5 constant_dynamic-update-slice_fusion.7
  119.5 9.8 %collective-permute-done.11 = bf16[64,2560]{1,0:T(8,128)(2,1)S(1)} collective-permute-done((bf16[64,2560]{1,0:T(8,128)(2,1)}, bf16[64,2560]{1,0:T(8,128)(2,1)S(1)}, u32[]{:S(2)}, u32[]{:S(2)}) %collective-permute-start.11) | collective-permute-done | bytes 327712 | tf_op jit(solution)/shard_map/ppermute | solution.py:346
  131.2 2.4 constant_dynamic-update-slice_fusion.6
  133.6 2.4 constant_dynamic-update-slice_fusion.5
  136.0 6.1 %collective-permute-done.12.o2 = bf16[64,2560]{1,0:T(8,128)(2,1)S(1)} collective-permute-done((bf16[64,2560]{1,0:T(8,128)(2,1)S(1)}, bf16[64,2560]{1,0:T(8,128)(2,1)S(1)}, u32[]{:S(2)}, u32[]{:S(2)}) %collective-permute-start.12) | collective-permute-done | bytes 327712 | tf_op jit(solution)/shard_map/ppermute | solution.py:346
  151.0 2.8 norm_second.1
  153.8 2.6 collective-permute-start.15
  156.4 2.4 slice_dynamic-update-slice_fusion.1
  158.8 12.2 %collective-permute-done.16.p2 = bf16[64,2560]{1,0:T(8,128)(2,1)S(1)} collective-permute-done((bf16[64,2560]{1,0:T(8,128)(2,1)}, bf16[64,2560]{1,0:T(8,128)(2,1)S(1)}, u32[]{:S(2)}, u32[]{:S(2)}) %collective-permute-start.16) | collective-permute-done | bytes 327712 | tf_op jit(solution)/shard_map/ppermute | solution.py:346
  171.0 2.6 slice_dynamic-update-slice_fusion
  173.6 7.0 %collective-permute-done.18.p3 = bf16[64,2560]{1,0:T(8,128)(2,1)S(1)} collective-permute-done((bf16[64,2560]{1,0:T(8,128)(2,1)S(1)}, bf16[64,2560]{1,0:T(8,128)(2,1)S(1)}, u32[]{:S(2)}, u32[]{:S(2)}) %collective-permute-start.18) | collective-permute-done | bytes 327712 | tf_op jit(solution)/shard_map/ppermute | solution.py:346
  181.3 2.5 second_all.1.refs_1_.refs_0_
  183.8 11.9 %ffn_0.1 = (bf16[256,1280]{1,0:T(8,128)(2,1)}, bf16[256,640]{1,0:T(8,128)(2,1)}, f32[256,2560]{1,0:T(8,128)}, f32[256,2560]{1,0:T(8,128)}) custom-call(s32[1]{0:T(128)} %bitcast.z_ref.refs_0_, bf16[256,2560]{1,0:T(8,128)(2,1)} %second_all.1.refs_1_.refs_0_, bf16[256,2560]{1,0:T(8,128)(2,1)} %concatenate.132.refs_2_.refs_1_.cot_ref, ...), custom_call_target="tpu_custom_call" | custom-call | flops 5033164800 | bytes 18677764 | tf_op jit(solution)/shard_map/ffn_0/pallas_call | solution.py:39
  195.7 5.7 %grads_out_ffn_0.1 = bf16[1280,1920]{1,0:T(8,128)(2,1)} custom-call(bf16[256,2560]{1,0:T(8,128)(2,1)} %second_all.1.refs_1_.refs_0_, bf16[256,2560]{1,0:T(8,128)(2,1)} %concatenate.132.refs_2_.refs_1_.cot_ref, bf16[256,1280]{1,0:T(8,128)(2,1)} %get-tuple-element.230.refs_2_, bf16[256,640]{1,0:T(8,128)(2,1)} %get-tuple-element.231.refs_3_), custom_call_target="tpu_custom_call" | custom-call | flops 1258291200 | bytes 8519680 | tf_op jit(solution)/shard_map/grads_out_ffn_0/pallas_call | solution.py:39
  212.8 2.5 slice_dynamic-update-slice_fusion.2
  215.3 7.8 %grads_own_ffn_0.1 = (f32[320,1920]{1,0:T(8,128)}, f32[160,1920]{1,0:T(8,128)}, f32[160,1920]{1,0:T(8,128)}, bf16[320,1920]{1,0:T(8,128)(2,1)}, bf16[320,1920]{1,0:T(8,128)(2,1)}) custom-call(bf16[256,2560]{1,0:T(8,128)(2,1)} %second_all.1.refs_1_.refs_0_, bf16[256,2560]{1,0:T(8,128)(2,1)} %concatenate.132.refs_2_.refs_1_.cot_ref, ...), custom_call_target="tpu_custom_call" | custom-call | flops 1258291200 | bytes 15892480 | tf_op jit(solution)/shard_map/grads_own_ffn_0/pallas_call | solution.py:39
  223.1 13.4 %ffn_1.1 = (bf16[256,1280]{1,0:T(8,128)(2,1)}, bf16[256,640]{1,0:T(8,128)(2,1)}, f32[256,2560]{1,0:T(8,128)}, f32[256,2560]{1,0:T(8,128)}) custom-call(s32[1]{0:T(128)} %bitcast.z_ref.refs_0_, bf16[256,2560]{1,0:T(8,128)(2,1)} %second_all.1.refs_1_.refs_0_, bf16[256,2560]{1,0:T(8,128)(2,1)} %concatenate.132.refs_2_.refs_1_.cot_ref, ...), custom_call_target="tpu_custom_call" | custom-call | flops 5033164800 | bytes 23920644 | tf_op jit(solution)/shard_map/ffn_1/pallas_call | solution.py:39
  238.3 5.7 %grads_out_ffn_1.1 = bf16[1280,1920]{1,0:T(8,128)(2,1)} custom-call(bf16[256,2560]{1,0:T(8,128)(2,1)} %second_all.1.refs_1_.refs_0_, bf16[256,2560]{1,0:T(8,128)(2,1)} %concatenate.132.refs_2_.refs_1_.cot_ref, bf16[256,1280]{1,0:T(8,128)(2,1)} %get-tuple-element.247.refs_2_, bf16[256,640]{1,0:T(8,128)(2,1)} %get-tuple-element.248.refs_3_), custom_call_target="tpu_custom_call" | custom-call | flops 1258291200 | bytes 8519680 | tf_op jit(solution)/shard_map/grads_out_ffn_1/pallas_call | solution.py:39
  244.0 2.8 collective-permute-done.25.refs_4_
  246.9 13.5 %ffn_2.1 = (bf16[256,1280]{1,0:T(8,128)(2,1)}, bf16[256,640]{1,0:T(8,128)(2,1)}, f32[64,2560]{1,0:T(8,128)}, bf16[64,2560]{1,0:T(8,128)(2,1)}, f32[64,2560]{1,0:...) custom-call(s32[1]{0:T(128)} %bitcast.z_ref.refs_0_, ...), custom_call_target="tpu_custom_call" | custom-call | flops 5033164800 | bytes 22609924 | tf_op jit(solution)/shard_map/ffn_2/pallas_call | solution.py:39
  263.8 7.8 %grads_own_ffn_1.1 = (f32[320,1920]{1,0:T(8,128)}, f32[160,1920]{1,0:T(8,128)}, f32[160,1920]{1,0:T(8,128)}, bf16[320,1920]{1,0:T(8,128)(2,1)}, bf16[320,1920]{1,0:T(8,128)(2,1)}) custom-call(bf16[256,2560]{1,0:T(8,128)(2,1)} %second_all.1.refs_1_.refs_0_, bf16[256,2560]{1,0:T(8,128)(2,1)} %concatenate.132.refs_2_.refs_1_.cot_ref, ...), custom_call_target="tpu_custom_call" | custom-call | flops 1258291200 | bytes 15892480 | tf_op jit(solution)/shard_map/grads_own_ffn_1/pallas_call | solution.py:39
  273.0 5.8 %grads_out_ffn_2.1 = bf16[1280,1920]{1,0:T(8,128)(2,1)} custom-call(bf16[256,2560]{1,0:T(8,128)(2,1)} %second_all.1.refs_1_.refs_0_, bf16[256,2560]{1,0:T(8,128)(2,1)} %concatenate.132.refs_2_.refs_1_.cot_ref, bf16[256,1280]{1,0:T(8,128)(2,1)} %get-tuple-element.265.refs_2_, bf16[256,640]{1,0:T(8,128)(2,1)} %get-tuple-element.266.refs_3_), custom_call_target="tpu_custom_call" | custom-call | flops 1258291200 | bytes 8519680 | tf_op jit(solution)/shard_map/grads_out_ffn_2/pallas_call | solution.py:39
  278.9 11.2 %collective-permute-done.30 = bf16[320,1920]{1,0:T(8,128)(2,1)S(1)} collective-permute-done((bf16[320,1920]{1,0:T(8,128)(2,1)}, bf16[320,1920]{1,0:T(8,128)(2,1)S(1)}, u32[]{:S(2)}, u32[]{:S(2)}) %collective-permute-start.30) | collective-permute-done | bytes 1228832 | tf_op jit(solution)/shard_map/ppermute | solution.py:346
  294.5 3.3 second_back.1
  300.2 7.9 %grads_own_ffn_2.1 = (f32[320,1920]{1,0:T(8,128)}, f32[160,1920]{1,0:T(8,128)}, f32[160,1920]{1,0:T(8,128)}, bf16[320,1920]{1,0:T(8,128)(2,1)}, bf16[320,1920]{1,0:T(8,128)(2,1)}) custom-call(bf16[256,2560]{1,0:T(8,128)(2,1)} %second_all.1.refs_1_.refs_0_, bf16[256,2560]{1,0:T(8,128)(2,1)} %concatenate.132.refs_2_.refs_1_.cot_ref, ...), custom_call_target="tpu_custom_call" | custom-call | flops 1258291200 | bytes 15892480 | tf_op jit(solution)/shard_map/grads_own_ffn_2/pallas_call | solution.py:39
  308.0 7.5 %collective-permute-done.33.p2 = bf16[64,2560]{1,0:T(8,128)(2,1)} collective-permute-done((bf16[64,2560]{1,0:T(8,128)(2,1)}, bf16[64,2560]{1,0:T(8,128)(2,1)}, u32[]{:S(2)}, u32[]{:S(2)}) %collective-permute-start.33) | collective-permute-done | bytes 327712 | tf_op jit(solution)/shard_map/ppermute | solution.py:346
  319.4 7.1 %collective-permute-done.35.p3 = bf16[64,2560]{1,0:T(8,128)(2,1)} collective-permute-done((bf16[64,2560]{1,0:T(8,128)(2,1)}, bf16[64,2560]{1,0:T(8,128)(2,1)}, u32[]{:S(2)}, u32[]{:S(2)}) %collective-permute-start.35) | collective-permute-done | bytes 327712 | tf_op jit(solution)/shard_map/ppermute | solution.py:346
  328.9 10.3 %backward_scan.1 = (bf16[256,640]{1,0:T(8,128)(2,1)}, f32[256,640]{1,0:T(8,128)}, bf16[256,640]{1,0:T(8,128)(2,1)}, f32[256,640]{1,0:T(8,128)}, bf16[256,640]{1,...) custom-call(bf16[256,2560]{1,0:T(8,128)(2,1)} %grad_rec_all.1.g_ref.refs_1_, ...), custom_call_target="tpu_custom_call" | custom-call | flops 1509949440 | bytes 12582912 | tf_op jit(solution)/shard_map/backward_scan/pallas_call | solution.py:674
  342.9 8.8 %collective-permute-done.40 = bf16[256,640]{1,0:T(8,128)(2,1)S(1)} collective-permute-done((bf16[256,640]{1,0:T(8,128)(2,1)}, bf16[256,640]{1,0:T(8,128)(2,1)S(1)}, u32[]{:S(2)}, u32[]{:S(2)}) %collective-permute-start.40) | collective-permute-done | bytes 327712 | tf_op jit(solution)/shard_map/ppermute | solution.py:346
  358.2 2.8 collective-permute-start.42
  361.3 10.7 %collective-permute-done.41.r2 = bf16[256,640]{1,0:T(8,128)(2,1)S(1)} collective-permute-done((bf16[256,640]{1,0:T(8,128)(2,1)S(1)}, bf16[256,640]{1,0:T(8,128)(2,1)S(1)}, u32[]{:S(2)}, u32[]{:S(2)}) %collective-permute-start.41) | collective-permute-done | bytes 327712 | tf_op jit(solution)/shard_map/ppermute | solution.py:346
  371.9 3.6 collective-permute-done.42.o2
  378.2 5.0 conv_back.1
  386.0 7.3 %grad_first.1 = (f32[64,2560]{1,0:T(8,128)}, bf16[64,2560]{1,0:T(8,128)(2,1)}, f32[64,2560]{1,0:T(8,128)}, bf16[64,2560]{1,0:T(8,128)(2,1)}) custom-call(s32[1]{0:T(128)} %bitcast.z_ref.refs_0_, bf16[256,1280]{1,0:T(8,128)(2,1)} %copy-done, bf16[1280,1920]{1,0:T(8,128)(2,1)} %constant_dynamic-update-slice_fusion.w0_ref, ...), custom_call_target="tpu_custom_call" | custom-call | flops 1677721600 | bytes 12451844 | tf_op jit(solution)/shard_map/grad_first/pallas_call | solution.py:39
  397.6 5.7 %grads_out_xyo.1 = bf16[1280,1920]{1,0:T(8,128)(2,1)} custom-call(bf16[256,2560]{1,0:T(8,128)(2,1)} %norm_first.1.nf_ref.refs_0_, bf16[256,2560]{1,0:T(8,128)(2,1)} %grad_rec_all.1.g_ref.refs_1_, bf16[256,1280]{1,0:T(8,128)(2,1)} %copy-done, bf16[256,640]{1,0:T(8,128)(2,1)} %get-tuple-element.211.a_ref.refs_3_), custom_call_target="tpu_custom_call" | custom-call | flops 1258291200 | bytes 8519680 | tf_op jit(solution)/shard_map/grads_out_xyo/pallas_call | solution.py:39
  419.0 7.8 %grads_own_xyo.1 = (f32[320,1920]{1,0:T(8,128)}, f32[160,1920]{1,0:T(8,128)}, f32[160,1920]{1,0:T(8,128)}, bf16[320,1920]{1,0:T(8,128)(2,1)}, bf16[320,1920]{1,0:T(8,128)(2,1)}) custom-call(bf16[256,2560]{1,0:T(8,128)(2,1)} %norm_first.1.nf_ref.refs_0_, bf16[256,2560]{1,0:T(8,128)(2,1)} %grad_rec_all.1.g_ref.refs_1_, bf16[256,1280]{1,0:T(8,128)(2,1)} %copy-done, ...), custom_call_target="tpu_custom_call" | custom-call | flops 1258291200 | bytes 15892480 | tf_op jit(solution)/shard_map/grads_own_xyo/pallas_call | solution.py:39
  426.8 13.2 %collective-permute-done.49.o2 = bf16[64,2560]{1,0:T(8,128)(2,1)} collective-permute-done((bf16[64,2560]{1,0:T(8,128)(2,1)}, bf16[64,2560]{1,0:T(8,128)(2,1)}, u32[]{:S(2)}, u32[]{:S(2)}) %collective-permute-start.49) | collective-permute-done | bytes 327712 | tf_op jit(solution)/shard_map/ppermute | solution.py:346
  440.0 6.4 %collective-permute-done.53.p2 = bf16[64,2560]{1,0:T(8,128)(2,1)S(1)} collective-permute-done((bf16[64,2560]{1,0:T(8,128)(2,1)S(1)}, bf16[64,2560]{1,0:T(8,128)(2,1)S(1)}, u32[]{:S(2)}, u32[]{:S(2)}) %collective-permute-start.53) | collective-permute-done | bytes 327712 | tf_op jit(solution)/shard_map/ppermute | solution.py:346
  446.5 3.3 first_back.1
  451.5 5.3 convert_add_fusion.5
  465.5 2.5 collective-permute-start.55
  470.7 2.7 pad_maximum_fusion.3
  478.1 11.3 %collective-permute-done.59 = f32[2,2560]{1,0:T(2,128)S(1)} collective-permute-done((f32[2,2560]{1,0:T(2,128)S(1)}, f32[2,2560]{1,0:T(2,128)S(1)}, u32[]{:S(2)}, u32[]{:S(2)}) %collective-permute-start.59) | collective-permute-done | bytes 20512 | tf_op jit(solution)/shard_map/ppermute | solution.py:346
  493.4 2.9 collective-permute-start.61
  501.1 16.5 %collective-permute-done.65 = f32[2,2560]{1,0:T(2,128)} collective-permute-done((f32[2,2560]{1,0:T(2,128)S(1)}, f32[2,2560]{1,0:T(2,128)}, u32[]{:S(2)}, u32[]{:S(2)}) %collective-permute-start.65) | collective-permute-done | bytes 20512 | tf_op jit(solution)/shard_map/ppermute | solution.py:346
  518.5 2.5 add_convert_fusion.1
  523.8 2.6 collective-permute-start.66
  529.6 7.1 %collective-permute-done.70 = f32[16,640]{1,0:T(8,128)S(1)} collective-permute-done((f32[16,640]{1,0:T(8,128)}, f32[16,640]{1,0:T(8,128)S(1)}, u32[]{:S(2)}, u32[]{:S(2)}) %collective-permute-start.70) | collective-permute-done | bytes 40992 | tf_op jit(solution)/shard_map/ppermute | solution.py:346
  542.2 3.1 tokens_grad_all.1
  (359 shorter events, 169.4 us)
Async XLA Ops:
  5.2 30.2 %collective-permute-start.1 = (bf16[320,1920]{1,0:T(8,128)(2,1)}, bf16[320,1920]{1,0:T(8,128)(2,1)S(1)}, u32[]{:S(2)}, u32[]{:S(2)}) collective-permute-start(bf16[320,1920]{1,0:T(8,128)(2,1)} %get-tuple-element.474), channel_id=1, source_target_pairs={{0,16},{4,20},{8,24},{12,28},{16,0},{20,4},{24,8},{28,12},{1,17},{... | collective-permute-start | bytes 3686408 | tf_op jit(solution)/shard_map/ppermute | solution.py:346
  8.2 28.7 %collective-permute-start = (bf16[320,1920]{1,0:T(8,128)(2,1)}, bf16[320,1920]{1,0:T(8,128)(2,1)S(1)}, u32[]{:S(2)}, u32[]{:S(2)}) collective-permute-start(bf16[320,1920]{1,0:T(8,128)(2,1)} %get-tuple-element.474), channel_id=1, source_target_pairs={{0,8},{4,12},{8,0},{12,4},{16,24},{20,28},{24,16},{28,20},{1,9},{5... | collective-permute-start | bytes 3686408 | tf_op jit(solution)/shard_map/ppermute | solution.py:346
  37.0 14.5 %collective-permute-start.2 = (bf16[160,1920]{1,0:T(8,128)(2,1)S(1)}, bf16[160,1920]{1,0:T(8,128)(2,1)S(1)}, u32[]{:S(2)}, u32[]{:S(2)}) collective-permute-start(bf16[160,1920]{1,0:T(8,128)(2,1)S(1)} %slice.268), channel_id=1, source_target_pairs={{0,8},{4,12},{8,0},{12,4},{16,24},{20,28},{24,16},{28,20},{1,9},{5... | collective-permute-start | bytes 1843208 | tf_op jit(solution)/shard_map/ppermute | solution.py:346
  38.5 14.1 %collective-permute-start.3 = (bf16[160,1920]{1,0:T(8,128)(2,1)S(1)}, bf16[160,1920]{1,0:T(8,128)(2,1)S(1)}, u32[]{:S(2)}, u32[]{:S(2)}) collective-permute-start(bf16[160,1920]{1,0:T(8,128)(2,1)S(1)} %slice.269), channel_id=1, source_target_pairs={{0,16},{4,20},{8,24},{12,28},{16,0},{20,4},{24,8},{28,12},{1,17},{... | collective-permute-start | bytes 1843208 | tf_op jit(solution)/shard_map/ppermute | solution.py:346
  57.1 29.8 %collective-permute-start.8 = (bf16[320,1920]{1,0:T(8,128)(2,1)}, bf16[320,1920]{1,0:T(8,128)(2,1)}, u32[]{:S(2)}, u32[]{:S(2)}) collective-permute-start(bf16[320,1920]{1,0:T(8,128)(2,1)} %pad_maximum_fusion.15), channel_id=1, source_target_pairs={{0,16},{4,20},{8,24},{12,28},{16,0},{20,4},{24,8},{28,12},{1,17},{... | collective-permute-start | bytes 3686408 | tf_op jit(solution)/shard_map/ppermute | solution.py:346
  57.8 29.5 %collective-permute-start.7 = (bf16[320,1920]{1,0:T(8,128)(2,1)}, bf16[320,1920]{1,0:T(8,128)(2,1)}, u32[]{:S(2)}, u32[]{:S(2)}) collective-permute-start(bf16[320,1920]{1,0:T(8,128)(2,1)} %pad_maximum_fusion.15), channel_id=1, source_target_pairs={{0,8},{4,12},{8,0},{12,4},{16,24},{20,28},{24,16},{28,20},{1,9},{5... | collective-permute-start | bytes 3686408 | tf_op jit(solution)/shard_map/ppermute | solution.py:346
  71.2 17.0 %collective-permute-start.6 = (bf16[256,640]{1,0:T(8,128)(2,1)}, bf16[256,640]{1,0:T(8,128)(2,1)}, u32[]{:S(2)}, u32[]{:S(2)}) collective-permute-start(bf16[256,640]{1,0:T(8,128)(2,1)} %get-tuple-element.199.c0), channel_id=1, source_target_pairs={{0,1},{1,0},{2,3},{3,2},{4,5},{5,4},{6,7},{7,6},{8,9},{9,8},{10,11... | collective-permute-start | bytes 983048 | tf_op jit(solution)/shard_map/ppermute | solution.py:346
  72.8 17.8 %collective-permute-start.5 = (bf16[256,640]{1,0:T(8,128)(2,1)}, bf16[256,640]{1,0:T(8,128)(2,1)}, u32[]{:S(2)}, u32[]{:S(2)}) collective-permute-start(bf16[256,640]{1,0:T(8,128)(2,1)} %get-tuple-element.199.c0), channel_id=1, source_target_pairs={{0,2},{1,3},{2,0},{3,1},{4,6},{5,7},{6,4},{7,5},{8,10},{9,11},{10,... | collective-permute-start | bytes 983048 | tf_op jit(solution)/shard_map/ppermute | solution.py:346
  95.4 46.7 %collective-permute-start.14 = (bf16[480,1920]{1,0:T(8,128)(2,1)}, bf16[480,1920]{1,0:T(8,128)(2,1)}, u32[]{:S(2)}, u32[]{:S(2)}) collective-permute-start(bf16[480,1920]{1,0:T(8,128)(2,1)} %get-tuple-element.462), channel_id=1, source_target_pairs={{0,16},{4,20},{8,24},{12,28},{16,0},{20,4},{24,8},{28,12},{1,17},{... | collective-permute-start | bytes 5529608 | tf_op jit(solution)/shard_map/ppermute | solution.py:346
  96.0 46.2 %collective-permute-start.13 = (bf16[480,1920]{1,0:T(8,128)(2,1)}, bf16[480,1920]{1,0:T(8,128)(2,1)}, u32[]{:S(2)}, u32[]{:S(2)}) collective-permute-start(bf16[480,1920]{1,0:T(8,128)(2,1)} %get-tuple-element.463), channel_id=1, source_target_pairs={{0,8},{4,12},{8,0},{12,4},{16,24},{20,28},{24,16},{28,20},{1,9},{5... | collective-permute-start | bytes 5529608 | tf_op jit(solution)/shard_map/ppermute | solution.py:346
  114.9 14.4 %collective-permute-start.11 = (bf16[64,2560]{1,0:T(8,128)(2,1)}, bf16[64,2560]{1,0:T(8,128)(2,1)S(1)}, u32[]{:S(2)}, u32[]{:S(2)}) collective-permute-start(bf16[64,2560]{1,0:T(8,128)(2,1)} %get-tuple-element.215), channel_id=1, source_target_pairs={{0,1},{1,0},{2,3},{3,2},{4,5},{5,4},{6,7},{7,6},{8,9},{9,8},{10,11... | collective-permute-start | bytes 983048 | tf_op jit(solution)/shard_map/ppermute | solution.py:346
  119.2 16.9 %collective-permute-start.10 = (bf16[64,2560]{1,0:T(8,128)(2,1)S(1)}, bf16[64,2560]{1,0:T(8,128)(2,1)S(1)}, u32[]{:S(2)}, u32[]{:S(2)}) collective-permute-start(bf16[64,2560]{1,0:T(8,128)(2,1)S(1)} %copy-done.59), channel_id=1, source_target_pairs={{0,1},{1,0},{2,3},{3,2},{4,5},{5,4},{6,7},{7,6},{8,9},{9,8},{10,11... | collective-permute-start | bytes 983048 | tf_op jit(solution)/shard_map/ppermute | solution.py:346
  129.4 12.8 %collective-permute-start.12 = (bf16[64,2560]{1,0:T(8,128)(2,1)S(1)}, bf16[64,2560]{1,0:T(8,128)(2,1)S(1)}, u32[]{:S(2)}, u32[]{:S(2)}) collective-permute-start(bf16[64,2560]{1,0:T(8,128)(2,1)S(1)} %add_convert_fusion.12), channel_id=1, source_target_pairs={{0,2},{1,3},{2,0},{3,1},{4,6},{5,7},{6,4},{7,5},{8,10},{9,11},{10,... | collective-permute-start | bytes 983048 | tf_op jit(solution)/shard_map/ppermute | solution.py:346
  146.6 24.4 %collective-permute-start.17 = (bf16[1280,1920]{1,0:T(8,128)(2,1)}, bf16[1280,1920]{1,0:T(8,128)(2,1)}, u32[]{:S(2)}, u32[]{:S(2)}) collective-permute-start(bf16[1280,1920]{1,0:T(8,128)(2,1)} %get-tuple-element.429.refs_3_), channel_id=1, source_target_pairs={{0,4},{4,0},{8,12},{12,8},{16,20},{20,16},{24,28},{28,24},{1,5},{5... | collective-permute-start | bytes 14745608 | tf_op jit(solution)/shard_map/ppermute | solution.py:346
  148.7 52.6 %collective-permute-start.20 = (bf16[480,1920]{1,0:T(8,128)(2,1)}, bf16[480,1920]{1,0:T(8,128)(2,1)}, u32[]{:S(2)}, u32[]{:S(2)}) collective-permute-start(bf16[480,1920]{1,0:T(8,128)(2,1)} %get-tuple-element.460), channel_id=1, source_target_pairs={{0,16},{4,20},{8,24},{12,28},{16,0},{20,4},{24,8},{28,12},{1,17},{... | collective-permute-start | bytes 5529608 | tf_op jit(solution)/shard_map/ppermute | solution.py:346
  149.3 52.0 %collective-permute-start.19 = (bf16[480,1920]{1,0:T(8,128)(2,1)}, bf16[480,1920]{1,0:T(8,128)(2,1)}, u32[]{:S(2)}, u32[]{:S(2)}) collective-permute-start(bf16[480,1920]{1,0:T(8,128)(2,1)} %get-tuple-element.461), channel_id=1, source_target_pairs={{0,8},{4,12},{8,0},{12,4},{16,24},{20,28},{24,16},{28,20},{1,9},{5... | collective-permute-start | bytes 5529608 | tf_op jit(solution)/shard_map/ppermute | solution.py:346
  153.8 17.2 %collective-permute-start.16 = (bf16[64,2560]{1,0:T(8,128)(2,1)}, bf16[64,2560]{1,0:T(8,128)(2,1)S(1)}, u32[]{:S(2)}, u32[]{:S(2)}) collective-permute-start(bf16[64,2560]{1,0:T(8,128)(2,1)} %get-tuple-element.222.p0), channel_id=1, source_target_pairs={{0,2},{1,3},{2,0},{3,1},{4,6},{5,7},{6,4},{7,5},{8,10},{9,11},{10,... | collective-permute-start | bytes 983048 | tf_op jit(solution)/shard_map/ppermute | solution.py:346
  153.8 19.8 %collective-permute-start.15 = (bf16[64,2560]{1,0:T(8,128)(2,1)}, bf16[64,2560]{1,0:T(8,128)(2,1)S(1)}, u32[]{:S(2)}, u32[]{:S(2)}) collective-permute-start(bf16[64,2560]{1,0:T(8,128)(2,1)} %get-tuple-element.222.p0), channel_id=1, source_target_pairs={{0,1},{1,0},{2,3},{3,2},{4,5},{5,4},{6,7},{7,6},{8,9},{9,8},{10,11... | collective-permute-start | bytes 983048 | tf_op jit(solution)/shard_map/ppermute | solution.py:346
  201.4 13.9 %collective-permute-start.22 = (bf16[1280,1920]{1,0:T(8,128)(2,1)}, bf16[1280,1920]{1,0:T(8,128)(2,1)}, u32[]{:S(2)}, u32[]{:S(2)}) collective-permute-start(bf16[1280,1920]{1,0:T(8,128)(2,1)} %grads_out_ffn_0.1), channel_id=1, source_target_pairs={{0,4},{4,0},{8,12},{12,8},{16,20},{20,16},{24,28},{28,24},{1,5},{5... | collective-permute-start | bytes 14745608 | tf_op jit(solution)/shard_map/ppermute | solution.py:346
  205.8 17.3 %collective-permute-start.21 = (bf16[1280,1920]{1,0:T(8,128)(2,1)}, bf16[1280,1920]{1,0:T(8,128)(2,1)}, u32[]{:S(2)}, u32[]{:S(2)}) collective-permute-start(bf16[1280,1920]{1,0:T(8,128)(2,1)} %get-tuple-element.425.refs_3_), channel_id=1, source_target_pairs={{0,4},{4,0},{8,12},{12,8},{16,20},{20,16},{24,28},{28,24},{1,5},{5... | collective-permute-start | bytes 14745608 | tf_op jit(solution)/shard_map/ppermute | solution.py:346
  207.5 29.0 %collective-permute-start.23 = (bf16[160,1920]{1,0:T(8,128)(2,1)S(1)}, bf16[160,1920]{1,0:T(8,128)(2,1)S(1)}, u32[]{:S(2)}, u32[]{:S(2)}) collective-permute-start(bf16[160,1920]{1,0:T(8,128)(2,1)S(1)} %get-tuple-element.426), channel_id=1, source_target_pairs={{0,8},{4,12},{8,0},{12,4},{16,24},{20,28},{24,16},{28,20},{1,9},{5... | collective-permute-start | bytes 1843208 | tf_op jit(solution)/shard_map/ppermute | solution.py:346
  209.0 27.5 %collective-permute-start.24 = (bf16[160,1920]{1,0:T(8,128)(2,1)S(1)}, bf16[160,1920]{1,0:T(8,128)(2,1)S(1)}, u32[]{:S(2)}, u32[]{:S(2)}) collective-permute-start(bf16[160,1920]{1,0:T(8,128)(2,1)S(1)} %get-tuple-element.424), channel_id=1, source_target_pairs={{0,16},{4,20},{8,24},{12,28},{16,0},{20,4},{24,8},{28,12},{1,17},{... | collective-permute-start | bytes 1843208 | tf_op jit(solution)/shard_map/ppermute | solution.py:346
  246.8 17.1 %collective-permute-start.28 = (bf16[1280,1920]{1,0:T(8,128)(2,1)}, bf16[1280,1920]{1,0:T(8,128)(2,1)}, u32[]{:S(2)}, u32[]{:S(2)}) collective-permute-start(bf16[1280,1920]{1,0:T(8,128)(2,1)} %grads_out_ffn_1.1), channel_id=1, source_target_pairs={{0,4},{4,0},{8,12},{12,8},{16,20},{20,16},{24,28},{28,24},{1,5},{5... | collective-permute-start | bytes 14745608 | tf_op jit(solution)/shard_map/ppermute | solution.py:346
  260.5 11.2 %collective-permute-start.27 = (bf16[64,2560]{1,0:T(8,128)(2,1)}, bf16[64,2560]{1,0:T(8,128)(2,1)S(1)}, u32[]{:S(2)}, u32[]{:S(2)}) collective-permute-start(bf16[64,2560]{1,0:T(8,128)(2,1)} %get-tuple-element.255), channel_id=1, source_target_pairs={{0,1},{1,0},{2,3},{3,2},{4,5},{5,4},{6,7},{7,6},{8,9},{9,8},{10,11... | collective-permute-start | bytes 983048 | tf_op jit(solution)/shard_map/ppermute | solution.py:346
  260.8 29.3 %collective-permute-start.30 = (bf16[320,1920]{1,0:T(8,128)(2,1)}, bf16[320,1920]{1,0:T(8,128)(2,1)S(1)}, u32[]{:S(2)}, u32[]{:S(2)}) collective-permute-start(bf16[320,1920]{1,0:T(8,128)(2,1)} %get-tuple-element.263), channel_id=1, source_target_pairs={{0,8},{4,12},{8,0},{12,4},{16,24},{20,28},{24,16},{28,20},{1,9},{5... | collective-permute-start | bytes 3686408 | tf_op jit(solution)/shard_map/ppermute | solution.py:346
  261.3 29.2 %collective-permute-start.31 = (bf16[320,1920]{1,0:T(8,128)(2,1)}, bf16[320,1920]{1,0:T(8,128)(2,1)S(1)}, u32[]{:S(2)}, u32[]{:S(2)}) collective-permute-start(bf16[320,1920]{1,0:T(8,128)(2,1)} %get-tuple-element.264), channel_id=1, source_target_pairs={{0,16},{4,20},{8,24},{12,28},{16,0},{20,4},{24,8},{28,12},{1,17},{... | collective-permute-start | bytes 3686408 | tf_op jit(solution)/shard_map/ppermute | solution.py:346
  262.1 28.4 %collective-permute-start.26 = (bf16[64,2560]{1,0:T(8,128)(2,1)}, bf16[64,2560]{1,0:T(8,128)(2,1)S(1)}, u32[]{:S(2)}, u32[]{:S(2)}) collective-permute-start(bf16[64,2560]{1,0:T(8,128)(2,1)} %get-tuple-element.253), channel_id=1, source_target_pairs={{0,1},{1,0},{2,3},{3,2},{4,5},{5,4},{6,7},{7,6},{8,9},{9,8},{10,11... | collective-permute-start | bytes 983048 | tf_op jit(solution)/shard_map/ppermute | solution.py:346
  272.4 18.1 %collective-permute-start.29 = (bf16[64,2560]{1,0:T(8,128)(2,1)}, bf16[64,2560]{1,0:T(8,128)(2,1)}, u32[]{:S(2)}, u32[]{:S(2)}) collective-permute-start(bf16[64,2560]{1,0:T(8,128)(2,1)} %add_convert_fusion.11), channel_id=1, source_target_pairs={{0,2},{1,3},{2,0},{3,1},{4,6},{5,7},{6,4},{7,5},{8,10},{9,11},{10,... | collective-permute-start | bytes 983048 | tf_op jit(solution)/shard_map/ppermute | solution.py:346
  290.5 9.6 %collective-permute-start.34 = (bf16[1280,1920]{1,0:T(8,128)(2,1)}, bf16[1280,1920]{1,0:T(8,128)(2,1)}, u32[]{:S(2)}, u32[]{:S(2)}) collective-permute-start(bf16[1280,1920]{1,0:T(8,128)(2,1)} %grads_out_ffn_2.1), channel_id=1, source_target_pairs={{0,4},{4,0},{8,12},{12,8},{16,20},{20,16},{24,28},{28,24},{1,5},{5... | collective-permute-start | bytes 14745608 | tf_op jit(solution)/shard_map/ppermute | solution.py:346
  291.6 51.3 %collective-permute-start.39 = (bf16[480,1920]{1,0:T(8,128)(2,1)S(1)}, bf16[480,1920]{1,0:T(8,128)(2,1)}, u32[]{:S(2)}, u32[]{:S(2)}) collective-permute-start(bf16[480,1920]{1,0:T(8,128)(2,1)S(1)} %pad_maximum_fusion.9), channel_id=1, source_target_pairs={{0,16},{4,20},{8,24},{12,28},{16,0},{20,4},{24,8},{28,12},{1,17},{... | collective-permute-start | bytes 5529608 | tf_op jit(solution)/shard_map/ppermute | solution.py:346
  293.1 49.8 %collective-permute-start.38 = (bf16[480,1920]{1,0:T(8,128)(2,1)S(1)}, bf16[480,1920]{1,0:T(8,128)(2,1)}, u32[]{:S(2)}, u32[]{:S(2)}) collective-permute-start(bf16[480,1920]{1,0:T(8,128)(2,1)S(1)} %pad_maximum_fusion.8), channel_id=1, source_target_pairs={{0,8},{4,12},{8,0},{12,4},{16,24},{20,28},{24,16},{28,20},{1,9},{5... | collective-permute-start | bytes 5529608 | tf_op jit(solution)/shard_map/ppermute | solution.py:346
  297.8 17.7 %collective-permute-start.33 = (bf16[64,2560]{1,0:T(8,128)(2,1)}, bf16[64,2560]{1,0:T(8,128)(2,1)}, u32[]{:S(2)}, u32[]{:S(2)}) collective-permute-start(bf16[64,2560]{1,0:T(8,128)(2,1)} %get-tuple-element.270.p0), channel_id=1, source_target_pairs={{0,2},{1,3},{2,0},{3,1},{4,6},{5,7},{6,4},{7,5},{8,10},{9,11},{10,... | collective-permute-start | bytes 983048 | tf_op jit(solution)/shard_map/ppermute | solution.py:346
  299.8 19.6 %collective-permute-start.32 = (bf16[64,2560]{1,0:T(8,128)(2,1)}, bf16[64,2560]{1,0:T(8,128)(2,1)}, u32[]{:S(2)}, u32[]{:S(2)}) collective-permute-start(bf16[64,2560]{1,0:T(8,128)(2,1)} %get-tuple-element.270.p0), channel_id=1, source_target_pairs={{0,1},{1,0},{2,3},{3,2},{4,5},{5,4},{6,7},{7,6},{8,9},{9,8},{10,11... | collective-permute-start | bytes 983048 | tf_op jit(solution)/shard_map/ppermute | solution.py:346
  315.5 11.0 %collective-permute-start.35 = (bf16[64,2560]{1,0:T(8,128)(2,1)}, bf16[64,2560]{1,0:T(8,128)(2,1)}, u32[]{:S(2)}, u32[]{:S(2)}) collective-permute-start(bf16[64,2560]{1,0:T(8,128)(2,1)} %collective-permute-done.33.p2), channel_id=1, source_target_pairs={{0,1},{1,0},{2,3},{3,2},{4,5},{5,4},{6,7},{7,6},{8,9},{9,8},{10,11... | collective-permute-start | bytes 983048 | tf_op jit(solution)/shard_map/ppermute | solution.py:346
  317.4 25.4 %collective-permute-start.37 = (bf16[128,2560]{1,0:T(8,128)(2,1)}, bf16[128,2560]{1,0:T(8,128)(2,1)}, u32[]{:S(2)}, u32[]{:S(2)}) collective-permute-start(bf16[128,2560]{1,0:T(8,128)(2,1)} %pad_maximum_fusion.19), channel_id=1, source_target_pairs={{0,1},{1,0},{2,3},{3,2},{4,5},{5,4},{6,7},{7,6},{8,9},{9,8},{10,11... | collective-permute-start | bytes 1966088 | tf_op jit(solution)/shard_map/ppermute | solution.py:346
  339.3 12.4 %collective-permute-start.40 = (bf16[256,640]{1,0:T(8,128)(2,1)}, bf16[256,640]{1,0:T(8,128)(2,1)S(1)}, u32[]{:S(2)}, u32[]{:S(2)}) collective-permute-start(bf16[256,640]{1,0:T(8,128)(2,1)} %get-tuple-element.292), channel_id=1, source_target_pairs={{0,1},{1,0},{2,3},{3,2},{4,5},{5,4},{6,7},{7,6},{8,9},{9,8},{10,11... | collective-permute-start | bytes 983048 | tf_op jit(solution)/shard_map/ppermute | solution.py:346
  339.3 21.9 %collective-permute-start.36 = (bf16[256,640]{1,0:T(8,128)(2,1)}, bf16[256,640]{1,0:T(8,128)(2,1)S(1)}, u32[]{:S(2)}, u32[]{:S(2)}) collective-permute-start(bf16[256,640]{1,0:T(8,128)(2,1)} %get-tuple-element.282), channel_id=1, source_target_pairs={{0,1},{1,0},{2,3},{3,2},{4,5},{5,4},{6,7},{7,6},{8,9},{9,8},{10,11... | collective-permute-start | bytes 983048 | tf_op jit(solution)/shard_map/ppermute | solution.py:346
  342.8 15.4 %collective-permute-start.43 = (bf16[10,4,64,128]{3,2,1,0:T(8,128)(2,1)S(1)}, bf16[10,4,64,128]{3,2,1,0:T(8,128)(2,1)S(1)}, u32[]{:S(2)}, u32[]{:S(2)}) collective-permute-start(bf16[10,4,64,128]{3,2,1,0:T(8,128)(2,1)S(1)} %convert_element_type.173), channel_id=1, source_target_pairs={{0,4},{4,0},{8,12},{12,8},{16,20},{20,16},{24,28},{28,24},{1,5},{5... | collective-permute-start | bytes 1966088 | tf_op jit(solution)/shard_map/ppermute | solution.py:346
  351.8 20.2 %collective-permute-start.41 = (bf16[256,640]{1,0:T(8,128)(2,1)S(1)}, bf16[256,640]{1,0:T(8,128)(2,1)S(1)}, u32[]{:S(2)}, u32[]{:S(2)}) collective-permute-start(bf16[256,640]{1,0:T(8,128)(2,1)S(1)} %add_convert_fusion.10), channel_id=1, source_target_pairs={{0,2},{1,3},{2,0},{3,1},{4,6},{5,7},{6,4},{7,5},{8,10},{9,11},{10,... | collective-permute-start | bytes 983048 | tf_op jit(solution)/shard_map/ppermute | solution.py:346
  353.4 52.9 %collective-permute-start.47 = (bf16[480,1920]{1,0:T(8,128)(2,1)S(1)}, bf16[480,1920]{1,0:T(8,128)(2,1)}, u32[]{:S(2)}, u32[]{:S(2)}) collective-permute-start(bf16[480,1920]{1,0:T(8,128)(2,1)S(1)} %pad_maximum_fusion.11), channel_id=1, source_target_pairs={{0,16},{4,20},{8,24},{12,28},{16,0},{20,4},{24,8},{28,12},{1,17},{... | collective-permute-start | bytes 5529608 | tf_op jit(solution)/shard_map/ppermute | solution.py:346
  357.1 49.2 %collective-permute-start.46 = (bf16[480,1920]{1,0:T(8,128)(2,1)}, bf16[480,1920]{1,0:T(8,128)(2,1)}, u32[]{:S(2)}, u32[]{:S(2)}) collective-permute-start(bf16[480,1920]{1,0:T(8,128)(2,1)} %pad_maximum_fusion.10), channel_id=1, source_target_pairs={{0,8},{4,12},{8,0},{12,4},{16,24},{20,28},{24,16},{28,20},{1,9},{5... | collective-permute-start | bytes 5529608 | tf_op jit(solution)/shard_map/ppermute | solution.py:346
  358.2 17.4 %collective-permute-start.42 = (bf16[64,2560]{1,0:T(8,128)(2,1)S(1)}, bf16[64,2560]{1,0:T(8,128)(2,1)}, u32[]{:S(2)}, u32[]{:S(2)}) collective-permute-start(bf16[64,2560]{1,0:T(8,128)(2,1)S(1)} %add_convert_fusion.9), channel_id=1, source_target_pairs={{0,2},{1,3},{2,0},{3,1},{4,6},{5,7},{6,4},{7,5},{8,10},{9,11},{10,... | collective-permute-start | bytes 983048 | tf_op jit(solution)/shard_map/ppermute | solution.py:346
  375.6 29.6 %collective-permute-start.48 = (bf16[10,4,64,128]{3,2,1,0:T(8,128)(2,1)S(1)}, bf16[10,4,64,128]{3,2,1,0:T(8,128)(2,1)S(1)}, u32[]{:S(2)}, u32[]{:S(2)}) collective-permute-start(bf16[10,4,64,128]{3,2,1,0:T(8,128)(2,1)S(1)} %convert_add_fusion.2), channel_id=1, source_target_pairs={{0,8},{4,12},{8,0},{12,4},{16,24},{20,28},{24,16},{28,20},{1,9},{5... | collective-permute-start | bytes 1966088 | tf_op jit(solution)/shard_map/ppermute | solution.py:346
  393.3 12.9 %collective-permute-start.45 = (bf16[64,2560]{1,0:T(8,128)(2,1)}, bf16[64,2560]{1,0:T(8,128)(2,1)}, u32[]{:S(2)}, u32[]{:S(2)}) collective-permute-start(bf16[64,2560]{1,0:T(8,128)(2,1)} %get-tuple-element.305), channel_id=1, source_target_pairs={{0,1},{1,0},{2,3},{3,2},{4,5},{5,4},{6,7},{7,6},{8,9},{9,8},{10,11... | collective-permute-start | bytes 983048 | tf_op jit(solution)/shard_map/ppermute | solution.py:346
  406.2 9.8 %collective-permute-start.52 = (bf16[1280,1920]{1,0:T(8,128)(2,1)}, bf16[1280,1920]{1,0:T(8,128)(2,1)}, u32[]{:S(2)}, u32[]{:S(2)}) collective-permute-start(bf16[1280,1920]{1,0:T(8,128)(2,1)} %grads_out_xyo.1), channel_id=1, source_target_pairs={{0,4},{4,0},{8,12},{12,8},{16,20},{20,16},{24,28},{28,24},{1,5},{5... | collective-permute-start | bytes 14745608 | tf_op jit(solution)/shard_map/ppermute | solution.py:346
  406.9 19.9 %collective-permute-start.44 = (bf16[64,2560]{1,0:T(8,128)(2,1)}, bf16[64,2560]{1,0:T(8,128)(2,1)}, u32[]{:S(2)}, u32[]{:S(2)}) collective-permute-start(bf16[64,2560]{1,0:T(8,128)(2,1)} %get-tuple-element.303), channel_id=1, source_target_pairs={{0,1},{1,0},{2,3},{3,2},{4,5},{5,4},{6,7},{7,6},{8,9},{9,8},{10,11... | collective-permute-start | bytes 983048 | tf_op jit(solution)/shard_map/ppermute | solution.py:346
  410.3 36.1 %collective-permute-start.50 = (bf16[160,1920]{1,0:T(8,128)(2,1)S(1)}, bf16[160,1920]{1,0:T(8,128)(2,1)}, u32[]{:S(2)}, u32[]{:S(2)}) collective-permute-start(bf16[160,1920]{1,0:T(8,128)(2,1)S(1)} %add_convert_fusion.3), channel_id=1, source_target_pairs={{0,8},{4,12},{8,0},{12,4},{16,24},{20,28},{24,16},{28,20},{1,9},{5... | collective-permute-start | bytes 1843208 | tf_op jit(solution)/shard_map/ppermute | solution.py:346
  413.0 33.4 %collective-permute-start.51 = (bf16[160,1920]{1,0:T(8,128)(2,1)}, bf16[160,1920]{1,0:T(8,128)(2,1)}, u32[]{:S(2)}, u32[]{:S(2)}) collective-permute-start(bf16[160,1920]{1,0:T(8,128)(2,1)} %add_convert_fusion.2), channel_id=1, source_target_pairs={{0,16},{4,20},{8,24},{12,28},{16,0},{20,4},{24,8},{28,12},{1,17},{... | collective-permute-start | bytes 1843208 | tf_op jit(solution)/shard_map/ppermute | solution.py:346
  415.4 24.6 %collective-permute-start.49 = (bf16[64,2560]{1,0:T(8,128)(2,1)}, bf16[64,2560]{1,0:T(8,128)(2,1)}, u32[]{:S(2)}, u32[]{:S(2)}) collective-permute-start(bf16[64,2560]{1,0:T(8,128)(2,1)} %add_convert_fusion.8), channel_id=1, source_target_pairs={{0,2},{1,3},{2,0},{3,1},{4,6},{5,7},{6,4},{7,5},{8,10},{9,11},{10,... | collective-permute-start | bytes 983048 | tf_op jit(solution)/shard_map/ppermute | solution.py:346
  416.1 30.4 %collective-permute-start.53 = (bf16[64,2560]{1,0:T(8,128)(2,1)S(1)}, bf16[64,2560]{1,0:T(8,128)(2,1)S(1)}, u32[]{:S(2)}, u32[]{:S(2)}) collective-permute-start(bf16[64,2560]{1,0:T(8,128)(2,1)S(1)} %concatenate.147.p0), channel_id=1, source_target_pairs={{0,2},{1,3},{2,0},{3,1},{4,6},{5,7},{6,4},{7,5},{8,10},{9,11},{10,... | collective-permute-start | bytes 983048 | tf_op jit(solution)/shard_map/ppermute | solution.py:346
  460.6 12.8 %collective-permute-start.58 = (f32[2,2560]{1,0:T(2,128)S(1)}, f32[2,2560]{1,0:T(2,128)}, u32[]{:S(2)}, u32[]{:S(2)}) collective-permute-start(f32[2,2560]{1,0:T(2,128)S(1)} %concatenate.158), channel_id=1, source_target_pairs={{0,1},{1,0},{2,3},{3,2},{4,5},{5,4},{6,7},{7,6},{8,9},{9,8},{10,11... | collective-permute-start | bytes 61448 | tf_op jit(solution)/shard_map/ppermute | solution.py:346
  460.7 29.5 %collective-permute-start.57 = (f32[16,640]{1,0:T(8,128)}, f32[16,640]{1,0:T(8,128)}, u32[]{:S(2)}, u32[]{:S(2)}) collective-permute-start(f32[16,640]{1,0:T(8,128)} %add.372), channel_id=1, source_target_pairs={{0,8},{4,12},{8,0},{12,4},{16,24},{20,28},{24,16},{28,20},{1,9},{5... | collective-permute-start | bytes 122888 | tf_op jit(solution)/shard_map/ppermute | solution.py:346
  465.5 27.8 %collective-permute-start.55 = (bf16[64,2560]{1,0:T(8,128)(2,1)}, bf16[64,2560]{1,0:T(8,128)(2,1)}, u32[]{:S(2)}, u32[]{:S(2)}) collective-permute-start(bf16[64,2560]{1,0:T(8,128)(2,1)} %concatenate.149.p0), channel_id=1, source_target_pairs={{0,2},{1,3},{2,0},{3,1},{4,6},{5,7},{6,4},{7,5},{8,10},{9,11},{10,... | collective-permute-start | bytes 983048 | tf_op jit(solution)/shard_map/ppermute | solution.py:346
  468.1 24.7 %collective-permute-start.56 = (bf16[10,4,64,128]{3,2,1,0:T(8,128)(2,1)}, bf16[10,4,64,128]{3,2,1,0:T(8,128)(2,1)S(1)}, u32[]{:S(2)}, u32[]{:S(2)}) collective-permute-start(bf16[10,4,64,128]{3,2,1,0:T(8,128)(2,1)} %convert_add_fusion.1), channel_id=1, source_target_pairs={{0,16},{4,20},{8,24},{12,28},{16,0},{20,4},{24,8},{28,12},{1,17},{... | collective-permute-start | bytes 1966088 | tf_op jit(solution)/shard_map/ppermute | solution.py:346
  470.5 22.8 %collective-permute-start.60 = (bf16[128,2560]{1,0:T(8,128)(2,1)S(1)}, bf16[128,2560]{1,0:T(8,128)(2,1)S(1)}, u32[]{:S(2)}, u32[]{:S(2)}) collective-permute-start(bf16[128,2560]{1,0:T(8,128)(2,1)S(1)} %pad_maximum_fusion.20), channel_id=1, source_target_pairs={{0,1},{1,0},{2,3},{3,2},{4,5},{5,4},{6,7},{7,6},{8,9},{9,8},{10,11... | collective-permute-start | bytes 1966088 | tf_op jit(solution)/shard_map/ppermute | solution.py:346
  474.2 15.2 %collective-permute-start.59 = (f32[2,2560]{1,0:T(2,128)S(1)}, f32[2,2560]{1,0:T(2,128)S(1)}, u32[]{:S(2)}, u32[]{:S(2)}) collective-permute-start(f32[2,2560]{1,0:T(2,128)S(1)} %add.387), channel_id=1, source_target_pairs={{0,2},{1,3},{2,0},{3,1},{4,6},{5,7},{6,4},{7,5},{8,10},{9,11},{10,... | collective-permute-start | bytes 61448 | tf_op jit(solution)/shard_map/ppermute | solution.py:346
  489.4 29.0 %collective-permute-start.62 = (bf16[320,1920]{1,0:T(8,128)(2,1)}, bf16[320,1920]{1,0:T(8,128)(2,1)S(1)}, u32[]{:S(2)}, u32[]{:S(2)}) collective-permute-start(bf16[320,1920]{1,0:T(8,128)(2,1)} %get-tuple-element.344), channel_id=1, source_target_pairs={{0,8},{4,12},{8,0},{12,4},{16,24},{20,28},{24,16},{28,20},{1,9},{5... | collective-permute-start | bytes 3686408 | tf_op jit(solution)/shard_map/ppermute | solution.py:346
  490.1 28.3 %collective-permute-start.63 = (bf16[320,1920]{1,0:T(8,128)(2,1)}, bf16[320,1920]{1,0:T(8,128)(2,1)}, u32[]{:S(2)}, u32[]{:S(2)}) collective-permute-start(bf16[320,1920]{1,0:T(8,128)(2,1)} %get-tuple-element.345), channel_id=1, source_target_pairs={{0,16},{4,20},{8,24},{12,28},{16,0},{20,4},{24,8},{28,12},{1,17},{... | collective-permute-start | bytes 3686408 | tf_op jit(solution)/shard_map/ppermute | solution.py:346
  493.4 25.0 %collective-permute-start.61 = (bf16[64,2560]{1,0:T(8,128)(2,1)}, bf16[64,2560]{1,0:T(8,128)(2,1)S(1)}, u32[]{:S(2)}, u32[]{:S(2)}) collective-permute-start(bf16[64,2560]{1,0:T(8,128)(2,1)} %collective-permute-done.55.p2), channel_id=1, source_target_pairs={{0,1},{1,0},{2,3},{3,2},{4,5},{5,4},{6,7},{7,6},{8,9},{9,8},{10,11... | collective-permute-start | bytes 983048 | tf_op jit(solution)/shard_map/ppermute | solution.py:346
  496.4 21.3 %collective-permute-start.65 = (f32[2,2560]{1,0:T(2,128)S(1)}, f32[2,2560]{1,0:T(2,128)}, u32[]{:S(2)}, u32[]{:S(2)}) collective-permute-start(f32[2,2560]{1,0:T(2,128)S(1)} %add.389), channel_id=1, source_target_pairs={{0,8},{4,12},{8,0},{12,4},{16,24},{20,28},{24,16},{28,20},{1,9},{5... | collective-permute-start | bytes 61448 | tf_op jit(solution)/shard_map/ppermute | solution.py:346
  521.0 25.0 %collective-permute-start.68 = (bf16[160,1920]{1,0:T(8,128)(2,1)}, bf16[160,1920]{1,0:T(8,128)(2,1)}, u32[]{:S(2)}, u32[]{:S(2)}) collective-permute-start(bf16[160,1920]{1,0:T(8,128)(2,1)} %add_convert_fusion.1), channel_id=1, source_target_pairs={{0,8},{4,12},{8,0},{12,4},{16,24},{20,28},{24,16},{28,20},{1,9},{5... | collective-permute-start | bytes 1843208 | tf_op jit(solution)/shard_map/ppermute | solution.py:346
  522.5 23.5 %collective-permute-start.69 = (bf16[160,1920]{1,0:T(8,128)(2,1)}, bf16[160,1920]{1,0:T(8,128)(2,1)}, u32[]{:S(2)}, u32[]{:S(2)}) collective-permute-start(bf16[160,1920]{1,0:T(8,128)(2,1)} %add_convert_fusion), channel_id=1, source_target_pairs={{0,16},{4,20},{8,24},{12,28},{16,0},{20,4},{24,8},{28,12},{1,17},{... | collective-permute-start | bytes 1843208 | tf_op jit(solution)/shard_map/ppermute | solution.py:346
  523.8 18.4 %collective-permute-start.66 = (bf16[64,2560]{1,0:T(8,128)(2,1)}, bf16[64,2560]{1,0:T(8,128)(2,1)}, u32[]{:S(2)}, u32[]{:S(2)}) collective-permute-start(bf16[64,2560]{1,0:T(8,128)(2,1)} %concatenate.149.p0), channel_id=1, source_target_pairs={{0,1},{1,0},{2,3},{3,2},{4,5},{5,4},{6,7},{7,6},{8,9},{9,8},{10,11... | collective-permute-start | bytes 983048 | tf_op jit(solution)/shard_map/ppermute | solution.py:346
  526.3 10.4 %collective-permute-start.70 = (f32[16,640]{1,0:T(8,128)}, f32[16,640]{1,0:T(8,128)S(1)}, u32[]{:S(2)}, u32[]{:S(2)}) collective-permute-start(f32[16,640]{1,0:T(8,128)} %add.386), channel_id=1, source_target_pairs={{0,16},{4,20},{8,24},{12,28},{16,0},{20,4},{24,8},{28,12},{1,17},{... | collective-permute-start | bytes 122888 | tf_op jit(solution)/shard_map/ppermute | solution.py:346
  (67 other events, 494.7 us)

commit v3 on v2

v3 whole, which is shorter than its diff:
```python
from functools import partial

import jax
import jax.numpy as jnp
from jax import lax
from jax.experimental import pallas as pl
from jax.experimental.pallas import tpu as pltpu
from jax.sharding import PartitionSpec as P

eps = 1e-06
f32 = jnp.float32
bf16 = jnp.bfloat16
vmem = pl.BlockSpec(memory_space=pltpu.VMEM)
smem = pl.BlockSpec(memory_space=pltpu.SMEM)
MIB = 1024 * 1024
chunk_count = 3


def nn(a, b):
    return lax.dot_general(a, b, (((1,), (0,)), ((), ())), preferred_element_type=f32)


def nt(a, b):
    return lax.dot_general(a, b, (((1,), (1,)), ((), ())), preferred_element_type=f32)


def tn(a, b):
    return lax.dot_general(a, b, (((0,), (0,)), ((), ())), preferred_element_type=f32)


def full(v):
    zeros = (0,) * len(v.shape)
    return pl.BlockSpec(v.shape, lambda i: zeros, pipeline_mode=pl.Buffered(1))


def block(shape, *index):
    return pl.BlockSpec(shape, lambda i: index)


def hint_of(micros):
    return pl.CostEstimate(
        flops=1, bytes_accessed=max(1, int(micros * 3.0e6)), transcendentals=0
    )


hint = hint_of(0)


def call(kernel, outs, *args, scalars=0, mem=60, specs=None, out_specs=None, alias=None, scratch=(), micros=0, name=None):
    specs = specs or {}
    return pl.pallas_call(
        kernel,
        grid=(1,),
        out_shape=outs,
        in_specs=[smem] * scalars
        + [specs.get(i) or full(a) for i, a in enumerate(args) if i >= scalars],
        out_specs=out_specs or [full(s) for s in outs],
        scratch_shapes=scratch,
        input_output_aliases=alias or {},
        compiler_params=pltpu.CompilerParams(vmem_limit_bytes=mem * MIB),
        cost_estimate=hint_of(micros),
        name=name,
    )(*args)


def like(shape, dtype):
    return jax.ShapeDtypeStruct(shape, dtype)


def gelu_pair(v):
    c = 0.7978845608028654
    sq = v * v
    t = jnp.tanh(c * v * (1.0 + 0.044715 * sq))
    half = 0.5 * (1.0 + t)
    slope = half + 0.5 * v * (1.0 - t * t) * c * (1.0 + 3.0 * 0.044715 * sq)
    return v * half, slope


def one_less_exp(x):
    series = x * (
        1.0
        - x * (1 / 2) * (1.0 - x * (1 / 3) * (1.0 - x * (1 / 4) * (1.0 - x * (1 / 5) * (
            1.0 - x * (1 / 6) * (1.0 - x * (1 / 7) * (1.0 - x * (1 / 8)))))))
    )
    return jnp.where(x < 0.5, series, 1.0 - jnp.exp(-x))


def softplus(v):
    return jnp.maximum(v, 0.0) + jnp.log1p(jnp.exp(-jnp.abs(v)))


def sigmoid(v):
    return 1.0 / (1.0 + jnp.exp(-v))


def row_ids(shape):
    return lax.broadcasted_iota(jnp.int32, shape, 0)


def down_rows(v, steps, fill=0.0):
    return jnp.where(row_ids(v.shape) >= steps, pltpu.roll(v, steps, 0), fill)


def up_rows(v, steps, fill=0.0):
    rows = v.shape[0]
    return jnp.where(row_ids(v.shape) < rows - steps, pltpu.roll(v, rows - steps, 0), fill)


def scan_rows(decay, drive, shift):
    steps = 1
    while steps < decay.shape[0]:
        drive = decay * shift(drive, steps) + drive
        if steps * 2 < decay.shape[0]:
            decay = decay * shift(decay, steps, 1.0)
        steps *= 2
    return drive


def norm_first_kernel(size, z_ref, x_ref, one_ref, two_ref, rel_ref, out_ref, one_out, two_out):
    me = z_ref[1]
    gain = to_rel(me, size, one_ref[...])
    rel = to_rel(me, size, x_ref[...].astype(f32))
    rel_ref[...] = rel.astype(bf16)
    inv = lax.rsqrt(jnp.mean(rel * rel, axis=1, keepdims=True) + eps)
    out_ref[...] = (rel * inv * gain).astype(bf16)
    one_out[...] = gain
    two_out[...] = to_rel(me, size, two_ref[...])


def to_rel_kernel(size, z_ref, x_ref, rel_ref):
    rel_ref[...] = to_rel(z_ref[1], size, x_ref[...].astype(f32)).astype(bf16)


def shard_kernel(gate_ref, up_ref, down_ref, out_ref):
    width = gate_ref.shape[1]
    out_ref[:, :width] = gate_ref[...]
    out_ref[:, width : 2 * width] = up_ref[...]
    out_ref[:, 2 * width :] = down_ref[...]


def blocks_kernel(z_ref, rate_ref, input_ref, out_ref):
    units = rate_ref.shape[1]
    zero = jnp.zeros((units, units), bf16)
    for p in range(out_ref.shape[0]):
        for a in range(2):
            parts = [ref[2 * p + a].T for ref in (rate_ref, input_ref)]
            rows = []
            for k in range(4):
                row = []
                for part in parts:
                    one = jnp.zeros_like(zero)
                    for owner in range(4):
                        one = jnp.where(
                            (z_ref[0] ^ k) == owner, part[owner * units : (owner + 1) * units], one
                        )
                    row += [zero, one] if a else [one, zero]
                at = slice((2 * k + a) * units, (2 * k + a + 1) * units)
                out_ref[p, at, :] = jnp.concatenate(row, axis=1)


def land(pieces, w_ref, sems, first=0):
    copies, at = [], 0
    for n, piece in enumerate(pieces):
        rows = piece.shape[0]
        copy = pltpu.make_async_copy(piece, w_ref.at[pl.ds(at, rows)], sems.at[first + n])
        copy.start()
        copies.append((at, copy))
        at += rows
    return copies


def await_rows(copies, until):
    while copies and copies[0][0] < until:
        copies.pop(0)[1].wait()


def join_kernel(count, *refs):
    pieces, (first, second, sems) = refs[:-3], refs[-3:]
    copies = land(pieces[:count], first, sems) + land(pieces[count:], second, sems, count)
    for _, copy in copies:
        copy.wait()


def branches_kernel(nf_ref, taps_ref, bias_ref, mask_ref, *refs):
    pieces, (x_ref, y_ref, conv_ref, total_ref, w_ref, sems) = refs[:-6], refs[-6:]
    chan = x_ref.shape[1]
    step = w_ref.shape[0] // 4
    copies = land(pieces, w_ref, sems)
    for i in range(4):
        rows = slice(i * step, (i + 1) * step)
        await_rows(copies, (i + 1) * step)
        part = nn(nf_ref[:, rows], w_ref[rows, :])
        total_ref[...] = part if i == 0 else total_ref[...] + part
    both = total_ref[...]
    x_ref[...] = both[:, :chan]
    y_ref[...] = both[:, chan:]
    for c in range(0, chan, 128):
        cols = slice(c, c + 128)
        x = x_ref[:, cols]
        total = x * taps_ref[0:1, cols] + bias_ref[:, cols]
        for lag in range(1, taps_ref.shape[0]):
            total = total + down_rows(x, lag) * mask_ref[lag - 1] * taps_ref[lag : lag + 1, cols]
        conv_ref[:, cols] = total.astype(bf16)


def gates_of(rate, decay_logit, start):
    soft = softplus(-decay_logit)
    minus_log = 8.0 * rate * soft
    lost = one_less_exp(2.0 * minus_log)
    mult = jnp.where(start, 1.0, jnp.sqrt(lost))
    carried = jnp.where(start, 0.0, jnp.exp(-minus_log))
    return soft, mult, carried


def forward_scan_kernel(
    z_ref, c0, c1, c2, c3, block_ref, rb_ref, ib_ref, dl_ref, y_ref, mask_ref, w0, w1, w2, w3,
    rate_ref, entry_ref, hidden_ref, mixed_ref, o0, o1, o2, o3, total_ref,
):
    step, part = pl.program_id(0), w0.shape[0]
    start = mask_ref[0] == 0.0
    pre = nn(jnp.concatenate([c0[...], c1[...], c2[...], c3[...]], axis=1), block_ref[0])
    rate = sigmoid(pre[:, :128] + rb_ref[...])
    entry = sigmoid(pre[:, 128:] + ib_ref[...])
    _, mult, carried = gates_of(rate, dl_ref[...], start)
    driven = c0[...].astype(f32) * entry * mult
    hidden = scan_rows(carried, driven, down_rows)
    rate_ref[...] = rate
    entry_ref[...] = entry
    hidden_ref[...] = hidden
    mixed = (hidden * gelu_pair(y_ref[...])[0]).astype(bf16)
    mixed_ref[...] = mixed
    add_product(step, total_ref, mixed, [(k * part, w[...]) for k, w in enumerate((w0, w1, w2, w3))])

    @pl.when(step == pl.num_programs(0) - 1)
    def _():
        split_rows(z_ref, total_ref, (o0, o1, o2, o3))


def add_product(step, total_ref, left, sides):
    @pl.when(step == 0)
    def _():
        total_ref[...] = jnp.zeros_like(total_ref)

    for at, right in sides:
        total_ref[:, at : at + right.shape[0]] += nt(left, right)


def backward_scan_kernel(
    z_ref, p0, p1, p2, p3, w0, w1, w2, w3, c0, c1, c2, c3, block_ref, dl_ref, y_ref, mask_ref, rate_ref, entry_ref,
    hidden_ref,
    g_ref, gy_ref, direct_ref, h1_ref, h2_ref, h3_ref, mine_ref, theirs_ref, sums_ref,
):
    @pl.when(pl.program_id(0) == 0)
    def _():
        assemble_kernel(z_ref, p0, p1, p2, p3, g_ref)

    start = mask_ref[0] == 0.0
    part = w0.shape[0]
    grad_mixed = nn(g_ref[:, :part], w0[...])
    for k, w in enumerate((w1, w2, w3)):
        grad_mixed += nn(g_ref[:, (k + 1) * part : (k + 2) * part], w[...])
    hidden, rate, entry = hidden_ref[...], rate_ref[...], entry_ref[...]
    conv = c0[...].astype(f32)
    gelu_y, slope_y = gelu_pair(y_ref[...])
    gy_ref[...] = (grad_mixed * hidden * slope_y).astype(bf16)
    decay_logit = dl_ref[...]
    soft, mult, carried = gates_of(rate, decay_logit, start)
    state = scan_rows(up_rows(carried, 1), grad_mixed * gelu_y, up_rows)
    kept = carried * carried
    grad_log = jnp.where(
        start, 0.0, state * (down_rows(hidden, 1) * carried - conv * entry * kept / mult)
    )
    rate_low = (grad_log * (-8.0 * soft) * rate * (1.0 - rate)).astype(bf16)
    entry_low = (state * conv * mult * entry * (1.0 - entry)).astype(bf16)
    both = jnp.concatenate([rate_low, entry_low], axis=1)
    sums_ref[...] = jnp.concatenate(
        [
            jnp.sum(grad_log * rate, axis=0, keepdims=True) * (8.0 * sigmoid(-decay_logit)),
            jnp.sum(rate_low.astype(f32), axis=0, keepdims=True),
            jnp.sum(entry_low.astype(f32), axis=0, keepdims=True),
            jnp.zeros((5, 128), f32),
        ],
        axis=0,
    )
    heads = nt(both, block_ref[0])
    direct_ref[...] = state * entry * mult + heads[:, :128]
    h1_ref[...] = heads[:, 128:256].astype(bf16)
    h2_ref[...] = heads[:, 256:384]
    h3_ref[...] = heads[:, 384:].astype(bf16)
    units = jnp.concatenate([c0[...], c1[...], c2[...], c3[...]], axis=1)
    grads = tn(units, both)
    first = jnp.concatenate([grads[:, 0:64], grads[:, 128:192]], axis=1)
    second = jnp.concatenate([grads[:, 64:128], grads[:, 192:256]], axis=1)
    for k in range(4):
        even, odd = first[k * 128 : k * 128 + 64], second[k * 128 + 64 : k * 128 + 128]
        own = z_ref[1] % 2 == 0
        mine_ref[0, k] = jnp.where(own, even, odd).astype(bf16)
        theirs_ref[0, k] = jnp.where(own, odd, even).astype(bf16)


def conv_back_kernel(
    z_ref, direct_ref, r1, r2, x_ref, taps_ref, mask_ref, gy_ref, wx0, wx1, wy0, wy1,
    gx_ref, sums_ref, o0, o1, o2, o3, total_ref,
):
    step, half = pl.program_id(0), wx0.shape[0]
    total = direct_ref[...] + r1[...].astype(f32) + r2[...].astype(f32)
    x = x_ref[...]
    grad = total * taps_ref[0:1]
    sums = [jnp.sum(total * x, axis=0, keepdims=True)]
    for lag in range(1, taps_ref.shape[0]):
        kept = total * mask_ref[lag - 1]
        grad = grad + up_rows(kept, lag) * taps_ref[lag : lag + 1]
        sums.append(jnp.sum(kept * down_rows(x, lag), axis=0, keepdims=True))
    low = grad.astype(bf16)
    gx_ref[...] = low
    sums.append(jnp.sum(total, axis=0, keepdims=True))
    sums.append(jnp.zeros((8 - len(sums), x.shape[1]), f32))
    sums_ref[...] = jnp.concatenate(sums, axis=0)
    left = jnp.concatenate([low, gy_ref[...]], axis=1)
    first = jnp.concatenate([wx0[...], wy0[...]], axis=1)
    second = jnp.concatenate([wx1[...], wy1[...]], axis=1)
    add_product(step, total_ref, left, ((0, first), (half, second)))

    @pl.when(step == pl.num_programs(0) - 1)
    def _():
        split_rows(z_ref, total_ref, (o0, o1, o2, o3))


def split_rows(z_ref, total_ref, outs):
    rows = next(out for out in outs if out is not None).shape[0]
    for k, out in enumerate(outs):
        if out is None:
            continue
        at = pl.multiple_of((z_ref[0] ^ k) * rows, rows)
        out[...] = total_ref[pl.ds(at, rows), :].astype(out.dtype)


def assemble_kernel(z_ref, p0, p1, p2, p3, out_ref):
    rows = p0.shape[0]
    for k, piece in enumerate((p0, p1, p2, p3)):
        at = pl.multiple_of((z_ref[0] ^ k) * rows, rows)
        out_ref[pl.ds(at, rows), :] = piece[...].astype(out_ref.dtype)


def to_abs(me, size, v):
    part = v.shape[1] // size

    def picked(v, places):
        return jnp.concatenate([v[:, p * part : (p + 1) * part] for p in places], axis=1)

    v = picked(v, [(s % 2) * (size // 2) + s // 2 for s in range(size)])
    bit = 1
    while bit < size:
        v = jnp.where((me // bit) % 2 == 1, picked(v, [s ^ bit for s in range(size)]), v)
        bit *= 2
    return v


def to_rel(me, size, v):
    part = v.shape[1] // size

    def picked(v, places):
        return jnp.concatenate([v[:, p * part : (p + 1) * part] for p in places], axis=1)

    bit = 1
    while bit < size:
        v = jnp.where((me // bit) % 2 == 1, picked(v, [s ^ bit for s in range(size)]), v)
        bit *= 2
    return picked(v, [2 * j + c for c in range(2) for j in range(size // 2)])


def sum_pieces(pieces):
    total = pieces[0][...]
    for piece in pieces[1:]:
        total = total + piece[...].astype(f32)
    return total


def my_rows(z_ref, ref, rows):
    return ref[pl.ds(pl.multiple_of(z_ref[0] * rows, rows), rows), :].astype(f32)


def norm_second_kernel(z_ref, x_ref, gain_ref, o0, o1, o2, res_ref, low_ref):
    residual = my_rows(z_ref, x_ref, res_ref.shape[0]) + sum_pieces((o0, o1, o2))
    inv = lax.rsqrt(jnp.mean(residual * residual, axis=1, keepdims=True) + eps)
    res_ref[...] = residual
    low_ref[...] = (residual * inv * gain_ref[...]).astype(bf16)


def norm_back(x, gain, grad):
    inv = lax.rsqrt(jnp.mean(x * x, axis=1, keepdims=True) + eps)
    unit = x * inv
    scaled = grad * gain
    out = inv * (scaled - unit * jnp.mean(scaled * unit, axis=1, keepdims=True))
    return out, jnp.sum(grad * unit, axis=0, keepdims=True)


def second_back_kernel(size, z_ref, cot_ref, gain_ref, res_ref, o0, o1, o2, gr_ref, low_ref, gain_out):
    grad, gain_grad = norm_back(res_ref[...], gain_ref[...], sum_pieces((o0, o1, o2)))
    grad = grad + my_rows(z_ref, cot_ref, res_ref.shape[0])
    gr_ref[...] = grad
    low_ref[...] = grad.astype(bf16)
    gain_out[...] = to_abs(z_ref[1], size, gain_grad)


def first_back_kernel(size, z_ref, x_ref, gain_ref, gr_ref, o0, o1, o2, out_ref, gain_out):
    x = my_rows(z_ref, x_ref, gr_ref.shape[0])
    grad, gain_grad = norm_back(x, gain_ref[...], sum_pieces((o0, o1, o2)))
    out_ref[...] = to_abs(z_ref[1], size, gr_ref[...] + grad).astype(bf16)
    gain_out[...] = to_abs(z_ref[1], size, gain_grad)


def block_out_kernel(size, z_ref, res_ref, o0, o1, o2, out_ref):
    out_ref[...] = to_abs(z_ref[1], size, res_ref[...] + sum_pieces((o0, o1, o2))).astype(bf16)


def ffn_kernel(groups, first, last, *refs):
    refs = list(refs)

    def take(n):
        taken = refs[:n]
        del refs[:n]
        return taken

    (z_ref,) = take(1)
    if first:
        pieces = take(4)
    else:
        s_any, in_out, in_grad = take(3)
    (cot_any,) = take(1)
    s_ref, cot_ref, pre_ref, back_ref, w_ref, acc_out, acc_grad, sems, out_sems = refs[-9:]
    del refs[-9:]
    n_outs = 2 * groups + (7 if last else 2 + first)
    outs = refs[-n_outs:]
    del refs[-n_outs:]
    per = len(refs) // groups
    rows, width = w_ref.shape[1] // 4, back_ref.shape[1]
    copies = []

    def load(src, dst):
        copy = pltpu.make_async_copy(src, dst, sems.at[len(copies)])
        copy.start()
        copies.append(copy)
        return copy

    held = []
    if not first:
        held.append(load(s_any, s_ref))
    held.append(load(cot_any, cot_ref))
    landing = []
    for g in range(groups):
        at, marks = 0, []
        for piece in refs[g * per : (g + 1) * per]:
            marks.append((at, load(piece, w_ref.at[g, pl.ds(at, piece.shape[0])])))
            at += piece.shape[0]
        landing.append(marks)
    if not first:
        sums = [load(in_out, acc_out), load(in_grad, acc_grad)]
    if first:
        assemble_kernel(z_ref, *pieces, s_ref)
    for copy in held:
        copy.wait()
    stores = []

    def store(src, dst):
        copy = pltpu.make_async_copy(src, dst, out_sems.at[len(stores)])
        copy.start()
        stores.append(copy)

    if first:
        store(s_ref, outs[2 * groups])
    for g in range(groups):
        ggu_ref, mid_ref = outs[2 * g : 2 * g + 2]
        for i in range(4):
            at = slice(i * rows, (i + 1) * rows)
            await_rows(landing[g], (i + 1) * rows)
            pre = nn(s_ref[:, at], w_ref[g, at, : 2 * width])
            back = nn(cot_ref[:, at], w_ref[g, at, 2 * width :])
            if i == 0:
                pre_ref[...] = pre
                back_ref[...] = back
            else:
                pre_ref[...] += pre
                back_ref[...] += back
        for c in range(0, width, 128):
            gate, up = pre_ref[:, c : c + 128], pre_ref[:, width + c : width + c + 128]
            back = back_ref[:, c : c + 128]
            gelu_gate, slope = gelu_pair(gate)
            mid_ref[:, c : c + 128] = (gelu_gate * up).astype(bf16)
            ggu_ref[:, c : c + 128] = (back * up * slope).astype(bf16)
            ggu_ref[:, width + c : width + c + 128] = (back * gelu_gate).astype(bf16)
        if g == 0 and not first:
            for copy in sums:
                copy.wait()
        for i in range(4):
            at = slice(i * rows, (i + 1) * rows)
            grad = nt(ggu_ref[...], w_ref[g, at, : 2 * width])
            out = nt(mid_ref[...], w_ref[g, at, 2 * width :])
            if first and g == 0:
                acc_out[:, at] = out
                acc_grad[:, at] = grad
            else:
                acc_out[:, at] += out
                acc_grad[:, at] += grad
            if g == groups - 1 and not last:
                cols = pl.ds(i * rows, rows)
                store(acc_out.at[:, cols], outs[-2].at[:, cols])
                store(acc_grad.at[:, cols], outs[-1].at[:, cols])
    if last:
        out_parts, grad_parts = outs[2:5], outs[5:9]
        split_rows(z_ref, acc_grad, grad_parts)
        split_rows(z_ref, acc_out, [out_parts[0], None, out_parts[1], None])
        count = out_parts[0].shape[0]
        both = [out_parts[2].at[pl.ds(count, count)], out_parts[2].at[pl.ds(0, count)]]
        split_rows(z_ref, acc_out, [None, both[0], None, both[1]])
    for copy in stores:
        copy.wait()


def grads_out_kernel(sides, *refs):
    lefts, rights, out = refs[:sides], refs[sides : 2 * sides], refs[2 * sides]
    at = 0
    for left, right in zip(lefts, rights):
        width = right.shape[1]
        out[:, at : at + width] = tn(left[...], right[...]).astype(bf16)
        at += width


def grads_own_kernel(sides, room, *refs):
    lefts, rights = refs[:sides], refs[sides : 2 * sides]
    got, own, x_top, y_bot, send_x, send_y = refs[2 * sides :]
    at = 0
    q = x_top.shape[0]
    one, two = [slice((room + k) * q, (room + k + 1) * q) for k in range(2)]
    for left, right in zip(lefts, rights):
        half, width = left.shape[1], right.shape[1]
        cols = slice(at, at + width)
        at += width
        near = tn(left[:, : half // 2], right[...]) + got[: half // 2, cols].astype(f32)
        own[:, cols] = near[: 2 * q]
        x_top[:, cols] = near[2 * q : 3 * q]
        send_x[two, cols] = near[3 * q :].astype(bf16)
        far = tn(left[:, half // 2 :], right[...]) + got[half // 2 :, cols].astype(f32)
        send_y[two, cols] = far[:q].astype(bf16)
        y_bot[:, cols] = far[q : 2 * q]
        send_y[one, cols] = far[2 * q : 3 * q].astype(bf16)
        send_x[one, cols] = far[3 * q :].astype(bf16)


def relay_kernel(groups, has_next, *refs):
    refs = list(refs)
    out_x, out_y = refs[-2:]
    at = 0
    for _ in range(groups):
        x_top, y_bot, got_x, got_y = refs[:4]
        del refs[:4]
        q, cols = x_top.shape[0], slice(at, at + x_top.shape[1])
        out_x[:q, cols] = (x_top[...] + got_y[:, cols].astype(f32)).astype(bf16)
        out_y[:q, cols] = (y_bot[...] + got_x[:, cols].astype(f32)).astype(bf16)
        at += x_top.shape[1]
    at = 0
    for _ in range(has_next):
        send_x, send_y = refs[:2]
        del refs[:2]
        cols = slice(at, at + send_x.shape[1])
        out_x[q:, cols] = send_x[...]
        out_y[q:, cols] = send_y[...]
        at += send_x.shape[1]


def joined(own, got_x, got_y, last_x, last_y, at, cols):
    q = last_x.shape[0]
    top = own[:q, at] + got_y[:, cols].astype(f32) + last_x[:, cols].astype(f32)
    bottom = own[q:, at] + got_x[:, cols].astype(f32) + last_y[:, cols].astype(f32)
    return jnp.concatenate([top, bottom], axis=0)


def join_ffn_kernel(*refs):
    gate_ref, up_ref, down_ref = refs[-3:]
    for c in range(chunk_count):
        parts = refs[5 * c : 5 * c + 5]
        width = parts[0].shape[1] // 3
        at = slice(c * width, (c + 1) * width)
        gate, up, down = [slice(k * width, (k + 1) * width) for k in range(3)]
        gate_ref[:, at] = joined(*parts, gate, gate)
        up_ref[:, at] = joined(*parts, up, up)
        down_ref[:, at] = joined(*parts, down, down)


def add_kernel(a_ref, b_ref, out_ref):
    out_ref[...] = (a_ref[...].astype(f32) + b_ref[...].astype(f32)).astype(out_ref.dtype)


def gate_join_kernel(z_ref, mine_ref, other_ref, rate_ref, input_ref):
    pairs, _, units, _ = mine_ref.shape
    core = z_ref[1] % 2
    for src, head in ((mine_ref, core), (other_ref, 1 - core)):
        for p in range(pairs):
            whole = jnp.concatenate([src[p, z_ref[0] ^ owner] for owner in range(4)], axis=0)
            rate_ref[2 * p + head] = whole[:, :units].T
            input_ref[2 * p + head] = whole[:, units:].T


def relay_mixed_kernel(x_top, y_bot, got_x, got_y, send_x, send_y, out_x, out_y):
    q, width = x_top.shape[0], out_x.shape[1]
    for k in range(x_top.shape[1] // width):
        rows, cols = slice(k * q, (k + 1) * q), slice(k * width, (k + 1) * width)
        out_x[rows, :] = (x_top[:, cols] + got_y[:, cols].astype(f32)).astype(bf16)
        out_y[rows, :] = (y_bot[:, cols] + got_x[:, cols].astype(f32)).astype(bf16)
    out_x[(k + 1) * q :, :] = send_x[...]
    out_y[(k + 1) * q :, :] = send_y[...]


def join_yox_kernel(yo_own, x_own, yo_got_x, yo_got_y, y_x, y_y, o_x, o_y, x_got_x, x_got_y, x_x, x_y,
                    x_ref, y_ref, out_ref):
    width = x_ref.shape[0]
    first, second = slice(0, width), slice(width, 2 * width)
    y_ref[...] = joined(yo_own, yo_got_x[:, first], yo_got_y[:, first], y_x, y_y, first, first).T
    out_ref[...] = joined(
        yo_own, yo_got_x[:, second], yo_got_y[:, second], o_x, o_y, second, first
    ).T
    x_ref[...] = joined(x_own, x_got_x, x_got_y, x_x, x_y, first, first).T


def exchange(v, axis, size, bit):
    return lax.ppermute(v, axis, [(i, i ^ bit) for i in range(size)])


def tie(*values):
    return lax.optimization_barrier(values)


def along(size, bit, v):
    return exchange(v, "dp", 8, bit) if size == 8 else v


def move(size, send_x, send_y):
    return along(size, 2, send_x), along(size, 4, send_y)


def gather_all(shard, size):
    mine, bit = shard, 2
    while bit < size:
        mine = jnp.concatenate([mine, exchange(mine, "dp", size, bit)], axis=0)
        bit *= 2
    return [mine], [exchange(mine, "dp", size, 1)]


class Scatter:
    def __init__(self, size, lefts, rights, name):
        self.size, self.name = size, name
        self.lefts, self.rights = lefts, rights
        self.model = lefts[0].shape[1]
        self.width = sum(r.shape[1] for r in rights)

    def halves(self, side):
        tokens = self.lefts[0].shape[0]
        return {i: block((tokens, self.model // 2), 0, side) for i in range(len(self.lefts))}

    def sibling(self, run, micros=0):
        return run(
            partial(grads_out_kernel, len(self.lefts)),
            [like((self.model // 2, self.width), bf16)],
            *self.lefts, *self.rights, specs=self.halves(1), micros=micros,
            name="grads_out_" + self.name,
        )[0]

    def swap(self, out):
        return exchange(out, "dp", self.size, 1)

    def own(self, run, got, room=0):
        q, w = self.model // 16, self.width
        sends = [like(((2 + room) * q, w), bf16)] * 2
        return run(
            partial(grads_own_kernel, len(self.lefts), room),
            [like((2 * q, w), f32), like((q, w), f32), like((q, w), f32)] + sends,
            *self.lefts, *self.rights, got, specs=self.halves(0), name="grads_own_" + self.name,
        )

    def join(self, cut):
        own, x_top, y_bot, from_x, from_y = cut
        q = x_top.shape[0]
        from_x, from_y = from_x[-2 * q :], from_y[-2 * q :]
        total = jnp.concatenate(
            [own, x_top, from_x[q:].astype(f32), from_y[q:].astype(f32), y_bot,
             from_y[:q].astype(f32), from_x[:q].astype(f32)],
            axis=0,
        )
        bit = self.size // 2
        while bit > 1:
            half = total.shape[0] // 2
            total = total[:half] + exchange(total[half:].astype(bf16), "dp", self.size, bit).astype(f32)
            bit //= 2
        return total


def relay(run, cuts, got, base, nexts, name):
    q = cuts[0][1].shape[0]
    width = sum(cut[1].shape[1] for cut in cuts)
    ins, specs, options = [], {}, {}
    for cut in cuts:
        ins += [cut[1], cut[2]]
        for v in got:
            specs[len(ins)] = block((q, v.shape[1]), base, 0)
            ins.append(v)
    if len(nexts) == 1:
        options = dict(
            alias={len(ins): 0, len(ins) + 1: 1}, out_specs=[block((q, width), 0, 0)] * 2
        )
        specs[len(ins)] = specs[len(ins) + 1] = pl.BlockSpec(memory_space=pl.ANY)
    for cut in nexts:
        ins += [cut[3], cut[4]]
    return run(
        partial(relay_kernel, len(cuts), 0 if len(nexts) == 1 else len(nexts)),
        [like((3 * q if nexts else q, width), bf16)] * 2, *ins, specs=specs, name=name, **options,
    )


def to_owner(part):
    return exchange(part, "tensor", 4, 1)


def pass_on(part, got):
    return exchange((part + got.astype(f32)).astype(bf16), "tensor", 4, 2)


class Order:
    def __init__(self):
        self.last = None

    def after(self, *values):
        if self.last is not None:
            values, _ = lax.optimization_barrier((values, self.last))
        return values if len(values) > 1 else values[0]

    def wait(self, *values):
        values = self.after(*values)
        self.last = jax.tree.leaves(values)[0]
        return values

    def run(self, kernel, outs, *args, **options):
        results = call(kernel, outs, *self.after(*args), **options)
        self.last = results[0]
        return results


def spread(piece):
    return exchange(piece, "tensor", 4, 2), exchange(piece, "tensor", 4, 1)


def neighbour(v):
    return exchange(v, "tensor", 4, 1)


def sum_over(v, axis, size, first=1, until=None):
    bit = first
    while bit < (until or size):
        v = v + exchange(v, axis, size, bit)
        bit *= 2
    return v


def sum_low(v, axis, size, first=1, until=None):
    bit = first
    while bit < (until or size):
        low = v.astype(bf16)
        v = low.astype(f32) + exchange(low, axis, size, bit).astype(f32)
        bit *= 2
    return v


def body(
    tokens, segments, first_gain, x_weight, y_weight, conv_weight, conv_bias, rate_weight,
    input_weight, rate_bias, input_bias, decay_logit, out_weight, second_gain, gate_weight,
    up_weight, down_weight, cotangent, dp_size,
):
    count, model = tokens.shape
    heads, _, units = rate_weight.shape
    chan = heads * units
    pairs = heads // 2
    taps = conv_weight.shape[0]
    hidden_units = gate_weight.shape[1]
    width = hidden_units // chunk_count
    me = lax.axis_index("dp")
    z = lax.axis_index("tensor").astype(jnp.int32)
    ids = jnp.stack([z, me.astype(jnp.int32)])
    part = model // dp_size
    q = model // 16
    rows = count // 4
    size = dp_size
    order = Order()
    after, wait, run = order.after, order.wait, order.run
    anywhere = pl.BlockSpec(memory_space=pl.ANY)
    lane = pl.BlockSpec((count, 128), lambda p: (0, p))
    line = pl.BlockSpec((1, 128), lambda p: (0, p))
    sums_spec = pl.BlockSpec((8, 128), lambda p: (0, p))
    block_spec = pl.BlockSpec((1, 8 * units, 4 * units), lambda p: (p, 0, 0))
    mask_spec = pl.BlockSpec((taps - 1, count, 128), lambda p: (0, 0, 0))
    pair_grid = dict(
        grid=(pairs,), cost_estimate=hint,
        compiler_params=pltpu.CompilerParams(vmem_limit_bytes=60 * MIB),
    )
    split_shapes = [like((rows, model), t) for t in (f32, bf16, f32, bf16)]
    split_specs = [pl.BlockSpec((rows, model), lambda p: (0, 0))] * 4
    total_scratch = [pltpu.VMEM((count, model), f32)]

    out_block = pl.BlockSpec((model // 4, 128), lambda p: (0, p))

    def weight_block(at):
        return pl.BlockSpec((model // 2, 128), lambda p: (0, at * pairs + p))

    def sibling(v):
        return exchange(v, "dp", size, 1)

    def halves(by_x, by_y):
        half = by_x.shape[0] // 2
        lower, upper = move(size, by_y[half:], by_x[:half])
        return upper, lower

    def pieces_of(shard, *got):
        if size == 8:
            return [shard, *got[: len(got) // 2]], list(got[len(got) // 2 :])
        return gather_all(shard, size)

    def assemble(pieces, dtype, name):
        return run(
            assemble_kernel, [like((count, model), dtype)], ids, *pieces, scalars=1, name=name
        )[0]

    x_flat, y_flat = x_weight.reshape(part, chan), y_weight.reshape(part, chan)
    out_shard = out_weight.reshape(chan, part).T
    half = part // 2
    xy_t = jnp.concatenate([x_flat[:half], y_flat[:half]], axis=1)
    xy_b = jnp.concatenate([x_flat[half:], y_flat[half:]], axis=1)
    xt, yt = move(size, xy_t, xy_t)
    xb, yb = move(size, xy_b, xy_b)

    def ffn_shard(c):
        cols = block((part, width), 0, c)
        return run(
            shard_kernel, [like((part, 3 * width), bf16)], gate_weight, up_weight, down_weight.T,
            specs={0: cols, 1: cols, 2: cols}, name="shard",
        )[0]

    x_rel, nf, gain_one, gain_two = run(
        partial(norm_first_kernel, size),
        [like((count, model), bf16)] * 2 + [like((1, model), f32)] * 2,
        ids, tokens, first_gain.reshape(1, model), second_gain.reshape(1, model), scalars=1,
        name="norm_first",
    )
    f0, f1 = ffn_shard(0), ffn_shard(1)
    xt, xb, yt, yb, out_shard = wait(xt, xb, yt, yb, out_shard)

    top, bot = along(size, 4, xt), along(size, 2, yb)
    st, sb, sxt = sibling(xy_t), sibling(xy_b), sibling(xt)
    (cot_rel,) = run(
        partial(to_rel_kernel, size), [like((count, model), bf16)], ids, cotangent, scalars=1,
        name="cotangent",
    )
    segs = after(segments)
    masks = jnp.stack(
        [
            jnp.concatenate([jnp.full((lag,), -1, jnp.int32), segs[:-lag]]) == segs
            for lag in range(1, taps)
        ]
    ).astype(f32)
    masks = jnp.broadcast_to(masks[:, :, None], (taps - 1, count, 128))
    taps_flat = conv_weight.reshape(taps, chan)
    bias_flat = conv_bias.reshape(1, chan)
    rate_flat, input_flat = rate_bias.reshape(1, chan), input_bias.reshape(1, chan)
    decay_flat = decay_logit.reshape(1, chan)
    masks, taps_flat, bias_flat, rate_flat, input_flat, decay_flat, top, bot, st, sb, sxt = wait(
        masks, taps_flat, bias_flat, rate_flat, input_flat, decay_flat, top, bot, st, sb, sxt
    )
    sxb, syt, syb = sibling(after(xb)), sibling(after(yt)), sibling(after(yb))
    s_top, s_bot = sibling(top), sibling(bot)
    sxb, syt, syb, s_top, s_bot = wait(sxb, syt, syb, s_top, s_bot)
    out_x, out_y = move(size, out_shard, out_shard)
    if size == 8:
        own_w = [xy_t, xy_b, xt, xb, yt, yb, top, bot]
        sib_w = [st, sb, sxt, sxb, syt, syb, s_top, s_bot]
    else:
        own_w, sib_w = gather_all(jnp.concatenate([xy_t, xy_b], axis=0), size)
    all_w = own_w + sib_w
    x_branch, y_branch, conv_low = run(
        branches_kernel,
        [like((count, chan), f32), like((count, chan), f32), like((count, chan), bf16)],
        nf, taps_flat, bias_flat, masks, *all_w,
        specs={4 + i: anywhere for i in range(len(all_w))},
        scratch=[
            pltpu.VMEM((count, 2 * chan), f32),
            pltpu.VMEM((model, 2 * chan), bf16),
            pltpu.SemaphoreType.DMA((len(all_w),)),
        ],
        name="branches",
    )
    conv_low, out_x, out_y = wait(conv_low, out_x, out_y)
    conv2, conv1 = spread(conv_low)
    out_far = along(size, 2, out_y)
    f0_x, f0_y = move(size, *after(f0, f0))
    xy0, xy1 = run(
        partial(join_kernel, len(own_w)), [like((model // 2, 2 * chan), bf16)] * 2, *all_w,
        specs={i: anywhere for i in range(len(all_w))},
        scratch=[pltpu.SemaphoreType.DMA((len(all_w),))], name="join_xy",
    )
    (blocks,) = run(
        blocks_kernel, [like((pairs, 8 * units, 4 * units), bf16)], ids,
        rate_weight.transpose(0, 2, 1), input_weight.transpose(0, 2, 1),
        scalars=1, name="gate_blocks",
    )
    conv2, conv1, out_far = wait(conv2, conv1, out_far)
    conv3 = neighbour(conv2)
    if size == 8:
        pieces = [out_shard, out_x, out_y, out_far]
        outs = run(
            partial(join_kernel, 2), [like((model // 4, chan), bf16)] * 2, *pieces,
            specs={i: anywhere for i in range(4)}, scratch=[pltpu.SemaphoreType.DMA((4,))],
            name="join_out",
        )
    else:
        whole_out = gather_all(out_shard, size)[0][0]
        outs = [whole_out[: model // 4], whole_out[model // 4 :]]
    outs = [*outs, *[sibling(v) for v in outs]]
    conv3, f0_x, f0_y, outs = wait(conv3, f0_x, f0_y, outs)
    conv = [conv_low, conv1, conv2, conv3]
    f0_s, f1_s = [sibling(v) for v in after(f0, f1)]
    f1_x, f1_y = move(size, f1, after(f1))
    f0_sx = sibling(f0_x)
    rate, entry, hidden, mixed, *parts = pl.pallas_call(
        forward_scan_kernel,
        in_specs=[smem] + [lane] * 4 + [block_spec] + [line] * 3 + [lane, mask_spec]
        + [out_block] * 4,
        out_specs=[lane] * 4 + split_specs,
        out_shape=[like((count, chan), t) for t in (f32, f32, f32, bf16)] + split_shapes,
        scratch_shapes=total_scratch,
        name="forward_scan",
        **pair_grid,
    )(ids, *conv, blocks, rate_flat, input_flat, decay_flat, y_branch, masks, *outs)
    order.last = rate
    parts, f0_s, f1_s, f0_sx = wait(tuple(parts), f0_s, f1_s, f0_sx)
    got3 = to_owner(parts[3])
    f0_sy = sibling(after(f0_y))
    got3, f0_sy = wait(got3, f0_sy)
    got2, got1 = pass_on(parts[2], got3), to_owner(after(parts[1]))
    got2, got1, f1_x, f1_y = wait(got2, got1, f1_x, f1_y)
    f0_far, f1_far = along(size, 2, after(f0_y)), along(size, 4, f1_x)
    f1_sx, f1_sy = sibling(f1_x), sibling(f1_y)
    residual, second_rows = run(
        norm_second_kernel, [like((rows, model), f32), like((rows, model), bf16)],
        ids, x_rel, gain_two, parts[0], got1, got2, scalars=1, name="norm_second",
    )
    second_rows, f1_sx, f1_sy = wait(second_rows, f1_sx, f1_sy)
    sec2, sec1 = spread(second_rows)
    f2 = ffn_shard(2)
    sec2, sec1 = wait(sec2, sec1)
    sec3 = neighbour(sec2)
    sec3, f0_far, f1_far = wait(sec3, f0_far, f1_far)
    f2_x, f2_y = move(size, *after(f2, f2))
    f0_sf, f1_sf, f2_s = sibling(f0_far), sibling(f1_far), sibling(after(f2))
    f0_sf, f1_sf, f2_s = wait(f0_sf, f1_sf, f2_s)

    def ffn(left, groups, sums, first, last, name):
        outs = [like((count, 2 * width), bf16), like((count, width), bf16)] * len(groups)
        out_specs = [full(v) for v in outs]
        if first:
            outs.append(like((count, model), bf16))
            out_specs.append(anywhere)
        if last:
            more = [like((rows, model), f32)] * 2 + [like((2 * rows, model), bf16)] + split_shapes
            outs += more
            out_specs += [full(v) for v in more]
        else:
            outs += [like((count, model), f32)] * 2
            out_specs += [anywhere] * 2
        weights = sum([own + sib for own, sib in groups], [])
        scratch = [
            pltpu.VMEM((count, model), bf16),
            pltpu.VMEM((count, model), bf16),
            pltpu.VMEM((count, 2 * width), f32),
            pltpu.VMEM((count, width), f32),
            pltpu.VMEM((len(groups), model, 3 * width), bf16),
            pltpu.VMEM((count, model), f32),
            pltpu.VMEM((count, model), f32),
            pltpu.SemaphoreType.DMA((len(weights) + 4,)),
            pltpu.SemaphoreType.DMA((9,)),
        ]
        ins = [ids, *left, *sums, cot_rel, *weights]
        at = 1 + len(left) * first
        return run(
            partial(ffn_kernel, len(groups), first, last), outs, *ins, scalars=1, scratch=scratch,
            specs={i: anywhere for i in range(at, len(ins))}, out_specs=out_specs, name=name,
        )

    a, b, c, d, second, *sums = ffn(
        [second_rows, sec1, sec2, sec3],
        [
            pieces_of(f0, f0_x, f0_y, f0_far, f0_s, f0_sx, f0_sy, f0_sf),
            pieces_of(f1, f1_x, f1_y, f1_far, f1_s, f1_sx, f1_sy, f1_sf),
        ],
        [], True, False, "ffn_01",
    )
    s0 = Scatter(size, [second, cot_rel], [a, b], "ffn_0")
    s1 = Scatter(size, [second, cot_rel], [c, d], "ffn_1")
    s0_out = s0.sibling(run)
    s0_out, f2_x, f2_y = wait(s0_out, f2_x, f2_y)
    f2_top, f2_bot = halves(f2_x, f2_y)
    f2_sx, f2_sy = sibling(f2_x), sibling(f2_y)
    s0_swap = s0.swap(s0_out)
    s1_out = s1.sibling(run)
    f2_sx, f2_sy, s0_swap = wait(f2_sx, f2_sy, s0_swap)
    s0_cut = s0.own(run, s0_swap)
    f2_top, f2_bot, s0_send = wait(f2_top, f2_bot, tuple(s0_cut[3:]))
    f2_st, f2_sb = sibling(f2_top), sibling(f2_bot)
    f2_st, f2_sb = wait(f2_st, f2_sb)
    s0_got = move(size, *after(*s0_send))
    s1_swap = s1.swap(after(s1_out))
    a, b, *sums = ffn(
        [second],
        [pieces_of(f2, f2_x, f2_y, f2_top, f2_bot, f2_s, f2_sx, f2_sy, f2_st, f2_sb)], sums, False,
        True, "ffn_2",
    )
    s2 = Scatter(size, [second, cot_rel], [a, b], "ffn_2")
    out_parts, grad_parts, s1_swap = wait(tuple(sums[:3]), tuple(sums[3:]), s1_swap)

    got3, got1 = to_owner(grad_parts[3]), to_owner(grad_parts[1])
    s1_cut = s1.own(run, s1_swap, 1)
    s2_out = s2.sibling(run)
    got3, s0_got, s2_out = wait(got3, s0_got, s2_out)
    got2 = pass_on(grad_parts[2], got3)
    slot1 = move(size, *relay(run, [s0_cut], s0_got, 0, [s1_cut], "relay_0"))
    s2_swap = s2.swap(s2_out)
    got2, got1, s2_swap = wait(got2, got1, s2_swap)
    grad_res, rec_rows, second_gain = run(
        partial(second_back_kernel, size),
        [like((rows, model), f32), like((rows, model), bf16), like((1, model), f32)],
        ids, cot_rel, gain_two, residual, grad_parts[0], got1, got2, scalars=1, micros=6, name="second_back",
    )
    rec2, rec1 = spread(rec_rows)
    s2_cut = s2.own(run, s2_swap, 1)
    rec2, rec1 = wait(rec2, rec1)
    rec3 = neighbour(rec2)
    rec3, slot1 = wait(rec3, slot1)
    out_got = neighbour(after(out_parts[2]))
    slot2 = move(size, *relay(run, [s1_cut], slot1, 1, [s2_cut], "relay_1"))

    whole = pl.BlockSpec((count, model), lambda p: (0, 0))
    piece = pl.BlockSpec((rows, model), lambda p: (0, 0))
    gate_spec = pl.BlockSpec((1, 4, units, 2 * units), lambda p: (p, 0, 0, 0))
    gate_half = like((pairs, 4, units, 2 * units), bf16)
    grad_rec, grad_y, direct, h1, h2, h3, gate_mine, gate_theirs, scan_sums = pl.pallas_call(
        backward_scan_kernel,
        in_specs=[smem] + [piece] * 4 + [out_block] * 4 + [lane] * 4
        + [block_spec, line, lane, mask_spec] + [lane] * 3,
        out_specs=[whole, lane, lane, lane, lane, lane, gate_spec, gate_spec, sums_spec],
        out_shape=[like((count, model), bf16)]
        + [like((count, chan), t) for t in (bf16, f32, bf16, f32, bf16)]
        + [gate_half, gate_half, like((8, chan), f32)],
        name="backward_scan",
        **pair_grid,
    )(
        *after(ids, rec_rows, rec1, rec2, rec3, *outs, *conv, blocks, decay_flat, y_branch, masks),
        rate, entry, hidden,
    )
    order.last = grad_rec
    out_got, h1, h2, h3 = wait(out_got, h1, h2, h3)
    got3 = to_owner(h3)
    out_got2 = pass_on(out_parts[1], out_got[:rows])
    gate_got = sibling(gate_theirs)
    syo = Scatter(size, [nf, grad_rec], [grad_y, mixed], "yo")
    syo_out = syo.sibling(run)
    got3, syo_out, gate_got = wait(got3, syo_out, gate_got)
    got2, got1 = pass_on(h2, got3), to_owner(after(h1))
    (gate_sum,) = run(add_kernel, [gate_half], gate_mine, gate_got, name="gate_add")
    got2, got1, slot2, out_got2 = wait(got2, got1, slot2, out_got2)
    syo_swap = syo.swap(after(syo_out))
    gate_got = along(size, 2, after(gate_sum))
    grad_x, conv_sums, *first_parts = pl.pallas_call(
        conv_back_kernel,
        in_specs=[smem] + [lane] * 4 + [pl.BlockSpec((taps, 128), lambda p: (0, p)), mask_spec, lane]
        + [weight_block(0)] * 2 + [weight_block(1)] * 2,
        out_specs=[lane, sums_spec] + split_specs,
        out_shape=[like((count, chan), bf16), like((8, chan), f32)] + split_shapes,
        scratch_shapes=total_scratch,
        name="conv_back",
        **pair_grid,
    )(*after(ids, direct, got1, got2, x_branch, taps_flat, masks, grad_y, xy0, xy1, xy0, xy1))
    order.last = grad_x
    first_parts, syo_swap, gate_got = wait(tuple(first_parts), syo_swap, gate_got)
    got3 = to_owner(first_parts[3])
    sx = Scatter(size, [nf], [grad_x], "x")
    sx_out = sx.sibling(run)
    syo_cut = syo.own(run, syo_swap)
    got3, sx_out, yo_send = wait(got3, sx_out, tuple(syo_cut[3:]))
    got2, got1 = pass_on(first_parts[2], got3), to_owner(after(first_parts[1]))
    sx_swap = sx.swap(sx_out)
    yo_got = move(size, *yo_send)
    s2_send = relay(run, [s2_cut], slot2, 1, [], "relay_2")
    (block_rows,) = run(
        partial(block_out_kernel, size), [like((rows, model), bf16)],
        ids, residual, out_parts[0], out_got[rows:], out_got2, scalars=1, name="block_out",
    )
    (gate_sum2,) = run(add_kernel, [gate_half], gate_sum, gate_got, name="gate_add")
    got2, got1, sx_swap, yo_got = wait(got2, got1, sx_swap, yo_got)
    tokens_rows, first_gain_part = run(
        partial(first_back_kernel, size), [like((rows, model), bf16), like((1, model), f32)],
        ids, x_rel, gain_one, grad_res, first_parts[0], got1, got2, scalars=1, name="first_back",
    )
    tok2, tok1 = spread(tokens_rows)
    s2_last = move(size, *after(*s2_send))
    sx_cut = sx.own(run, sx_swap)
    specs = {k: block((q, 2 * chan), 0, 0) for k in (2, 3)}
    mixed_sends = run(
        relay_mixed_kernel, [like((4 * q, chan), bf16)] * 2, syo_cut[1], syo_cut[2], *yo_got,
        *sx_cut[3:], specs=specs, name="relay_3",
    )
    tok2, tok1, s2_last, mixed_sends = wait(tok2, tok1, s2_last, tuple(mixed_sends))
    tok3 = neighbour(tok2)
    slot3 = move(size, *mixed_sends)
    block2 = exchange(after(block_rows), "tensor", 4, 2)
    gains = jnp.concatenate([first_gain_part, second_gain], axis=0)
    gains = sum_over(after(gains), "tensor", 4, 1, 2)
    if size == 8:
        ins, specs = [], {}
        for cut, (got, base), last in (
            (s0_cut, (s0_got, 0), slot1), (s1_cut, (slot1, 1), slot2), (s2_cut, (slot2, 1), s2_last)
        ):
            ins.append(cut[0])
            for v, at in ((got[0], base + 1), (got[1], base + 1), (last[0], 0), (last[1], 0)):
                specs[len(ins)] = block((q, v.shape[1]), at, 0)
                ins.append(v)
        gate_share, up_share, down_share = run(
            join_ffn_kernel,
            [like((part, hidden_units), f32)] * 3,
            *ins, specs=specs, name="join_ffn",
        )
    else:
        shares = [s0.join(s0_cut), s1.join(s1_cut), s2.join(s2_cut)]
        gate_share, up_share, down_share = [
            jnp.concatenate([v[:, k * width : (k + 1) * width] for v in shares], axis=1)
            for k in range(3)
        ]
    tok3, gains, slot3, block2 = wait(tok3, gains, slot3, block2)
    x_last = move(size, *relay(run, [sx_cut], slot3, 2, [], "relay_4"))
    block1, block3 = neighbour(after(block_rows)), neighbour(block2)
    gains = sum_over(gains, "tensor", 4, 2)
    tokens_grad = assemble([tokens_rows, tok1, tok2, tok3], f32, "tokens_grad_all")
    gains, x_last = wait(gains, x_last)
    gate_got = along(size, 4, after(gate_sum2))
    small = jnp.concatenate([scan_sums, conv_sums, gains.reshape(8, chan)], axis=0)
    small = sum_over(small, "dp", size, 1, 2)
    small, gate_got = wait(small, gate_got)
    (gate_sum,) = run(
        add_kernel, [like(gate_half.shape, f32)], gate_sum2, gate_got, name="gate_add"
    )
    gate_got = sibling(gate_sum)
    if size == 8:
        by_x, by_y, across = [exchange(small, "dp", size, bit) for bit in (2, 4, 6)]
        ins = [syo_cut[0], sx_cut[0], *yo_got, *slot3, *slot3, *slot3, *x_last]
        specs = {2: block((q, 2 * chan), 1, 0), 3: block((q, 2 * chan), 1, 0)}
        for k, at in enumerate((0, 0, 1, 1, 3, 3, 0, 0)):
            specs[4 + k] = block((q, chan), at, 0)
        x_share, y_share, out_share = run(
            join_yox_kernel, [like((chan, part), f32)] * 3, *ins,
            specs=specs, name="join_yox",
        )
        gate_got = wait(gate_got)
        rate_grad, input_grad = run(
            gate_join_kernel, [like((heads, units, 4 * units), f32)] * 2, ids, gate_sum, gate_got,
            scalars=1, name="gate_join",
        )
        rate_grad, input_grad = rate_grad.transpose(0, 2, 1), input_grad.transpose(0, 2, 1)
        by_x, by_y, across = wait(by_x, by_y, across)
        small = (small + by_x) + (by_y + across)
    else:
        small = sum_over(small, "dp", size, 2)
        yo_share, x_share = syo.join(syo_cut), sx.join(sx_cut)
        x_share, y_share, out_share = x_share.T, yo_share[:, :chan].T, yo_share[:, chan:].T
        mine = sum_low(gate_mine + sibling(gate_theirs), "dp", size, 2)
        other, core = sibling(mine), me % 2
        gate_sum = jnp.stack(
            [jnp.where(core == 0, mine, other), jnp.where(core == 0, other, mine)], axis=1
        ).reshape(heads, 4, units, 2 * units)
        gate_sum = jnp.concatenate(
            [lax.dynamic_index_in_dim(gate_sum, z ^ k, 1, False) for k in range(4)], axis=1
        )
        rate_grad, input_grad = gate_sum[:, :, :units], gate_sum[:, :, units:]
    block1, block3 = wait(block1, block3)
    block_out = assemble([block_rows, block1, block2, block3], bf16, "block_out_all")
    x_share = x_share.reshape(heads, units, part).transpose(2, 0, 1)
    y_share = y_share.reshape(heads, units, part).transpose(2, 0, 1)
    gains = small[16:].reshape(2, model)
    return (
        block_out,
        tokens_grad,
        gains[0],
        x_share,
        y_share,
        small[8 : 8 + taps].reshape(taps, heads, units),
        small[8 + taps].reshape(heads, units),
        rate_grad,
        input_grad,
        small[1].reshape(heads, units),
        small[2].reshape(heads, units),
        small[0].reshape(heads, units),
        out_share.reshape(heads, units, part),
        gains[1],
        gate_share,
        up_share,
        down_share.T,
    )


def solution(mesh):
    return jax.shard_map(
        partial(body, dp_size=mesh.shape["dp"]),
        mesh=mesh,
        in_specs=(
            P("dp", None),
            P("dp"),
            P(),
            P("dp", None, "tensor"),
            P("dp", None, "tensor"),
            P(None, None, "tensor"),
            P(None, "tensor"),
            P(None, None, "tensor"),
            P(None, None, "tensor"),
            P(None, "tensor"),
            P(None, "tensor"),
            P(None, "tensor"),
            P(None, "tensor", "dp"),
            P(),
            P("dp", "tensor"),
            P("dp", "tensor"),
            P("tensor", "dp"),
            P("dp", None),
        ),
        out_specs=(
            P("dp", None),
            P("dp", None),
            P(),
            P("dp", None, "tensor"),
            P("dp", None, "tensor"),
            P(None, None, "tensor"),
            P(None, "tensor"),
            P(None, None, "tensor"),
            P(None, None, "tensor"),
            P(None, "tensor"),
            P(None, "tensor"),
            P(None, "tensor"),
            P(None, "tensor", "dp"),
            P(),
            P("dp", "tensor"),
            P("dp", "tensor"),
            P("tensor", "dp"),
        ),
        check_vma=False,
    )
```

time: 557 us -> 501 us (0.90)
  local copies, waits for them, and re-layouts: 96.4 us -> 24.7 us
  Pallas kernels: 162 us -> 208 us
  other arithmetic: 51.7 us -> 8.77 us
  starting transfers between devices: 68.3 us -> 88.1 us
  waiting for transfers between devices: 172 us -> 159 us
    pallas_call x23 -> x38, Pallas kernels: 140 us -> 177 us  [call(): pl.pallas_call(kernel, grid=(1,), out_shape=outs, in_specs=[smem] * scala...]
    unnamed x139 -> x164, local copies, waits for them, and re-layouts: 32.5 us -> 8.33 us
    ppermute x71 -> x100, starting transfers between devices: 68.3 us -> 88.1 us  [exchange(): return lax.ppermute(v, axis, [(i, i ^ bit) for i in range(size)])]
    concatenate x19 -> x3, other arithmetic: 19.4 us -> 0.09 us  [the longest x1 0.03 us: body(): xy_b = jnp.concatenate([x_flat[half:], y_flat[half:]], axis=1)]
    slice x15 -> x8, local copies, waits for them, and re-layouts: 18.4 us -> 3.9 us  [the longest x4 1.79 us: body(): xy_b = jnp.concatenate([x_flat[half:], y_flat[half:]], axis=1)]
    concatenate x11 -> x1, local copies, waits for them, and re-layouts: 13.7 us -> 0.01 us  [body(): jnp.concatenate([scan_sums, conv_sums, gains.reshape(8, chan)], axis=0)]
    ppermute x71 -> x100, waiting for transfers between devices: 172 us -> 159 us  [exchange(): return lax.ppermute(v, axis, [(i, i ^ bit) for i in range(size)])]
    convert_element_type x10 -> x1, other arithmetic: 11 us -> 0.01 us  [body(): masks = jnp.stack([jnp.concatenate([jnp.full((lag,), -1, jnp.int32), segs...]
  transfers between devices with their start and end apart: 71 -> 100, of which waited for: 28 -> 56; matrix products, arithmetic and copies ran while one was open for 20% -> 4% of each run, Pallas kernels for 29% -> 40%
where the time goes in v3:
time: 501 us; the launch traced here: 491 us
  Pallas kernels  208 us (42%)
  waiting for transfers between devices  159 us (32%)
  starting transfers between devices  88.1 us (18%)
  local copies, waits for them, and re-layouts  24.7 us (5%)
  other arithmetic  8.77 us (2%)
    pallas_call x38, Pallas kernels, call(): pl.pallas_call(kernel, grid=(1,), out_shape=outs, in_specs=[smem] * scala...  177 us
    ppermute x100, waiting for transfers between devices, exchange(): return lax.ppermute(v, axis, [(i, i ^ bit) for i in range(size)])  159 us
    ppermute x100, starting transfers between devices, exchange(): return lax.ppermute(v, axis, [(i, i ^ bit) for i in range(size)])  88.1 us
    pallas_call x1, Pallas kernels, body(): pl.pallas_call(forward_scan_kernel, in_specs=[smem] + [lane] * 4 + [block...  11.2 us
    pallas_call x1, Pallas kernels, body(): pl.pallas_call(backward_scan_kernel, in_specs=[smem] + [piece] * 4 + [out...  10.8 us
  transfers between devices with their start and end apart: 100, of which 56 were waited for; matrix products, arithmetic and copies ran while one was open for 4% of the time, Pallas kernels for 40%

profile of v3, /device:TPU:0, one launch (start us, length us, event | category | flops | bytes accessed | tf_op | source)
XLA Modules:
  0.0 491.2 jit_solution(16226982552744962866)
XLA Ops:
  2.6 3.0 collective-permute-start.2
  10.0 4.1 norm_first.1
  16.5 2.4 shard.4.refs_14_
  20.8 3.1 collective-permute-done.3.refs_5_
  30.6 3.4 cotangent.1.refs_5_.refs_1_.refs_4_.cot_ref
  35.4 3.4 collective-permute-done.4.refs_6_
  44.8 7.1 %branches.1 = (f32[256,640]{1,0:T(8,128)}, f32[256,640]{1,0:T(8,128)}, bf16[256,640]{1,0:T(8,128)(2,1)}) custom-call(bf16[256,2560]{1,0:T(8,128)(2,1)} %get-tuple-element.960.nf_ref.refs_0_, f32[4,640]{1,0:T(4,128)} %reshape.112.taps_ref, f32[1,640]{1,0:T(1,128)} %reshape.113.bias_ref, f32[3,256,128]{2,1,0:T(8,128)} %broadcast_in_dim.2.mask_ref, ...), custom_call_target="tpu_custom_call" | custom-call | flops 1 | bytes 1 | tf_op jit(solution)/shard_map/branches/pallas_call | solution.py:51
  58.4 2.6 collective-permute-start.16
  61.0 5.7 %join_xy.1 = (bf16[1280,1280]{1,0:T(8,128)(2,1)}, bf16[1280,1280]{1,0:T(8,128)(2,1)}) custom-call(bf16[160,1280]{1,0:T(8,128)(2,1)} %copy-done.10, bf16[160,1280]{1,0:T(8,128)(2,1)} %copy-done.11, bf16[160,1280]{1,0:T(8,128)(2,1)} %copy-done.21, bf16[160,1280]{1,0:T(8,128)(2,1)} %copy-done.23, bf16[160,1280]{1,0:T(8,128)(2,1)} %copy-done.20, ...), custom_call_target="tpu_custom_call" | custom-call | flops 1 | bytes 1 | tf_op jit(solution)/shard_map/join_xy/pallas_call | solution.py:51
  66.7 2.7 gate_blocks.1.block_ref
  71.7 2.4 collective-permute-done.16.c2
  74.9 2.6 join_out.1
  78.5 9.5 %collective-permute-done.19.c3 = bf16[256,640]{1,0:T(8,128)(2,1)S(1)} collective-permute-done((bf16[256,640]{1,0:T(8,128)(2,1)}, bf16[256,640]{1,0:T(8,128)(2,1)S(1)}, u32[]{:S(2)}, u32[]{:S(2)}) %collective-permute-start.19) | collective-permute-done | bytes 327712 | tf_op jit(solution)/shard_map/ppermute | solution.py:626
  87.9 3.0 collective-permute-done.20.refs_7_
  92.2 11.2 %forward_scan.1 = (f32[256,640]{1,0:T(8,128)}, f32[256,640]{1,0:T(8,128)}, f32[256,640]{1,0:T(8,128)}, bf16[256,640]{1,0:T(8,128)(2,1)}, f32[64,2560]{1,0:T(8,12...) custom-call(s32[2]{0:T(128)} %pad_add_fusion.z_ref.refs_0_, ...), custom_call_target="tpu_custom_call" | custom-call | flops 1 | bytes 1 | tf_op jit(solution)/shard_map/forward_scan/pallas_call | solution.py:929
  106.5 7.4 %collective-permute-done.27 = bf16[64,2560]{1,0:T(8,128)(2,1)S(1)} collective-permute-done((bf16[64,2560]{1,0:T(8,128)(2,1)}, bf16[64,2560]{1,0:T(8,128)(2,1)S(1)}, u32[]{:S(2)}, u32[]{:S(2)}) %collective-permute-start.27) | collective-permute-done | bytes 327712 | tf_op jit(solution)/shard_map/ppermute | solution.py:626
  116.6 2.6 collective-permute-start.29
  119.2 15.0 %collective-permute-done.31.refs_15_ = bf16[320,1920]{1,0:T(8,128)(2,1)S(1)} collective-permute-done((bf16[320,1920]{1,0:T(8,128)(2,1)S(1)}, bf16[320,1920]{1,0:T(8,128)(2,1)S(1)}, u32[]{:S(2)}, u32[]{:S(2)}) %collective-permute-start.31) | collective-permute-done | bytes 1228832 | tf_op jit(solution)/shard_map/ppermute | solution.py:626
  137.6 2.8 norm_second.1
  140.9 2.6 collective-permute-start.35
  145.9 10.8 %collective-permute-done.36.refs_2_ = bf16[64,2560]{1,0:T(8,128)(2,1)S(1)} collective-permute-done((bf16[64,2560]{1,0:T(8,128)(2,1)}, bf16[64,2560]{1,0:T(8,128)(2,1)S(1)}, u32[]{:S(2)}, u32[]{:S(2)}) %collective-permute-start.36) | collective-permute-done | bytes 327712 | tf_op jit(solution)/shard_map/ppermute | solution.py:626
  156.7 2.6 collective-permute-start.37
  159.3 5.1 %collective-permute-done.38.refs_9_ = bf16[320,1920]{1,0:T(8,128)(2,1)} collective-permute-done((bf16[320,1920]{1,0:T(8,128)(2,1)}, bf16[320,1920]{1,0:T(8,128)(2,1)}, u32[]{:S(2)}, u32[]{:S(2)}) %collective-permute-start.38) | collective-permute-done | bytes 1228832 | tf_op jit(solution)/shard_map/ppermute | solution.py:626
  172.4 20.9 %ffn_01.1 = (bf16[256,1280]{1,0:T(8,128)(2,1)}, bf16[256,640]{1,0:T(8,128)(2,1)}, bf16[256,1280]{1,0:T(8,128)(2,1)}, bf16[256,640]{1,0:T(8,128)(2,1)}, bf16[256,...) custom-call(s32[2]{0:T(128)} %pad_add_fusion.z_ref.refs_0_, ...), custom_call_target="tpu_custom_call" | custom-call | flops 1 | bytes 1 | tf_op jit(solution)/shard_map/ffn_01/pallas_call | solution.py:51
  193.3 5.3 %grads_out_ffn_0.1 = bf16[1280,1920]{1,0:T(8,128)(2,1)} custom-call(bf16[256,2560]{1,0:T(8,128)(2,1)} %get-tuple-element.820.refs_0_.refs_1_, bf16[256,2560]{1,0:T(8,128)(2,1)} %cotangent.1.refs_5_.refs_1_.refs_4_.cot_ref, bf16[256,1280]{1,0:T(8,128)(2,1)} %get-tuple-element.735.refs_2_, bf16[256,640]{1,0:T(8,128)(2,1)} %get-tuple-element.736.refs_3_), custom_call_target="tpu_custom_call" | custom-call | flops 1 | bytes 1 | tf_op jit(solution)/shard_map/grads_out_ffn_0/pallas_call | solution.py:51
  203.0 5.3 %grads_out_ffn_1.1 = bf16[1280,1920]{1,0:T(8,128)(2,1)} custom-call(bf16[256,2560]{1,0:T(8,128)(2,1)} %get-tuple-element.820.refs_0_.refs_1_, bf16[256,2560]{1,0:T(8,128)(2,1)} %cotangent.1.refs_5_.refs_1_.refs_4_.cot_ref, bf16[256,1280]{1,0:T(8,128)(2,1)} %get-tuple-element.784.refs_2_, bf16[256,640]{1,0:T(8,128)(2,1)} %get-tuple-element.785.refs_3_), custom_call_target="tpu_custom_call" | custom-call | flops 1 | bytes 1 | tf_op jit(solution)/shard_map/grads_out_ffn_1/pallas_call | solution.py:51
  210.7 7.3 %grads_own_ffn_0.1 = (f32[320,1920]{1,0:T(8,128)}, f32[160,1920]{1,0:T(8,128)}, f32[160,1920]{1,0:T(8,128)}, bf16[320,1920]{1,0:T(8,128)(2,1)}, bf16[320,1920]{1,0:T(8,128)(2,1)}) custom-call(bf16[256,2560]{1,0:T(8,128)(2,1)} %get-tuple-element.820.refs_0_.refs_1_, bf16[256,2560]{1,0:T(8,128)(2,1)} %cotangent.1.refs_5_.refs_1_.refs_4_.cot_ref, ...), custom_call_target="tpu_custom_call" | custom-call | flops 1 | bytes 1 | tf_op jit(solution)/shard_map/grads_own_ffn_0/pallas_call | solution.py:51
  223.7 13.0 %ffn_2.1 = (bf16[256,1280]{1,0:T(8,128)(2,1)}, bf16[256,640]{1,0:T(8,128)(2,1)}, f32[64,2560]{1,0:T(8,128)}, f32[64,2560]{1,0:T(8,128)}, bf16[128,2560]{1,0:T(8,...) custom-call(s32[2]{0:T(128)} %pad_add_fusion.z_ref.refs_0_, ...), custom_call_target="tpu_custom_call" | custom-call | flops 1 | bytes 1 | tf_op jit(solution)/shard_map/ffn_2/pallas_call | solution.py:51
  238.6 7.8 %grads_own_ffn_1.1 = (f32[320,1920]{1,0:T(8,128)}, f32[160,1920]{1,0:T(8,128)}, f32[160,1920]{1,0:T(8,128)}, bf16[480,1920]{1,0:T(8,128)(2,1)}, bf16[480,1920]{1,0:T(8,128)(2,1)}) custom-call(bf16[256,2560]{1,0:T(8,128)(2,1)} %get-tuple-element.820.refs_0_.refs_1_, bf16[256,2560]{1,0:T(8,128)(2,1)} %cotangent.1.refs_5_.refs_1_.refs_4_.cot_ref, ...), custom_call_target="tpu_custom_call" | custom-call | flops 1 | bytes 1 | tf_op jit(solution)/shard_map/grads_own_ffn_1/pallas_call | solution.py:51
  246.4 5.3 %grads_out_ffn_2.1 = bf16[1280,1920]{1,0:T(8,128)(2,1)} custom-call(bf16[256,2560]{1,0:T(8,128)(2,1)} %get-tuple-element.820.refs_0_.refs_1_, bf16[256,2560]{1,0:T(8,128)(2,1)} %cotangent.1.refs_5_.refs_1_.refs_4_.cot_ref, bf16[256,1280]{1,0:T(8,128)(2,1)} %get-tuple-element.822.refs_2_, bf16[256,640]{1,0:T(8,128)(2,1)} %get-tuple-element.823.refs_3_), custom_call_target="tpu_custom_call" | custom-call | flops 1 | bytes 1 | tf_op jit(solution)/shard_map/grads_out_ffn_2/pallas_call | solution.py:51
  253.2 3.1 relay_0.1
  260.9 2.5 collective-permute-start.56
  263.4 10.6 %collective-permute-done.57.o1 = bf16[64,2560]{1,0:T(8,128)(2,1)} collective-permute-done((bf16[64,2560]{1,0:T(8,128)(2,1)}, bf16[64,2560]{1,0:T(8,128)(2,1)}, u32[]{:S(2)}, u32[]{:S(2)}) %collective-permute-start.57) | collective-permute-done | bytes 327712 | tf_op jit(solution)/shard_map/ppermute | solution.py:626
  274.0 3.2 collective-permute-done.56.o2
  277.9 3.4 second_back.1
  281.4 3.4 collective-permute-start.59
  284.8 7.8 %grads_own_ffn_2.1 = (f32[320,1920]{1,0:T(8,128)}, f32[160,1920]{1,0:T(8,128)}, f32[160,1920]{1,0:T(8,128)}, bf16[480,1920]{1,0:T(8,128)(2,1)}, bf16[480,1920]{1,0:T(8,128)(2,1)}) custom-call(bf16[256,2560]{1,0:T(8,128)(2,1)} %get-tuple-element.820.refs_0_.refs_1_, bf16[256,2560]{1,0:T(8,128)(2,1)} %cotangent.1.refs_5_.refs_1_.refs_4_.cot_ref, ...), custom_call_target="tpu_custom_call" | custom-call | flops 1 | bytes 1 | tf_op jit(solution)/shard_map/grads_own_ffn_2/pallas_call | solution.py:51
  294.0 3.7 collective-permute-done.59.p2
  299.2 8.3 %collective-permute-done.61.p3 = bf16[64,2560]{1,0:T(8,128)(2,1)} collective-permute-done((bf16[64,2560]{1,0:T(8,128)(2,1)}, bf16[64,2560]{1,0:T(8,128)(2,1)}, u32[]{:S(2)}, u32[]{:S(2)}) %collective-permute-start.61) | collective-permute-done | bytes 327712 | tf_op jit(solution)/shard_map/ppermute | solution.py:626
  307.5 3.1 relay_1.1
  312.5 10.8 %backward_scan.1 = (bf16[256,2560]{1,0:T(8,128)(2,1)}, bf16[256,640]{1,0:T(8,128)(2,1)}, f32[256,640]{1,0:T(8,128)}, bf16[256,640]{1,0:T(8,128)(2,1)}, f32[256,6...) custom-call(s32[2]{0:T(128)} %pad_add_fusion.z_ref.refs_0_, ...), custom_call_target="tpu_custom_call" | custom-call | flops 1 | bytes 1 | tf_op jit(solution)/shard_map/backward_scan/pallas_call | solution.py:1050
  328.5 4.4 grads_out_yo.1
  332.9 4.5 collective-permute-done.65
  339.3 5.1 %collective-permute-start.67 = (bf16[256,640]{1,0:T(8,128)(2,1)}, bf16[256,640]{1,0:T(8,128)(2,1)}, u32[]{:S(2)}, u32[]{:S(2)}) collective-permute-start(bf16[256,640]{1,0:T(8,128)(2,1)} %add_convert_fusion.2), channel_id=1, source_target_pairs={{0,2},{1,3},{2,0},{3,1},{4,6},{5,7},{6,4},{7,5},{8,10},{9,11},{10,... | collective-permute-start | bytes 983048 | tf_op jit(solution)/shard_map/ppermute | solution.py:626
  346.3 12.5 %collective-permute-done.68.r1 = bf16[256,640]{1,0:T(8,128)(2,1)} collective-permute-done((bf16[256,640]{1,0:T(8,128)(2,1)}, bf16[256,640]{1,0:T(8,128)(2,1)}, u32[]{:S(2)}, u32[]{:S(2)}) %collective-permute-start.68) | collective-permute-done | bytes 327712 | tf_op jit(solution)/shard_map/ppermute | solution.py:626
  360.9 9.1 %conv_back.1 = (bf16[256,640]{1,0:T(8,128)(2,1)}, f32[8,640]{1,0:T(8,128)}, f32[64,2560]{1,0:T(8,128)}, bf16[64,2560]{1,0:T(8,128)(2,1)}, f32[64,2560]{1,0:T(8,128)}, /*index=5*/bf16[64,2560]{1,0:T(8,128)(2,1)}) custom-call(s32[2]{0:T(128)} %pad_add_fusion.z_ref.refs_0_, f32[256,640]{1,0:T(8,128)} %get-tuple-element.896.direct_ref, ...), custom_call_target="tpu_custom_call" | custom-call | flops 1 | bytes 1 | tf_op jit(solution)/shard_map/conv_back/pallas_call | solution.py:1077
  370.2 3.1 grads_out_x.1
  373.2 5.8 %grads_own_yo.1 = (f32[320,1280]{1,0:T(8,128)}, f32[160,1280]{1,0:T(8,128)}, f32[160,1280]{1,0:T(8,128)}, bf16[320,1280]{1,0:T(8,128)(2,1)}, bf16[320,1280]{1,0:T(8,128)(2,1)}) custom-call(bf16[256,2560]{1,0:T(8,128)(2,1)} %get-tuple-element.960.nf_ref.refs_0_, bf16[256,2560]{1,0:T(8,128)(2,1)} %get-tuple-element.921.refs_1_, ...), custom_call_target="tpu_custom_call" | custom-call | flops 1 | bytes 1 | tf_op jit(solution)/shard_map/grads_own_yo/pallas_call | solution.py:51
  388.0 3.1 relay_2.1
  391.1 2.5 block_out.1.p0
  395.4 4.5 collective-permute-done.76.o1
  400.0 3.2 collective-permute-done.75.o2
  403.9 3.8 first_back.1
  412.0 3.6 grads_own_x.1
  415.7 3.2 relay_3.1
  418.9 4.4 collective-permute-done.81.p1
  423.3 2.8 collective-permute-done.80.p2
  430.8 8.6 %join_ffn.1 = (f32[320,1920]{1,0:T(8,128)}, f32[320,1920]{1,0:T(8,128)}, f32[320,1920]{1,0:T(8,128)}) custom-call(f32[320,1920]{1,0:T(8,128)} %get-tuple-element.992.refs_0_, bf16[320,1920]{1,0:T(8,128)(2,1)} %copy-done.8, bf16[320,1920]{1,0:T(8,128)(2,1)} %copy-done.9, bf16[480,1920]{1,0:T(8,128)(2,1)} %copy-done.1, bf16[480,1920]{1,0:T(8,128)(2,1)} %copy-done, ...), custom_call_target="tpu_custom_call" | custom-call | flops 1 | bytes 1 | tf_op jit(solution)/shard_map/join_ffn/pallas_call | solution.py:51
  450.3 2.9 tokens_grad_all.1
  456.5 4.7 collective-permute-done.95.b_ref
  468.2 4.3 join_yox.1
  473.7 3.4 gate_join.1
  478.0 5.7 %collective-permute-done.90.p3 = bf16[64,2560]{1,0:T(8,128)(2,1)S(1)} collective-permute-done((bf16[64,2560]{1,0:T(8,128)(2,1)}, bf16[64,2560]{1,0:T(8,128)(2,1)S(1)}, u32[]{:S(2)}, u32[]{:S(2)}) %collective-permute-start.90) | collective-permute-done | bytes 327712 | tf_op jit(solution)/shard_map/ppermute | solution.py:626
  488.3 2.4 block_out_all.1
  (388 shorter events, 141.5 us)
Async XLA Ops:
  2.6 17.6 %collective-permute-start.2 = (bf16[160,1280]{1,0:T(8,128)(2,1)S(1)}, bf16[160,1280]{1,0:T(8,128)(2,1)S(1)}, u32[]{:S(2)}, u32[]{:S(2)}) collective-permute-start(bf16[160,1280]{1,0:T(8,128)(2,1)S(1)} %pad_maximum_fusion.refs_0_), channel_id=1, source_target_pairs={{0,16},{4,20},{8,24},{12,28},{16,0},{20,4},{24,8},{28,12},{1,17},{... | collective-permute-start | bytes 1228808 | tf_op jit(solution)/shard_map/ppermute | solution.py:626
  5.6 15.2 %collective-permute-start = (bf16[160,1280]{1,0:T(8,128)(2,1)S(1)}, bf16[160,1280]{1,0:T(8,128)(2,1)S(1)}, u32[]{:S(2)}, u32[]{:S(2)}) collective-permute-start(bf16[160,1280]{1,0:T(8,128)(2,1)S(1)} %pad_maximum_fusion.refs_0_), channel_id=1, source_target_pairs={{0,8},{4,12},{8,0},{12,4},{16,24},{20,28},{24,16},{28,20},{1,9},{5... | collective-permute-start | bytes 1228808 | tf_op jit(solution)/shard_map/ppermute | solution.py:626
  7.5 16.4 %collective-permute-start.3 = (bf16[160,1280]{1,0:T(8,128)(2,1)S(1)}, bf16[160,1280]{1,0:T(8,128)(2,1)S(1)}, u32[]{:S(2)}, u32[]{:S(2)}) collective-permute-start(bf16[160,1280]{1,0:T(8,128)(2,1)S(1)} %pad_maximum_fusion.1.refs_1_), channel_id=1, source_target_pairs={{0,16},{4,20},{8,24},{12,28},{16,0},{20,4},{24,8},{28,12},{1,17},{... | collective-permute-start | bytes 1228808 | tf_op jit(solution)/shard_map/ppermute | solution.py:626
  8.0 17.2 %collective-permute-start.1 = (bf16[160,1280]{1,0:T(8,128)(2,1)S(1)}, bf16[160,1280]{1,0:T(8,128)(2,1)S(1)}, u32[]{:S(2)}, u32[]{:S(2)}) collective-permute-start(bf16[160,1280]{1,0:T(8,128)(2,1)S(1)} %pad_maximum_fusion.1.refs_1_), channel_id=1, source_target_pairs={{0,8},{4,12},{8,0},{12,4},{16,24},{20,28},{24,16},{28,20},{1,9},{5... | collective-permute-start | bytes 1228808 | tf_op jit(solution)/shard_map/ppermute | solution.py:626
  8.1 26.0 %collective-permute-start.6 = (bf16[160,1280]{1,0:T(8,128)(2,1)S(1)}, bf16[160,1280]{1,0:T(8,128)(2,1)S(1)}, u32[]{:S(2)}, u32[]{:S(2)}) collective-permute-start(bf16[160,1280]{1,0:T(8,128)(2,1)S(1)} %pad_maximum_fusion.refs_0_), channel_id=1, source_target_pairs={{0,4},{4,0},{8,12},{12,8},{16,20},{20,16},{24,28},{28,24},{1,5},{5... | collective-permute-start | bytes 1228808 | tf_op jit(solution)/shard_map/ppermute | solution.py:626
  20.2 14.0 %collective-permute-start.7 = (bf16[160,1280]{1,0:T(8,128)(2,1)S(1)}, bf16[160,1280]{1,0:T(8,128)(2,1)}, u32[]{:S(2)}, u32[]{:S(2)}) collective-permute-start(bf16[160,1280]{1,0:T(8,128)(2,1)S(1)} %pad_maximum_fusion.1.refs_1_), channel_id=1, source_target_pairs={{0,4},{4,0},{8,12},{12,8},{16,20},{20,16},{24,28},{28,24},{1,5},{5... | collective-permute-start | bytes 1228808 | tf_op jit(solution)/shard_map/ppermute | solution.py:626
  26.8 12.0 %collective-permute-start.4 = (bf16[160,1280]{1,0:T(8,128)(2,1)S(1)}, bf16[160,1280]{1,0:T(8,128)(2,1)}, u32[]{:S(2)}, u32[]{:S(2)}) collective-permute-start(bf16[160,1280]{1,0:T(8,128)(2,1)S(1)} %collective-permute-done.refs_2_), channel_id=1, source_target_pairs={{0,16},{4,20},{8,24},{12,28},{16,0},{20,4},{24,8},{28,12},{1,17},{... | collective-permute-start | bytes 1228808 | tf_op jit(solution)/shard_map/ppermute | solution.py:626
  41.4 11.6 %collective-permute-start.15 = (bf16[320,640]{1,0:T(8,128)(2,1)S(1)}, bf16[320,640]{1,0:T(8,128)(2,1)}, u32[]{:S(2)}, u32[]{:S(2)}) collective-permute-start(bf16[320,640]{1,0:T(8,128)(2,1)S(1)} %bitcast.27), channel_id=1, source_target_pairs={{0,16},{4,20},{8,24},{12,28},{16,0},{20,4},{24,8},{28,12},{1,17},{... | collective-permute-start | bytes 1228808 | tf_op jit(solution)/shard_map/ppermute | solution.py:626
  53.5 20.5 %collective-permute-start.18 = (bf16[320,640]{1,0:T(8,128)(2,1)}, bf16[320,640]{1,0:T(8,128)(2,1)S(1)}, u32[]{:S(2)}, u32[]{:S(2)}) collective-permute-start(bf16[320,640]{1,0:T(8,128)(2,1)} %collective-permute-done.15.refs_2_), channel_id=1, source_target_pairs={{0,8},{4,12},{8,0},{12,4},{16,24},{20,28},{24,16},{28,20},{1,9},{5... | collective-permute-start | bytes 1228808 | tf_op jit(solution)/shard_map/ppermute | solution.py:626
  54.1 36.9 %collective-permute-start.20 = (bf16[320,1920]{1,0:T(8,128)(2,1)S(1)}, bf16[320,1920]{1,0:T(8,128)(2,1)}, u32[]{:S(2)}, u32[]{:S(2)}) collective-permute-start(bf16[320,1920]{1,0:T(8,128)(2,1)S(1)} %copy-done.6), channel_id=1, source_target_pairs={{0,8},{4,12},{8,0},{12,4},{16,24},{20,28},{24,16},{28,20},{1,9},{5... | collective-permute-start | bytes 3686408 | tf_op jit(solution)/shard_map/ppermute | solution.py:626
  55.6 35.4 %collective-permute-start.21 = (bf16[320,1920]{1,0:T(8,128)(2,1)S(1)}, bf16[320,1920]{1,0:T(8,128)(2,1)}, u32[]{:S(2)}, u32[]{:S(2)}) collective-permute-start(bf16[320,1920]{1,0:T(8,128)(2,1)S(1)} %copy-done.6), channel_id=1, source_target_pairs={{0,16},{4,20},{8,24},{12,28},{16,0},{20,4},{24,8},{28,12},{1,17},{... | collective-permute-start | bytes 3686408 | tf_op jit(solution)/shard_map/ppermute | solution.py:626
  56.8 14.9 %collective-permute-start.17 = (bf16[256,640]{1,0:T(8,128)(2,1)}, bf16[256,640]{1,0:T(8,128)(2,1)S(1)}, u32[]{:S(2)}, u32[]{:S(2)}) collective-permute-start(bf16[256,640]{1,0:T(8,128)(2,1)} %get-tuple-element.853.c0), channel_id=1, source_target_pairs={{0,1},{1,0},{2,3},{3,2},{4,5},{5,4},{6,7},{7,6},{8,9},{9,8},{10,11... | collective-permute-start | bytes 983048 | tf_op jit(solution)/shard_map/ppermute | solution.py:626
  58.4 15.7 %collective-permute-start.16 = (bf16[256,640]{1,0:T(8,128)(2,1)}, bf16[256,640]{1,0:T(8,128)(2,1)S(1)}, u32[]{:S(2)}, u32[]{:S(2)}) collective-permute-start(bf16[256,640]{1,0:T(8,128)(2,1)} %get-tuple-element.853.c0), channel_id=1, source_target_pairs={{0,2},{1,3},{2,0},{3,1},{4,6},{5,7},{6,4},{7,5},{8,10},{9,11},{10,... | collective-permute-start | bytes 983048 | tf_op jit(solution)/shard_map/ppermute | solution.py:626
  77.4 13.5 %collective-permute-start.22 = (bf16[640,640]{1,0:T(8,128)(2,1)}, bf16[640,640]{1,0:T(8,128)(2,1)S(1)}, u32[]{:S(2)}, u32[]{:S(2)}) collective-permute-start(bf16[640,640]{1,0:T(8,128)(2,1)} %get-tuple-element.849.w0), channel_id=1, source_target_pairs={{0,4},{4,0},{8,12},{12,8},{16,20},{20,16},{24,28},{28,24},{1,5},{5... | collective-permute-start | bytes 2457608 | tf_op jit(solution)/shard_map/ppermute | solution.py:626
  77.5 13.5 %collective-permute-start.23 = (bf16[640,640]{1,0:T(8,128)(2,1)}, bf16[640,640]{1,0:T(8,128)(2,1)S(1)}, u32[]{:S(2)}, u32[]{:S(2)}) collective-permute-start(bf16[640,640]{1,0:T(8,128)(2,1)} %get-tuple-element.850.w1), channel_id=1, source_target_pairs={{0,4},{4,0},{8,12},{12,8},{16,20},{20,16},{24,28},{28,24},{1,5},{5... | collective-permute-start | bytes 2457608 | tf_op jit(solution)/shard_map/ppermute | solution.py:626
  91.0 12.4 %collective-permute-start.24 = (bf16[320,1920]{1,0:T(8,128)(2,1)S(1)}, bf16[320,1920]{1,0:T(8,128)(2,1)}, u32[]{:S(2)}, u32[]{:S(2)}) collective-permute-start(bf16[320,1920]{1,0:T(8,128)(2,1)S(1)} %copy-done.6), channel_id=1, source_target_pairs={{0,4},{4,0},{8,12},{12,8},{16,20},{20,16},{24,28},{28,24},{1,5},{5... | collective-permute-start | bytes 3686408 | tf_op jit(solution)/shard_map/ppermute | solution.py:626
  91.1 12.3 %collective-permute-start.25 = (bf16[320,1920]{1,0:T(8,128)(2,1)S(1)}, bf16[320,1920]{1,0:T(8,128)(2,1)}, u32[]{:S(2)}, u32[]{:S(2)}) collective-permute-start(bf16[320,1920]{1,0:T(8,128)(2,1)S(1)} %copy-done.7), channel_id=1, source_target_pairs={{0,4},{4,0},{8,12},{12,8},{16,20},{20,16},{24,28},{28,24},{1,5},{5... | collective-permute-start | bytes 3686408 | tf_op jit(solution)/shard_map/ppermute | solution.py:626
  91.6 11.8 %collective-permute-start.26 = (bf16[320,1920]{1,0:T(8,128)(2,1)}, bf16[320,1920]{1,0:T(8,128)(2,1)}, u32[]{:S(2)}, u32[]{:S(2)}) collective-permute-start(bf16[320,1920]{1,0:T(8,128)(2,1)} %collective-permute-done.20.refs_7_), channel_id=1, source_target_pairs={{0,4},{4,0},{8,12},{12,8},{16,20},{20,16},{24,28},{28,24},{1,5},{5... | collective-permute-start | bytes 3686408 | tf_op jit(solution)/shard_map/ppermute | solution.py:626
  105.1 29.1 %collective-permute-start.31 = (bf16[320,1920]{1,0:T(8,128)(2,1)S(1)}, bf16[320,1920]{1,0:T(8,128)(2,1)S(1)}, u32[]{:S(2)}, u32[]{:S(2)}) collective-permute-start(bf16[320,1920]{1,0:T(8,128)(2,1)S(1)} %copy-done.7), channel_id=1, source_target_pairs={{0,8},{4,12},{8,0},{12,4},{16,24},{20,28},{24,16},{28,20},{1,9},{5... | collective-permute-start | bytes 3686408 | tf_op jit(solution)/shard_map/ppermute | solution.py:626
  105.7 28.8 %collective-permute-start.32 = (bf16[320,1920]{1,0:T(8,128)(2,1)S(1)}, bf16[320,1920]{1,0:T(8,128)(2,1)S(1)}, u32[]{:S(2)}, u32[]{:S(2)}) collective-permute-start(bf16[320,1920]{1,0:T(8,128)(2,1)S(1)} %copy-done.7), channel_id=1, source_target_pairs={{0,16},{4,20},{8,24},{12,28},{16,0},{20,4},{24,8},{28,12},{1,17},{... | collective-permute-start | bytes 3686408 | tf_op jit(solution)/shard_map/ppermute | solution.py:626
  115.0 19.5 %collective-permute-start.30 = (bf16[64,2560]{1,0:T(8,128)(2,1)S(1)}, bf16[64,2560]{1,0:T(8,128)(2,1)S(1)}, u32[]{:S(2)}, u32[]{:S(2)}) collective-permute-start(bf16[64,2560]{1,0:T(8,128)(2,1)S(1)} %copy-done.79), channel_id=1, source_target_pairs={{0,1},{1,0},{2,3},{3,2},{4,5},{5,4},{6,7},{7,6},{8,9},{9,8},{10,11... | collective-permute-start | bytes 983048 | tf_op jit(solution)/shard_map/ppermute | solution.py:626
  116.6 17.9 %collective-permute-start.29 = (bf16[64,2560]{1,0:T(8,128)(2,1)S(1)}, bf16[64,2560]{1,0:T(8,128)(2,1)S(1)}, u32[]{:S(2)}, u32[]{:S(2)}) collective-permute-start(bf16[64,2560]{1,0:T(8,128)(2,1)S(1)} %add_convert_fusion.4), channel_id=1, source_target_pairs={{0,2},{1,3},{2,0},{3,1},{4,6},{5,7},{6,4},{7,5},{8,10},{9,11},{10,... | collective-permute-start | bytes 983048 | tf_op jit(solution)/shard_map/ppermute | solution.py:626
  135.5 28.9 %collective-permute-start.38 = (bf16[320,1920]{1,0:T(8,128)(2,1)}, bf16[320,1920]{1,0:T(8,128)(2,1)}, u32[]{:S(2)}, u32[]{:S(2)}) collective-permute-start(bf16[320,1920]{1,0:T(8,128)(2,1)} %collective-permute-done.21.refs_8_), channel_id=1, source_target_pairs={{0,8},{4,12},{8,0},{12,4},{16,24},{20,28},{24,16},{28,20},{1,9},{5... | collective-permute-start | bytes 3686408 | tf_op jit(solution)/shard_map/ppermute | solution.py:626
  136.8 28.7 %collective-permute-start.39 = (bf16[320,1920]{1,0:T(8,128)(2,1)S(1)}, bf16[320,1920]{1,0:T(8,128)(2,1)}, u32[]{:S(2)}, u32[]{:S(2)}) collective-permute-start(bf16[320,1920]{1,0:T(8,128)(2,1)S(1)} %collective-permute-done.31.refs_15_), channel_id=1, source_target_pairs={{0,16},{4,20},{8,24},{12,28},{16,0},{20,4},{24,8},{28,12},{1,17},{... | collective-permute-start | bytes 3686408 | tf_op jit(solution)/shard_map/ppermute | solution.py:626
  140.4 16.3 %collective-permute-start.36 = (bf16[64,2560]{1,0:T(8,128)(2,1)}, bf16[64,2560]{1,0:T(8,128)(2,1)S(1)}, u32[]{:S(2)}, u32[]{:S(2)}) collective-permute-start(bf16[64,2560]{1,0:T(8,128)(2,1)} %get-tuple-element.690.refs_1_), channel_id=1, source_target_pairs={{0,1},{1,0},{2,3},{3,2},{4,5},{5,4},{6,7},{7,6},{8,9},{9,8},{10,11... | collective-permute-start | bytes 983048 | tf_op jit(solution)/shard_map/ppermute | solution.py:626
  140.9 15.8 %collective-permute-start.35 = (bf16[64,2560]{1,0:T(8,128)(2,1)}, bf16[64,2560]{1,0:T(8,128)(2,1)S(1)}, u32[]{:S(2)}, u32[]{:S(2)}) collective-permute-start(bf16[64,2560]{1,0:T(8,128)(2,1)} %get-tuple-element.690.refs_1_), channel_id=1, source_target_pairs={{0,2},{1,3},{2,0},{3,1},{4,6},{5,7},{6,4},{7,5},{8,10},{9,11},{10,... | collective-permute-start | bytes 983048 | tf_op jit(solution)/shard_map/ppermute | solution.py:626
  166.3 32.2 %collective-permute-start.43 = (bf16[320,1920]{1,0:T(8,128)(2,1)}, bf16[320,1920]{1,0:T(8,128)(2,1)S(1)}, u32[]{:S(2)}, u32[]{:S(2)}) collective-permute-start(bf16[320,1920]{1,0:T(8,128)(2,1)} %shard.5.refs_5_), channel_id=1, source_target_pairs={{0,8},{4,12},{8,0},{12,4},{16,24},{20,28},{24,16},{28,20},{1,9},{5... | collective-permute-start | bytes 3686408 | tf_op jit(solution)/shard_map/ppermute | solution.py:626
  168.0 30.6 %collective-permute-start.44 = (bf16[320,1920]{1,0:T(8,128)(2,1)}, bf16[320,1920]{1,0:T(8,128)(2,1)S(1)}, u32[]{:S(2)}, u32[]{:S(2)}) collective-permute-start(bf16[320,1920]{1,0:T(8,128)(2,1)} %shard.5.refs_5_), channel_id=1, source_target_pairs={{0,16},{4,20},{8,24},{12,28},{16,0},{20,4},{24,8},{28,12},{1,17},{... | collective-permute-start | bytes 3686408 | tf_op jit(solution)/shard_map/ppermute | solution.py:626
  198.6 12.1 %collective-permute-start.49 = (bf16[1280,1920]{1,0:T(8,128)(2,1)}, bf16[1280,1920]{1,0:T(8,128)(2,1)}, u32[]{:S(2)}, u32[]{:S(2)}) collective-permute-start(bf16[1280,1920]{1,0:T(8,128)(2,1)} %grads_out_ffn_0.1), channel_id=1, source_target_pairs={{0,4},{4,0},{8,12},{12,8},{16,20},{20,16},{24,28},{28,24},{1,5},{5... | collective-permute-start | bytes 14745608 | tf_op jit(solution)/shard_map/ppermute | solution.py:626
  201.0 17.0 %collective-permute-start.46 = (bf16[160,1920]{1,0:T(8,128)(2,1)}, bf16[160,1920]{1,0:T(8,128)(2,1)}, u32[]{:S(2)}, u32[]{:S(2)}) collective-permute-start(bf16[160,1920]{1,0:T(8,128)(2,1)} %slice.83), channel_id=1, source_target_pairs={{0,8},{4,12},{8,0},{12,4},{16,24},{20,28},{24,16},{28,20},{1,9},{5... | collective-permute-start | bytes 1843208 | tf_op jit(solution)/shard_map/ppermute | solution.py:626
  202.7 16.1 %collective-permute-start.45 = (bf16[160,1920]{1,0:T(8,128)(2,1)}, bf16[160,1920]{1,0:T(8,128)(2,1)}, u32[]{:S(2)}, u32[]{:S(2)}) collective-permute-start(bf16[160,1920]{1,0:T(8,128)(2,1)} %slice.82), channel_id=1, source_target_pairs={{0,16},{4,20},{8,24},{12,28},{16,0},{20,4},{24,8},{28,12},{1,17},{... | collective-permute-start | bytes 1843208 | tf_op jit(solution)/shard_map/ppermute | solution.py:626
  222.0 14.8 %collective-permute-start.52 = (bf16[1280,1920]{1,0:T(8,128)(2,1)}, bf16[1280,1920]{1,0:T(8,128)(2,1)}, u32[]{:S(2)}, u32[]{:S(2)}) collective-permute-start(bf16[1280,1920]{1,0:T(8,128)(2,1)} %grads_out_ffn_1.1), channel_id=1, source_target_pairs={{0,4},{4,0},{8,12},{12,8},{16,20},{20,16},{24,28},{28,24},{1,5},{5... | collective-permute-start | bytes 14745608 | tf_op jit(solution)/shard_map/ppermute | solution.py:626
  222.1 29.6 %collective-permute-start.54 = (bf16[320,1920]{1,0:T(8,128)(2,1)}, bf16[320,1920]{1,0:T(8,128)(2,1)S(1)}, u32[]{:S(2)}, u32[]{:S(2)}) collective-permute-start(bf16[320,1920]{1,0:T(8,128)(2,1)} %get-tuple-element.778), channel_id=1, source_target_pairs={{0,8},{4,12},{8,0},{12,4},{16,24},{20,28},{24,16},{28,20},{1,9},{5... | collective-permute-start | bytes 3686408 | tf_op jit(solution)/shard_map/ppermute | solution.py:626
  223.0 29.2 %collective-permute-start.55 = (bf16[320,1920]{1,0:T(8,128)(2,1)}, bf16[320,1920]{1,0:T(8,128)(2,1)S(1)}, u32[]{:S(2)}, u32[]{:S(2)}) collective-permute-start(bf16[320,1920]{1,0:T(8,128)(2,1)} %get-tuple-element.779), channel_id=1, source_target_pairs={{0,16},{4,20},{8,24},{12,28},{16,0},{20,4},{24,8},{28,12},{1,17},{... | collective-permute-start | bytes 3686408 | tf_op jit(solution)/shard_map/ppermute | solution.py:626
  236.8 15.5 %collective-permute-start.53 = (bf16[64,2560]{1,0:T(8,128)(2,1)}, bf16[64,2560]{1,0:T(8,128)(2,1)S(1)}, u32[]{:S(2)}, u32[]{:S(2)}) collective-permute-start(bf16[64,2560]{1,0:T(8,128)(2,1)} %get-tuple-element.775), channel_id=1, source_target_pairs={{0,1},{1,0},{2,3},{3,2},{4,5},{5,4},{6,7},{7,6},{8,9},{9,8},{10,11... | collective-permute-start | bytes 983048 | tf_op jit(solution)/shard_map/ppermute | solution.py:626
  252.2 24.9 %collective-permute-start.58 = (bf16[1280,1920]{1,0:T(8,128)(2,1)}, bf16[1280,1920]{1,0:T(8,128)(2,1)}, u32[]{:S(2)}, u32[]{:S(2)}) collective-permute-start(bf16[1280,1920]{1,0:T(8,128)(2,1)} %grads_out_ffn_2.1), channel_id=1, source_target_pairs={{0,4},{4,0},{8,12},{12,8},{16,20},{20,16},{24,28},{28,24},{1,5},{5... | collective-permute-start | bytes 14745608 | tf_op jit(solution)/shard_map/ppermute | solution.py:626
  256.4 41.8 %collective-permute-start.63 = (bf16[480,1920]{1,0:T(8,128)(2,1)}, bf16[480,1920]{1,0:T(8,128)(2,1)S(1)}, u32[]{:S(2)}, u32[]{:S(2)}) collective-permute-start(bf16[480,1920]{1,0:T(8,128)(2,1)} %get-tuple-element.827), channel_id=1, source_target_pairs={{0,16},{4,20},{8,24},{12,28},{16,0},{20,4},{24,8},{28,12},{1,17},{... | collective-permute-start | bytes 5529608 | tf_op jit(solution)/shard_map/ppermute | solution.py:626
  257.6 41.5 %collective-permute-start.62 = (bf16[480,1920]{1,0:T(8,128)(2,1)}, bf16[480,1920]{1,0:T(8,128)(2,1)S(1)}, u32[]{:S(2)}, u32[]{:S(2)}) collective-permute-start(bf16[480,1920]{1,0:T(8,128)(2,1)} %get-tuple-element.807), channel_id=1, source_target_pairs={{0,8},{4,12},{8,0},{12,4},{16,24},{20,28},{24,16},{28,20},{1,9},{5... | collective-permute-start | bytes 5529608 | tf_op jit(solution)/shard_map/ppermute | solution.py:626
  258.7 15.2 %collective-permute-start.57 = (bf16[64,2560]{1,0:T(8,128)(2,1)}, bf16[64,2560]{1,0:T(8,128)(2,1)}, u32[]{:S(2)}, u32[]{:S(2)}) collective-permute-start(bf16[64,2560]{1,0:T(8,128)(2,1)} %get-tuple-element.793), channel_id=1, source_target_pairs={{0,1},{1,0},{2,3},{3,2},{4,5},{5,4},{6,7},{7,6},{8,9},{9,8},{10,11... | collective-permute-start | bytes 983048 | tf_op jit(solution)/shard_map/ppermute | solution.py:626
  260.9 16.3 %collective-permute-start.56 = (bf16[64,2560]{1,0:T(8,128)(2,1)S(1)}, bf16[64,2560]{1,0:T(8,128)(2,1)S(1)}, u32[]{:S(2)}, u32[]{:S(2)}) collective-permute-start(bf16[64,2560]{1,0:T(8,128)(2,1)S(1)} %add_convert_fusion.3), channel_id=1, source_target_pairs={{0,2},{1,3},{2,0},{3,1},{4,6},{5,7},{6,4},{7,5},{8,10},{9,11},{10,... | collective-permute-start | bytes 983048 | tf_op jit(solution)/shard_map/ppermute | solution.py:626
  281.3 12.7 %collective-permute-start.60 = (bf16[64,2560]{1,0:T(8,128)(2,1)}, bf16[64,2560]{1,0:T(8,128)(2,1)S(1)}, u32[]{:S(2)}, u32[]{:S(2)}) collective-permute-start(bf16[64,2560]{1,0:T(8,128)(2,1)} %get-tuple-element.845.p0), channel_id=1, source_target_pairs={{0,1},{1,0},{2,3},{3,2},{4,5},{5,4},{6,7},{7,6},{8,9},{9,8},{10,11... | collective-permute-start | bytes 983048 | tf_op jit(solution)/shard_map/ppermute | solution.py:626
  281.4 16.4 %collective-permute-start.59 = (bf16[64,2560]{1,0:T(8,128)(2,1)}, bf16[64,2560]{1,0:T(8,128)(2,1)}, u32[]{:S(2)}, u32[]{:S(2)}) collective-permute-start(bf16[64,2560]{1,0:T(8,128)(2,1)} %get-tuple-element.845.p0), channel_id=1, source_target_pairs={{0,2},{1,3},{2,0},{3,1},{4,6},{5,7},{6,4},{7,5},{8,10},{9,11},{10,... | collective-permute-start | bytes 983048 | tf_op jit(solution)/shard_map/ppermute | solution.py:626
  307.5 15.9 %collective-permute-start.64 = (bf16[128,2560]{1,0:T(8,128)(2,1)}, bf16[128,2560]{1,0:T(8,128)(2,1)}, u32[]{:S(2)}, u32[]{:S(2)}) collective-permute-start(bf16[128,2560]{1,0:T(8,128)(2,1)} %get-tuple-element.829), channel_id=1, source_target_pairs={{0,1},{1,0},{2,3},{3,2},{4,5},{5,4},{6,7},{7,6},{8,9},{9,8},{10,11... | collective-permute-start | bytes 1966088 | tf_op jit(solution)/shard_map/ppermute | solution.py:626
  310.7 48.9 %collective-permute-start.70 = (bf16[480,1920]{1,0:T(8,128)(2,1)}, bf16[480,1920]{1,0:T(8,128)(2,1)S(1)}, u32[]{:S(2)}, u32[]{:S(2)}) collective-permute-start(bf16[480,1920]{1,0:T(8,128)(2,1)} %get-tuple-element.880), channel_id=1, source_target_pairs={{0,16},{4,20},{8,24},{12,28},{16,0},{20,4},{24,8},{28,12},{1,17},{... | collective-permute-start | bytes 5529608 | tf_op jit(solution)/shard_map/ppermute | solution.py:626
  311.6 48.0 %collective-permute-start.69 = (bf16[480,1920]{1,0:T(8,128)(2,1)}, bf16[480,1920]{1,0:T(8,128)(2,1)S(1)}, u32[]{:S(2)}, u32[]{:S(2)}) collective-permute-start(bf16[480,1920]{1,0:T(8,128)(2,1)} %get-tuple-element.843), channel_id=1, source_target_pairs={{0,8},{4,12},{8,0},{12,4},{16,24},{20,28},{24,16},{28,20},{1,9},{5... | collective-permute-start | bytes 5529608 | tf_op jit(solution)/shard_map/ppermute | solution.py:626
  323.4 13.9 %collective-permute-start.65 = (bf16[256,640]{1,0:T(8,128)(2,1)}, bf16[256,640]{1,0:T(8,128)(2,1)}, u32[]{:S(2)}, u32[]{:S(2)}) collective-permute-start(bf16[256,640]{1,0:T(8,128)(2,1)} %get-tuple-element.869), channel_id=1, source_target_pairs={{0,1},{1,0},{2,3},{3,2},{4,5},{5,4},{6,7},{7,6},{8,9},{9,8},{10,11... | collective-permute-start | bytes 983048 | tf_op jit(solution)/shard_map/ppermute | solution.py:626
  327.4 18.8 %collective-permute-start.71 = (bf16[64,2560]{1,0:T(8,128)(2,1)}, bf16[64,2560]{1,0:T(8,128)(2,1)S(1)}, u32[]{:S(2)}, u32[]{:S(2)}) collective-permute-start(bf16[64,2560]{1,0:T(8,128)(2,1)} %add_convert_fusion.1), channel_id=1, source_target_pairs={{0,2},{1,3},{2,0},{3,1},{4,6},{5,7},{6,4},{7,5},{8,10},{9,11},{10,... | collective-permute-start | bytes 983048 | tf_op jit(solution)/shard_map/ppermute | solution.py:626
  339.3 19.5 %collective-permute-start.68 = (bf16[256,640]{1,0:T(8,128)(2,1)}, bf16[256,640]{1,0:T(8,128)(2,1)}, u32[]{:S(2)}, u32[]{:S(2)}) collective-permute-start(bf16[256,640]{1,0:T(8,128)(2,1)} %get-tuple-element.879), channel_id=1, source_target_pairs={{0,1},{1,0},{2,3},{3,2},{4,5},{5,4},{6,7},{7,6},{8,9},{9,8},{10,11... | collective-permute-start | bytes 983048 | tf_op jit(solution)/shard_map/ppermute | solution.py:626
  339.3 20.3 %collective-permute-start.67 = (bf16[256,640]{1,0:T(8,128)(2,1)}, bf16[256,640]{1,0:T(8,128)(2,1)}, u32[]{:S(2)}, u32[]{:S(2)}) collective-permute-start(bf16[256,640]{1,0:T(8,128)(2,1)} %add_convert_fusion.2), channel_id=1, source_target_pairs={{0,2},{1,3},{2,0},{3,1},{4,6},{5,7},{6,4},{7,5},{8,10},{9,11},{10,... | collective-permute-start | bytes 983048 | tf_op jit(solution)/shard_map/ppermute | solution.py:626
  380.9 22.3 %collective-permute-start.77 = (bf16[1280,640]{1,0:T(8,128)(2,1)}, bf16[1280,640]{1,0:T(8,128)(2,1)S(1)}, u32[]{:S(2)}, u32[]{:S(2)}) collective-permute-start(bf16[1280,640]{1,0:T(8,128)(2,1)} %grads_out_x.1), channel_id=1, source_target_pairs={{0,4},{4,0},{8,12},{12,8},{16,20},{20,16},{24,28},{28,24},{1,5},{5... | collective-permute-start | bytes 4915208 | tf_op jit(solution)/shard_map/ppermute | solution.py:626
  380.9 22.3 %collective-permute-start.78 = (bf16[320,1280]{1,0:T(8,128)(2,1)}, bf16[320,1280]{1,0:T(8,128)(2,1)S(1)}, u32[]{:S(2)}, u32[]{:S(2)}) collective-permute-start(bf16[320,1280]{1,0:T(8,128)(2,1)} %get-tuple-element.943), channel_id=1, source_target_pairs={{0,8},{4,12},{8,0},{12,4},{16,24},{20,28},{24,16},{28,20},{1,9},{5... | collective-permute-start | bytes 2457608 | tf_op jit(solution)/shard_map/ppermute | solution.py:626
  381.8 21.4 %collective-permute-start.79 = (bf16[320,1280]{1,0:T(8,128)(2,1)}, bf16[320,1280]{1,0:T(8,128)(2,1)S(1)}, u32[]{:S(2)}, u32[]{:S(2)}) collective-permute-start(bf16[320,1280]{1,0:T(8,128)(2,1)} %get-tuple-element.944), channel_id=1, source_target_pairs={{0,16},{4,20},{8,24},{12,28},{16,0},{20,4},{24,8},{28,12},{1,17},{... | collective-permute-start | bytes 2457608 | tf_op jit(solution)/shard_map/ppermute | solution.py:626
  384.6 15.4 %collective-permute-start.76 = (bf16[64,2560]{1,0:T(8,128)(2,1)}, bf16[64,2560]{1,0:T(8,128)(2,1)S(1)}, u32[]{:S(2)}, u32[]{:S(2)}) collective-permute-start(bf16[64,2560]{1,0:T(8,128)(2,1)} %get-tuple-element.941), channel_id=1, source_target_pairs={{0,1},{1,0},{2,3},{3,2},{4,5},{5,4},{6,7},{7,6},{8,9},{9,8},{10,11... | collective-permute-start | bytes 983048 | tf_op jit(solution)/shard_map/ppermute | solution.py:626
  385.7 17.5 %collective-permute-start.75 = (bf16[64,2560]{1,0:T(8,128)(2,1)}, bf16[64,2560]{1,0:T(8,128)(2,1)S(1)}, u32[]{:S(2)}, u32[]{:S(2)}) collective-permute-start(bf16[64,2560]{1,0:T(8,128)(2,1)} %add_convert_fusion), channel_id=1, source_target_pairs={{0,2},{1,3},{2,0},{3,1},{4,6},{5,7},{6,4},{7,5},{8,10},{9,11},{10,... | collective-permute-start | bytes 983048 | tf_op jit(solution)/shard_map/ppermute | solution.py:626
  407.7 18.4 %collective-permute-start.82 = (bf16[160,1920]{1,0:T(8,128)(2,1)}, bf16[160,1920]{1,0:T(8,128)(2,1)S(1)}, u32[]{:S(2)}, u32[]{:S(2)}) collective-permute-start(bf16[160,1920]{1,0:T(8,128)(2,1)} %get-tuple-element.966), channel_id=1, source_target_pairs={{0,8},{4,12},{8,0},{12,4},{16,24},{20,28},{24,16},{28,20},{1,9},{5... | collective-permute-start | bytes 1843208 | tf_op jit(solution)/shard_map/ppermute | solution.py:626
  408.7 17.4 %collective-permute-start.83 = (bf16[160,1920]{1,0:T(8,128)(2,1)}, bf16[160,1920]{1,0:T(8,128)(2,1)S(1)}, u32[]{:S(2)}, u32[]{:S(2)}) collective-permute-start(bf16[160,1920]{1,0:T(8,128)(2,1)} %get-tuple-element.967), channel_id=1, source_target_pairs={{0,16},{4,20},{8,24},{12,28},{16,0},{20,4},{24,8},{28,12},{1,17},{... | collective-permute-start | bytes 1843208 | tf_op jit(solution)/shard_map/ppermute | solution.py:626
  409.7 13.6 %collective-permute-start.81 = (bf16[64,2560]{1,0:T(8,128)(2,1)}, bf16[64,2560]{1,0:T(8,128)(2,1)S(1)}, u32[]{:S(2)}, u32[]{:S(2)}) collective-permute-start(bf16[64,2560]{1,0:T(8,128)(2,1)} %get-tuple-element.1024.p0), channel_id=1, source_target_pairs={{0,1},{1,0},{2,3},{3,2},{4,5},{5,4},{6,7},{7,6},{8,9},{9,8},{10,11... | collective-permute-start | bytes 983048 | tf_op jit(solution)/shard_map/ppermute | solution.py:626
  409.7 16.4 %collective-permute-start.80 = (bf16[64,2560]{1,0:T(8,128)(2,1)}, bf16[64,2560]{1,0:T(8,128)(2,1)S(1)}, u32[]{:S(2)}, u32[]{:S(2)}) collective-permute-start(bf16[64,2560]{1,0:T(8,128)(2,1)} %get-tuple-element.1024.p0), channel_id=1, source_target_pairs={{0,2},{1,3},{2,0},{3,1},{4,6},{5,7},{6,4},{7,5},{8,10},{9,11},{10,... | collective-permute-start | bytes 983048 | tf_op jit(solution)/shard_map/ppermute | solution.py:626
  426.1 16.6 %collective-permute-start.86 = (bf16[640,640]{1,0:T(8,128)(2,1)}, bf16[640,640]{1,0:T(8,128)(2,1)S(1)}, u32[]{:S(2)}, u32[]{:S(2)}) collective-permute-start(bf16[640,640]{1,0:T(8,128)(2,1)} %get-tuple-element.987), channel_id=1, source_target_pairs={{0,8},{4,12},{8,0},{12,4},{16,24},{20,28},{24,16},{28,20},{1,9},{5... | collective-permute-start | bytes 2457608 | tf_op jit(solution)/shard_map/ppermute | solution.py:626
  427.3 16.1 %collective-permute-start.87 = (bf16[640,640]{1,0:T(8,128)(2,1)}, bf16[640,640]{1,0:T(8,128)(2,1)S(1)}, u32[]{:S(2)}, u32[]{:S(2)}) collective-permute-start(bf16[640,640]{1,0:T(8,128)(2,1)} %get-tuple-element.988), channel_id=1, source_target_pairs={{0,16},{4,20},{8,24},{12,28},{16,0},{20,4},{24,8},{28,12},{1,17},{... | collective-permute-start | bytes 2457608 | tf_op jit(solution)/shard_map/ppermute | solution.py:626
  428.3 14.5 %collective-permute-start.84 = (bf16[64,2560]{1,0:T(8,128)(2,1)S(1)}, bf16[64,2560]{1,0:T(8,128)(2,1)}, u32[]{:S(2)}, u32[]{:S(2)}) collective-permute-start(bf16[64,2560]{1,0:T(8,128)(2,1)S(1)} %collective-permute-done.80.p2), channel_id=1, source_target_pairs={{0,1},{1,0},{2,3},{3,2},{4,5},{5,4},{6,7},{7,6},{8,9},{9,8},{10,11... | collective-permute-start | bytes 983048 | tf_op jit(solution)/shard_map/ppermute | solution.py:626
  428.3 14.5 %collective-permute-start.88 = (bf16[64,2560]{1,0:T(8,128)(2,1)S(1)}, bf16[64,2560]{1,0:T(8,128)(2,1)}, u32[]{:S(2)}, u32[]{:S(2)}) collective-permute-start(bf16[64,2560]{1,0:T(8,128)(2,1)S(1)} %copy-done.34), channel_id=1, source_target_pairs={{0,2},{1,3},{2,0},{3,1},{4,6},{5,7},{6,4},{7,5},{8,10},{9,11},{10,... | collective-permute-start | bytes 983048 | tf_op jit(solution)/shard_map/ppermute | solution.py:626
  463.9 13.3 %collective-permute-start.98 = (f32[24,640]{1,0:T(8,128)S(1)}, f32[24,640]{1,0:T(8,128)S(1)}, u32[]{:S(2)}, u32[]{:S(2)}) collective-permute-start(f32[24,640]{1,0:T(8,128)S(1)} %add.44), channel_id=1, source_target_pairs={{0,24},{4,28},{8,16},{12,20},{16,8},{20,12},{24,0},{28,4},{1,25},{... | collective-permute-start | bytes 184328 | tf_op jit(solution)/shard_map/ppermute | solution.py:626
  465.0 12.2 %collective-permute-start.97 = (f32[24,640]{1,0:T(8,128)S(1)}, f32[24,640]{1,0:T(8,128)S(1)}, u32[]{:S(2)}, u32[]{:S(2)}) collective-permute-start(f32[24,640]{1,0:T(8,128)S(1)} %add.44), channel_id=1, source_target_pairs={{0,16},{4,20},{8,24},{12,28},{16,0},{20,4},{24,8},{28,12},{1,17},{... | collective-permute-start | bytes 184328 | tf_op jit(solution)/shard_map/ppermute | solution.py:626
  (116 other events, 895.3 us)
